TPU v7x, 256 devices: a whole 4x4x8 slice. The times are simulated.
256 devices in a mesh: batch: 16 (over y, x), tensor: 16 (over z, core).
Axes of the slice: x: 4, y: 4, z: 8, core: 2. Of those that a mesh axis runs over, the one named last changes fastest.
Arguments:
- queries: bfloat16 [4, 256, 8192], P(None, 'batch', 'tensor'), may hold values from -130 to 130
- cache_keys: bfloat16 [256, 256, 16, 128], P('batch', None, 'tensor'), may hold values from -5 to 5, as said below
- cache_values: bfloat16 [256, 256, 16, 128], P('batch', None, 'tensor'), may hold values from -5 to 5, as said below
- new_keys: bfloat16 [4, 256, 16, 128], P(None, 'batch', 'tensor'), may hold values from -5 to 5, as said below
- new_values: bfloat16 [4, 256, 16, 128], P(None, 'batch', 'tensor'), may hold values from -5 to 5, as said below
- lengths: int32 [256], P('batch'), may hold values from 64 to 256, as said below
- admitted: int32 [4, 256], P(None, 'batch'), may hold values 0 or 1
- request_tenant: int32 [256], P('batch'), may hold values from 0 to 511, as said below
- tenant_adapter: int32 [512], replicated, may hold values from 0 to 127, as said below
- adapter_slot: int32 [128], replicated, may hold values from 0 to 127, as said below
- tenant_tokens: int32 [512], replicated, may hold values from 0 to 1023
- out_weight: bfloat16 [8192, 8192], P('tensor'), may hold values from -0.0625 to 0.0625
- adapter_down_factor: bfloat16 [128, 64, 8192], P('batch', None, 'tensor'), may hold values from -0.0625 to 0.0625
- adapter_up_factor: bfloat16 [128, 64, 8192], P('batch', None, 'tensor'), may hold values from -0.75 to 0.75
Outputs:
- outputs: bfloat16 [4, 256, 8192], P(None, 'batch', 'tensor')
Inputs may be any that keep to these rules, and one draw needn't show every extreme that they name: `cache_keys`: every slot c holds an equal copy of key and value head c * 8 // 16. `cache_values`: every slot c holds an equal copy of key and value head c * 8 // 16. `new_keys`: every slot c holds an equal copy of key and value head c * 8 // 16. `new_values`: every slot c holds an equal copy of key and value head c * 8 // 16. `lengths`: some request has length 256. `tenant_adapter`: each tenant's adapter is named by exactly 4 tenants. A permutation: adapter a lies at row adapter_slot[a], stored with batch index adapter_slot[a] // 8. `request_tenant`: among the requests of one batch index, at most 2 have adapters stored with any one batch index; in every draw one batch index stores the adapters of exactly 2 requests of every batch index.
All inputs are finite; a program needn't handle non-finite values. No bound on the sum of `admitted` on one device may be relied on, other than what follows from the above.
Results may differ from a plain program's by a relative error of at most 0.0063.
Values may be sent and summed in bfloat16 or wider, within the bound.
No kernel may reach another device: no remote copies, remote signals or barrier semaphores. Data moves between devices by JAX's collectives and lax.ppermute only.
A program may use at most 64 MiB of HBM per device.

v0:
```python
import jax
import jax.numpy as jnp
from jax import lax
from jax.sharding import PartitionSpec as P

adapter_scale = 2.0


def pick_rows(table, flat_index):
    merged = table.reshape((table.shape[0] * table.shape[1],) + table.shape[2:])
    return jnp.take(merged, flat_index, axis=0)


def per_device(
    queries,
    cache_keys,
    cache_values,
    new_keys,
    new_values,
    lengths,
    admitted,
    request_tenant,
    tenant_adapter,
    adapter_slot,
    tenant_tokens,
    out_weight,
    adapter_down_factor,
    adapter_up_factor,
):
    holder_count = lax.axis_size("batch")
    step_count, request_count, local_width = queries.shape
    head_dim = cache_keys.shape[3]
    local_heads = local_width // head_dim
    context = cache_keys.shape[1]
    adapters_held = adapter_down_factor.shape[0]
    tenant_count = tenant_tokens.shape[0]
    capacity = max(2, (2 * request_count + holder_count - 1) // holder_count)
    threshold = 3 * context
    score_scale = head_dim ** (-0.5)
    request_adapter_slot = jnp.take(adapter_slot, jnp.take(tenant_adapter, request_tenant))
    holder = request_adapter_slot // adapters_held
    held_index = request_adapter_slot % adapters_held
    request_order = jnp.arange(request_count, dtype=jnp.int32)
    same_holder = holder[:, None] == holder[None, :]
    earlier = request_order[None, :] < request_order[:, None]
    position = jnp.sum((same_holder & earlier).astype(jnp.int32), axis=1)
    flat_index = holder * capacity + position
    selector = flat_index[:, None] == jnp.arange(holder_count * capacity, dtype=jnp.int32)[None, :]
    request_ids = jnp.sum(jnp.where(selector, held_index[:, None], 0), axis=0).reshape(
        holder_count, capacity
    )
    cached_keys = cache_keys[:, :, 0]
    cached_values = cache_values[:, :, 0]
    fresh_keys = new_keys[:, :, 0]
    fresh_values = new_values[:, :, 0]
    cache_mask = jnp.arange(context, dtype=jnp.int32)[None, :] < lengths[:, None]
    ids_part = lax.all_to_all(request_ids, "batch", split_axis=0, concat_axis=0, tiled=True)
    first_got = lax.all_to_all(
        adapter_down_factor[ids_part], "batch", split_axis=0, concat_axis=0, tiled=True
    )
    second_got = lax.all_to_all(
        adapter_up_factor[ids_part], "batch", split_axis=0, concat_axis=0, tiled=True
    )
    first_rows = pick_rows(first_got, flat_index)
    second_rows = pick_rows(second_got, flat_index)
    counters = tenant_tokens
    served_rows = []
    results = []
    for step_index in range(step_count):
        current = jnp.take(counters, request_tenant)
        served = (admitted[step_index] == 1) & (current < threshold)
        served_rows.append(served)
        query_rows = queries[step_index].reshape(request_count, local_heads, head_dim)
        old_scores = (
            jnp.einsum("rhd,rpd->rhp", query_rows, cached_keys, preferred_element_type=jnp.float32)
            * score_scale
        )
        old_scores = jnp.where(cache_mask[:, None, :], old_scores, -jnp.inf)
        visible = jnp.stack(
            [
                (
                    served_rows[other]
                    if other < step_index
                    else jnp.full((request_count,), other == step_index)
                )
                for other in range(step_count)
            ],
            axis=1,
        )
        new_scores = (
            jnp.einsum("rhd,jrd->rhj", query_rows, fresh_keys, preferred_element_type=jnp.float32)
            * score_scale
        )
        new_scores = jnp.where(visible[:, None, :], new_scores, -jnp.inf)
        row_max = jnp.maximum(jnp.max(old_scores, axis=-1), jnp.max(new_scores, axis=-1))
        old_exp = jnp.exp(old_scores - row_max[..., None])
        new_exp = jnp.exp(new_scores - row_max[..., None])
        denominator = jnp.sum(old_exp, axis=-1) + jnp.sum(new_exp, axis=-1)
        old_weights = (old_exp / denominator[..., None]).astype(jnp.bfloat16)
        new_weights = (new_exp / denominator[..., None]).astype(jnp.bfloat16)
        attended_output = jnp.einsum(
            "rhp,rpd->rhd", old_weights, cached_values, preferred_element_type=jnp.float32
        )
        attended_output = attended_output + jnp.einsum(
            "rhj,jrd->rhd", new_weights, fresh_values, preferred_element_type=jnp.float32
        )
        attended_output = attended_output.reshape(request_count, local_width).astype(jnp.bfloat16)
        base_projection_term = lax.psum_scatter(
            lax.dot_general(
                out_weight,
                attended_output,
                (((0,), (1,)), ((), ())),
                preferred_element_type=jnp.float32,
            ),
            "tensor",
            scatter_dimension=0,
            tiled=True,
        ).T
        partial_low = jnp.einsum(
            "rd,rkd->rk", attended_output, first_rows, preferred_element_type=jnp.float32
        )
        low_rank = lax.psum(partial_low, "tensor").astype(jnp.bfloat16)
        adapter_correction = jnp.einsum(
            "rk,rkd->rd", low_rank, second_rows, preferred_element_type=jnp.float32
        )
        combined_output = base_projection_term + adapter_scale * adapter_correction
        results.append((served.astype(jnp.float32)[:, None] * combined_output).astype(jnp.bfloat16))
        if step_index + 1 < step_count:
            charge = jnp.where(served, lengths + step_index + 1, 0)
            local_table = jnp.zeros((tenant_count,), jnp.int32).at[request_tenant].add(charge)
            counters = counters + lax.psum(local_table, "batch")
    return jnp.stack(results)


def solution(mesh):
    placed = (
        P(None, "batch", "tensor"),
        P("batch", None, "tensor", None),
        P("batch", None, "tensor", None),
        P(None, "batch", "tensor", None),
        P(None, "batch", "tensor", None),
        P("batch"),
        P(None, "batch"),
        P("batch"),
        P(),
        P(),
        P(),
        P("tensor", None),
        P("batch", None, "tensor"),
        P("batch", None, "tensor"),
    )
    return jax.shard_map(
        per_device,
        mesh=mesh,
        in_specs=placed,
        out_specs=P(None, "batch", "tensor"),
        check_vma=False,
    )
```

profile of v0, /device:TPU:2, one launch (start us, length us, event | category | flops | bytes accessed | tf_op | source)
XLA Modules:
  0.0 273.0 jit_solution(5413086295183243913)
XLA Ops:
  6.5 0.7 compare_select_fusion.2
  7.3 1.3 gather_fusion.3
  8.6 1.3 gather_fusion.4
  10.0 0.7 fusion.96
  10.7 1.3 gather_fusion
  12.0 0.2 convert_reduce_fusion
  12.3 0.7 all_to_all.14
  13.0 7.5 %all-to-all-start = ((s32[16,1,2]{2,1,0:T(1,128)}), s32[16,1,2]{2,1,0:T(1,128)S(1)}, u32[]{:S(2)}, u32[]{:S(2)}) async-start(s32[16,1,2]{2,1,0:T(1,128)} %bitcast.7), calls=%async_computation.1 | async-start | bytes 16384 | tf_op jit(solution)/shard_map/all_to_all | solution.py:57
  20.6 0.8 fusion.99
  21.4 0.7 iota_compare_fusion
  22.1 0.5 fusion.106
  22.6 0.9 fusion.107
  23.5 0.2 fusion.24
  23.7 1.5 fusion.18
  25.2 1.0 fusion.8
  26.3 5.4 %convolution_bitcast_fusion.3 = f32[8192,16]{0,1:T(8,128)} fusion(bf16[512,8192]{1,0:T(8,128)(2,1)} %param.29, bf16[2,8,4,128]{3,2,1,0:T(4,128)(2,1)S(1)} %bitcast.183), kind=kOutput, calls=%fused_computation.16 | convolution fusion | flops 134217728 | bytes 8929280 | tf_op jit(solution)/shard_map/dot_general | solution.py:109
  31.8 0.7 scatter_custom_fusion
  32.5 15.3 %psum.50 = s32[512]{0:T(512)S(1)} all-reduce(s32[512]{0:T(512)S(1)} %scatter_custom_fusion), channel_id=1, replica_groups=mesh['batch'=16,'tensor'=16] {'batch'}, use_global_device_ids=true, to_apply=%region_9.12 | all-reduce | flops 512 | bytes 4096 | tf_op jit(solution)/shard_map/psum | solution.py:131
  47.7 0.7 gather_fusion.7
  48.4 0.7 scatter_custom_fusion.1
  49.1 12.5 %psum.52 = s32[512]{0:T(512)S(1)} all-reduce(s32[512]{0:T(512)S(1)} %scatter_custom_fusion.1), channel_id=1, replica_groups=mesh['batch'=16,'tensor'=16] {'batch'}, use_global_device_ids=true, to_apply=%region_17.20 | all-reduce | flops 512 | bytes 4096 | tf_op jit(solution)/shard_map/psum | solution.py:131
  61.6 0.7 gather_fusion.8
  62.7 0.5 fusion.104
  63.3 0.2 fusion.25
  63.6 0.3 fusion.16
  63.9 0.2 fusion.9
  64.1 5.5 %convolution_bitcast_fusion.2 = f32[8192,16]{0,1:T(8,128)} fusion(bf16[512,8192]{1,0:T(8,128)(2,1)} %param.29, bf16[2,8,4,128]{3,2,1,0:T(4,128)(2,1)S(1)} %bitcast.184), kind=kOutput, calls=%fused_computation.15 | convolution fusion | flops 134217728 | bytes 8929280 | tf_op jit(solution)/shard_map/dot_general | solution.py:109
  69.7 0.5 fusion.102
  70.4 0.2 fusion.26
  70.6 0.3 fusion.14
  70.9 0.2 fusion.10
  71.4 2.0 gather_fusion.1
  73.4 6.9 %all-to-all-start.1 = ((bf16[16,2,64,512]{3,2,1,0:T(8,128)(2,1)}), bf16[16,2,64,512]{3,2,1,0:T(8,128)(2,1)}, u32[]{:S(2)}, u32[]{:S(2)}) async-start(bf16[16,2,64,512]{3,2,1,0:T(8,128)(2,1)} %bitcast.9), calls=%async_computation.2 | async-start | bytes 4194304 | tf_op jit(solution)/shard_map/all_to_all | solution.py:58
  80.4 5.4 %convolution_bitcast_fusion.1 = f32[8192,16]{0,1:T(8,128)} fusion(bf16[512,8192]{1,0:T(8,128)(2,1)} %param.29, bf16[2,8,4,128]{3,2,1,0:T(4,128)(2,1)S(1)} %bitcast.185), kind=kOutput, calls=%fused_computation.14 | convolution fusion | flops 134217728 | bytes 8929280 | tf_op jit(solution)/shard_map/dot_general | solution.py:109
  86.1 0.5 fusion.100
  86.6 0.2 fusion.27
  86.9 0.3 fusion.12
  87.2 0.2 fusion.11
  87.4 5.4 %convolution_bitcast_fusion = f32[8192,16]{0,1:T(8,128)} fusion(bf16[512,8192]{1,0:T(8,128)(2,1)} %param.29, bf16[2,8,4,128]{3,2,1,0:T(4,128)(2,1)S(1)} %bitcast.186), kind=kOutput, calls=%fused_computation.13 | convolution fusion | flops 134217728 | bytes 8929280 | tf_op jit(solution)/shard_map/dot_general | solution.py:109
  92.9 2.0 gather_fusion.2
  94.9 7.9 %all-to-all-done.1 = bf16[16,2,64,512]{3,2,1,0:T(8,128)(2,1)} async-done(((bf16[16,2,64,512]{3,2,1,0:T(8,128)(2,1)}), bf16[16,2,64,512]{3,2,1,0:T(8,128)(2,1)}, u32[]{:S(2)}, u32[]{:S(2)}) %all-to-all-start.1) | async-done | bytes 2097184 | tf_op jit(solution)/shard_map/all_to_all | solution.py:58
  102.8 5.2 %all-to-all-start.2 = ((bf16[16,2,64,512]{3,2,1,0:T(8,128)(2,1)}), bf16[16,2,64,512]{3,2,1,0:T(8,128)(2,1)S(1)}, u32[]{:S(2)}, u32[]{:S(2)}) async-start(bf16[16,2,64,512]{3,2,1,0:T(8,128)(2,1)} %bitcast.14), calls=%async_computation.3 | async-start | bytes 4194304 | tf_op jit(solution)/shard_map/all_to_all | solution.py:61
  108.0 0.7 scatter_custom_fusion.2
  108.7 30.3 %psum.54 = s32[512]{0:T(512)S(1)} all-reduce(s32[512]{0:T(512)S(1)} %scatter_custom_fusion.2), channel_id=1, replica_groups=mesh['batch'=16,'tensor'=16] {'batch'}, use_global_device_ids=true, to_apply=%region_25.28 | all-reduce | flops 512 | bytes 4096 | tf_op jit(solution)/shard_map/psum | solution.py:131
  139.0 0.7 gather_fusion.9
  139.7 3.2 %gather_fusion.5 = bf16[16,64,512]{2,1,0:T(8,128)(2,1)} fusion(bf16[32,64,512]{2,1,0:T(8,128)(2,1)} %bitcast.10, s32[1024]{0:T(1024)S(1)} %pad_clamp_fusion), kind=kCustom, calls=%fused_computation.1.clone | custom fusion | bytes 2097216 | tf_op jit(solution)/shard_map/jit(_take)/gather | solution.py:11
  142.8 1.4 broadcast_select_fusion.1
  144.2 0.4 fusion.108
  144.6 0.4 fusion.109
  145.0 0.4 fusion.110
  145.4 0.4 fusion.111
  145.8 1.6 gather_fusion.6
  147.4 48.9 %all-reduce = (bf16[16,64]{1,0:T(8,128)(2,1)S(1)}, bf16[16,64]{1,0:T(8,128)(2,1)S(1)}, bf16[16,64]{1,0:T(8,128)(2,1)S(1)}, bf16[16,64]{1,0:T(8,128)(2,1)S(1)}) all-reduce(f32[16,64]{1,0:T(8,128)S(1)} %bitcast.190, f32[16,64]{1,0:T(8,128)S(1)} %bitcast.189, ...), channel_id=1, replica_groups=mesh['batch'=16,'tensor'=16] {'tensor'}, use_global_device_ids=true, to_apply=%region_31.34 | all-reduce | flops 4096 | bytes 24576 | tf_op jit(solution)/shard_map/psum | solution.py:122
  196.3 1.5 fusion.78
  197.8 1.6 fusion.76
  199.4 0.8 fusion.52
  200.2 0.8 fusion.53
  201.0 1.5 fusion.74
  202.6 5.1 %reduce-scatter.9.cloned.1.call-done = f32[512,16]{0,1:T(8,128)} async-done(((f32[8192,16]{0,1:T(8,128)}), f32[512,16]{0,1:T(8,128)}) %reduce-scatter.9.cloned.1.call-update) | async-done | bytes 32784 | tf_op jit(solution)/shard_map/reduce_scatter | solution.py:108
  207.7 0.8 fusion.54
  208.5 1.5 fusion.72
  210.0 55.0 %reduce-scatter.11.cloned.1.call-done = f32[512,16]{0,1:T(8,128)} async-done(((f32[8192,16]{0,1:T(8,128)}), f32[512,16]{0,1:T(8,128)}) %reduce-scatter.11.cloned.1.call-update) | async-done | bytes 32784 | tf_op jit(solution)/shard_map/reduce_scatter | solution.py:108
  265.0 0.8 fusion.55
  265.9 0.6 pad_maximum_fusion
  (84 shorter events, 2.1 us)
Async XLA Ops:
  6.5 15.6 %copy-start = (bf16[16,256,1,128]{3,1,2,0:T(8,128)(2,1)S(1)}, bf16[16,256,1,128]{3,1,2,0:T(8,128)(2,1)}, u32[]{:S(2)}) copy-start(bf16[16,256,1,128]{3,1,2,0:T(8,128)(2,1)} %param.19) | copy-start | bytes 3145732
  13.0 58.1 %all-to-all-start = ((s32[16,1,2]{2,1,0:T(1,128)}), s32[16,1,2]{2,1,0:T(1,128)S(1)}, u32[]{:S(2)}, u32[]{:S(2)}) async-start(s32[16,1,2]{2,1,0:T(1,128)} %bitcast.7), calls=%async_computation.1 | async-start | bytes 16384 | tf_op jit(solution)/shard_map/all_to_all | solution.py:57
  20.5 11.3 %copy-start.5 = (s32[16]{0:T(128)S(1)}, s32[16]{0:T(128)}, u32[]{:S(2)}) copy-start(s32[16]{0:T(128)} %param.23) | copy-start | bytes 196
  20.5 27.2 %copy-start.1 = (s32[512]{0:T(512)S(1)}, s32[512]{0:T(512)}, u32[]{:S(2)}) copy-start(s32[512]{0:T(512)} %param.28) | copy-start | bytes 6148
  20.5 178.8 %reduce-scatter.5.cloned.1.call-start = ((), (), s32[]{:S(2)}) async-start(), calls=%async_computation.7 | async-start | bytes 557056 | tf_op jit(solution)/shard_map/reduce_scatter | solution.py:108
  22.1 26.3 %copy-start.4 = (s32[4,16]{1,0:T(4,128)S(1)}, s32[4,16]{1,0:T(4,128)}, u32[]{:S(2)}) copy-start(s32[4,16]{1,0:T(4,128)} %param.24) | copy-start | bytes 772
  25.2 37.9 %copy-start.7 = (bf16[4,16,1,128]{3,1,2,0:T(8,128)(2,1)S(1)}, bf16[4,16,1,128]{3,1,2,0:T(8,128)(2,1)}, u32[]{:S(2)}) copy-start(bf16[4,16,1,128]{3,1,2,0:T(8,128)(2,1)} %param.21) | copy-start | bytes 49156
  25.2 38.3 %copy-start.6 = (bf16[16,256,1,128]{3,1,2,0:T(8,128)(2,1)S(1)}, bf16[16,256,1,128]{3,1,2,0:T(8,128)(2,1)}, u32[]{:S(2)}) copy-start(bf16[16,256,1,128]{3,1,2,0:T(8,128)(2,1)} %param.20) | copy-start | bytes 3145732
  26.3 37.6 %copy-start.8 = (bf16[4,16,1,128]{3,1,2,0:T(8,128)(2,1)S(1)}, bf16[4,16,1,128]{3,1,2,0:T(8,128)(2,1)}, u32[]{:S(2)}) copy-start(bf16[4,16,1,128]{3,1,2,0:T(8,128)(2,1)} %param.22) | copy-start | bytes 49156
  31.7 168.5 %reduce-scatter.7.cloned.1.call-start = ((), (), s32[]{:S(2)}) async-start(), calls=%async_computation.8 | async-start | bytes 557056 | tf_op jit(solution)/shard_map/reduce_scatter | solution.py:108
  64.1 7.3 %copy-start.2 = (bf16[8,64,512]{2,1,0:T(8,128)(2,1)S(1)}, bf16[8,64,512]{2,1,0:T(8,128)(2,1)}, u32[]{:S(2)}) copy-start(bf16[8,64,512]{2,1,0:T(8,128)(2,1)} %param.30) | copy-start | bytes 1572868
  73.4 29.4 %all-to-all-start.1 = ((bf16[16,2,64,512]{3,2,1,0:T(8,128)(2,1)}), bf16[16,2,64,512]{3,2,1,0:T(8,128)(2,1)}, u32[]{:S(2)}, u32[]{:S(2)}) async-start(bf16[16,2,64,512]{3,2,1,0:T(8,128)(2,1)} %bitcast.9), calls=%async_computation.2 | async-start | bytes 4194304 | tf_op jit(solution)/shard_map/all_to_all | solution.py:58
  80.3 127.4 %reduce-scatter.9.cloned.1.call-start = ((), (), s32[]{:S(2)}) async-start(), calls=%async_computation.9 | async-start | bytes 557056 | tf_op jit(solution)/shard_map/reduce_scatter | solution.py:108
  85.8 179.2 %reduce-scatter.11.cloned.1.call-start = ((), (), s32[]{:S(2)}) async-start(), calls=%async_computation.10 | async-start | bytes 557056 | tf_op jit(solution)/shard_map/reduce_scatter | solution.py:108
  86.0 6.9 %copy-start.3 = (bf16[8,64,512]{2,1,0:T(8,128)(2,1)S(1)}, bf16[8,64,512]{2,1,0:T(8,128)(2,1)}, u32[]{:S(2)}) copy-start(bf16[8,64,512]{2,1,0:T(8,128)(2,1)} %param.31) | copy-start | bytes 1572868
  102.8 43.0 %all-to-all-start.2 = ((bf16[16,2,64,512]{3,2,1,0:T(8,128)(2,1)}), bf16[16,2,64,512]{3,2,1,0:T(8,128)(2,1)S(1)}, u32[]{:S(2)}, u32[]{:S(2)}) async-start(bf16[16,2,64,512]{3,2,1,0:T(8,128)(2,1)} %bitcast.14), calls=%async_computation.3 | async-start | bytes 4194304 | tf_op jit(solution)/shard_map/all_to_all | solution.py:61
Sparse Core Ops, SparseCore 0:
  31.8 59.2 reduce-scatter.4
  93.8 55.9 reduce-scatter.6
  152.3 55.2 reduce-scatter.8
  210.2 54.7 reduce-scatter.10
where the time goes:
time: 274 us; the launch traced here: 273 us
  blocking collectives  107 us (39%)
  waiting for transfers between devices  68 us (25%)
  matrix products  36.8 us (13%)
  starting transfers between devices  19.8 us (7%)
  local copies, waits for them, and re-layouts  17.1 us (6%)
  between operations  13.5 us (5%)
  other arithmetic  10.9 us (4%)
    reduce_scatter x4, waiting for transfers between devices, per_device(): lax.psum_scatter(lax.dot_general(out_weight, attended_output, (((0,), (1,...  60.1 us
    psum x3, blocking collectives, per_device(): counters = counters + lax.psum(local_table, 'batch')  58.1 us
    psum x1, blocking collectives, per_device(): low_rank = lax.psum(partial_low, 'tensor').astype(jnp.bfloat16)  48.9 us
    dot_general x4, matrix products, per_device(): lax.dot_general(out_weight, attended_output, (((0,), (1,)), ((), ())), pr...  21.7 us
    all_to_all x1, waiting for transfers between devices, per_device(): lax.all_to_all(adapter_down_factor[ids_part], 'batch', split_axis=0, conc...  7.88 us
    all_to_all x1, starting transfers between devices, per_device(): lax.all_to_all(request_ids, 'batch', split_axis=0, concat_axis=0, tiled=T...  7.48 us
    all_to_all x1, starting transfers between devices, per_device(): lax.all_to_all(adapter_down_factor[ids_part], 'batch', split_axis=0, conc...  6.92 us
    dot_general x4, matrix products, per_device(): jnp.einsum('rk,rkd->rd', low_rank, second_rows, preferred_element_type=jn...  6.18 us
  transfers between devices with their start and end apart: 7, of which 3 were waited for; matrix products, arithmetic and copies ran while one was open for 21% of the time, Pallas kernels for 0%

commit v1 on v0

v1 whole, which is shorter than its diff:
```python
import functools

import jax
import jax.numpy as jnp
from jax import lax
from jax.experimental import pallas as pl
from jax.experimental.pallas import tpu as pltpu
from jax.sharding import Mesh
from jax.sharding import PartitionSpec as P

adapter_scale = 2.0
capacity = 2
lanes = 128
f32 = jnp.float32
bf16 = jnp.bfloat16
VMEM = pl.BlockSpec(memory_space=pltpu.VMEM)
SMEM = pl.BlockSpec(memory_space=pltpu.SMEM)
HBM = pl.BlockSpec(memory_space=pl.ANY)


def iota(shape, axis):
    return lax.broadcasted_iota(jnp.int32, shape, axis)


def dot(a, b):
    return jnp.dot(a, b, preferred_element_type=f32)


def dot_t(a, b):
    return lax.dot_general(a, b, (((1,), (1,)), ((), ())), preferred_element_type=f32)


def call(kernel, out_shape, in_specs, out_specs, flops, moved, scratch=(), limit=48 << 20):
    return pl.pallas_call(
        kernel,
        out_shape=out_shape,
        in_specs=in_specs,
        out_specs=out_specs,
        scratch_shapes=list(scratch),
        cost_estimate=pl.CostEstimate(flops=flops, bytes_accessed=moved, transcendentals=0),
        compiler_params=pltpu.CompilerParams(vmem_limit_bytes=limit),
    )


def score_kernel(
    steps,
    requests,
    heads,
    adapters_held,
    tenant_ref,
    length_ref,
    tenant_adapter_ref,
    adapter_slot_ref,
    query_ref,
    key_ref,
    new_key_ref,
    exp_ref,
    stat_ref,
    new_score_ref,
    flat_ref,
    held_ref,
    back_ref,
    seen,
):
    rows = steps * heads
    total = requests * rows
    width = key_ref.shape[2]
    context = key_ref.shape[1]
    scale = width ** (-0.5)
    for index in range(seen.shape[0]):
        seen[index] = 0
    flat_rows = jnp.zeros((steps * requests, 1), jnp.int32)
    place = iota((steps * requests, 1), 0)
    for r in range(requests):
        slot = adapter_slot_ref[tenant_adapter_ref[tenant_ref[r]]]
        holder = slot // adapters_held
        position = seen[holder]
        seen[holder] = position + 1
        flat = holder * capacity + position
        flat_ref[r] = flat
        held_ref[r] = slot - holder * adapters_held
        flat_rows = jnp.where(place % requests == r, flat, flat_rows)
    flat_rows = flat_rows * steps + place // requests
    back_ref[...] = (flat_rows == iota(back_ref.shape, 1)).astype(f32).astype(bf16)

    by_head = jnp.concatenate(
        [query_ref[:, h * width : (h + 1) * width] for h in range(heads)], axis=0
    )
    row = iota((total, total), 0)
    wanted = (row % heads) * (steps * requests) + ((row // heads) % steps) * requests + row // rows
    order = (wanted == iota((total, total), 1)).astype(f32).astype(bf16)
    by_request = dot(order, by_head).astype(bf16)
    new_score_ref[...] = dot_t(by_request, new_key_ref[...]) * scale
    position = iota((rows, context), 1)
    for r in range(requests):
        block = pl.ds(r * rows, rows)
        scores = dot_t(by_request[r * rows : (r + 1) * rows], key_ref[r]) * scale
        scores = jnp.where(position < length_ref[r], scores, -jnp.inf)
        top = jnp.max(scores, axis=1, keepdims=True)
        weight = jnp.exp(scores - top)
        exp_ref[block, :] = weight
        mass = jnp.sum(weight, axis=1, keepdims=True)
        stat_ref[block, :] = jnp.where(iota((rows, lanes), 1) == 0, top, mass)


def attend_kernel(
    steps,
    requests,
    heads,
    threshold,
    tenant_ref,
    token_ref,
    admitted_ref,
    flat_ref,
    held_ref,
    shared_ref,
    exp_ref,
    stat_ref,
    new_score_ref,
    value_ref,
    new_value_ref,
    home_ref,
    send_ref,
    attended,
):
    rows = steps * heads
    total = requests * rows
    width = value_ref.shape[2]
    tenants = shared_ref[:, 0, :]
    lengths = shared_ref[:, 1, :]
    charges = [
        jnp.where(shared_ref[:, 2 + s, :] == 1, lengths + (s + 1), 0).astype(f32)
        for s in range(steps - 1)
    ]
    step_of_row = iota((rows, 1), 0) // heads
    column = iota((rows, steps * requests), 1)
    column_step = column // requests
    for r in range(requests):
        block = pl.ds(r * rows, rows)
        same = tenants == tenant_ref[r]
        count = jnp.full((1, 1), token_ref[tenant_ref[r]], jnp.int32)
        served = []
        for s in range(steps):
            open_now = (count < threshold).astype(jnp.int32)
            served.append(open_now * (admitted_ref[s, r] == 1).astype(jnp.int32))
            if s + 1 < steps:
                charge = jnp.sum(jnp.where(same, charges[s], 0.0), axis=(0, 1), keepdims=True)
                count = count + open_now * charge.astype(jnp.int32)
        visible_step = jnp.zeros((rows, steps * requests), jnp.int32)
        served_row = jnp.zeros((rows, 1), f32)
        for s in range(steps):
            visible_step = jnp.where(column_step == s, served[s], visible_step)
            served_row = jnp.where(step_of_row == s, served[s].astype(f32), served_row)
        visible = (column_step == step_of_row) | (
            (column_step < step_of_row) & (visible_step == 1)
        )
        visible = visible & (column % requests == r)
        new_scores = jnp.where(visible, new_score_ref[block, :], -jnp.inf)
        old_top = stat_ref[block, 0:1]
        top = jnp.maximum(old_top, jnp.max(new_scores, axis=1, keepdims=True))
        shrink = jnp.exp(old_top - top)
        new_exp = jnp.exp(new_scores - top)
        mass = stat_ref[block, 1:2] * shrink + jnp.sum(new_exp, axis=1, keepdims=True)
        inverse = 1.0 / mass
        old_weights = (exp_ref[block, :] * (shrink * inverse)).astype(bf16)
        new_weights = (new_exp * inverse).astype(bf16)
        gathered = dot(old_weights, value_ref[r]) + dot(new_weights, new_value_ref[...])
        attended[block, :] = (gathered * served_row).astype(bf16)
    row = iota((total, total), 0)
    pairs = steps * requests
    wanted = (row % requests) * rows + ((row // requests) % steps) * heads + row // pairs
    order = (wanted == iota((total, total), 1)).astype(f32).astype(bf16)
    by_head = dot(order, attended[...]).astype(bf16)
    for h in range(heads):
        home_ref[:, h * width : (h + 1) * width] = by_head[h * pairs : (h + 1) * pairs]
    lane = iota((1, pairs), 1)
    flat = jnp.zeros((1, pairs), jnp.int32)
    place = iota((pairs, lanes), 0) % requests
    held = jnp.zeros((pairs, lanes), f32)
    for r in range(requests):
        flat = jnp.where(lane % requests == r, flat_ref[r], flat)
        held = jnp.where(place == r, held_ref[r].astype(f32), held)
    flat = flat * steps + lane // requests
    pick = (iota((send_ref.shape[0], pairs), 0) == flat).astype(f32).astype(bf16)
    features = heads * width
    send_ref[:, 0:features] = dot(pick, home_ref[...]).astype(bf16)
    send_ref[:, features:] = dot(pick, held.astype(bf16)).astype(bf16)


def project_kernel(flip, rows_ref, weight_ref, out_ref, blocks, sems):
    parts, _, width = out_ref.shape
    core = lax.axis_index("core")
    mine = core if flip == 0 else 1 - core
    copies = []
    for part in range(parts):
        start = pl.multiple_of((2 * part + mine) * width, width)
        copy = pltpu.make_async_copy(
            weight_ref.at[:, pl.ds(start, width)], blocks.at[part], sems.at[part]
        )
        copy.start()
        copies.append(copy)
    for part in range(parts):
        copies[part].wait()
        out_ref[part] = dot(rows_ref[...], blocks[part]).astype(out_ref.dtype)


def low_kernel(got_ref, held_ref, down_ref, low_ref):
    rank = down_ref.shape[1]
    every = down_ref.shape[0] * rank
    features = down_ref.shape[2]
    product = dot_t(got_ref[...], down_ref[...].reshape(every, features))
    owner = (iota(product.shape, 1) // rank).astype(f32)
    product = jnp.where(owner == held_ref[:, 0:1].astype(f32), product, 0.0)
    folded = product[:, 0:lanes]
    for start in range(lanes, every, lanes):
        folded = folded + product[:, start : start + lanes]
    folded = folded + pltpu.roll(folded, rank, 1)
    half = folded.shape[0] // 2
    first = iota((half, lanes), 1) < rank
    low_ref[...] = jnp.where(first, folded[0:half], folded[half:])


def up_kernel(parts_ref, held_ref, up_ref, out_ref):
    rank = up_ref.shape[1]
    every = up_ref.shape[0] * rank
    low = parts_ref[0].astype(f32)
    for part in range(1, parts_ref.shape[0]):
        low = low + parts_ref[part].astype(f32)
    other = pltpu.roll(low, rank, 1)
    first = iota(low.shape, 1) < rank
    low = jnp.concatenate(
        [jnp.where(first, low, other), jnp.where(first, other, low)], axis=0
    )
    wide = jnp.concatenate([low] * (every // lanes), axis=1)
    owner = (iota(wide.shape, 1) // rank).astype(f32)
    wide = jnp.where(owner == held_ref[:, 0:1].astype(f32), wide, 0.0).astype(bf16)
    out_ref[...] = dot(wide, up_ref[...].reshape(every, up_ref.shape[2])).astype(bf16)


def finish_kernel(base_ref, back_ref, term_ref, out_ref):
    total = base_ref[0].astype(f32)
    for part in range(1, base_ref.shape[0]):
        total = total + base_ref[part].astype(f32)
    term = dot(back_ref[...], term_ref[...])
    out_ref[...] = (total + adapter_scale * term).astype(bf16)


def per_device(
    queries,
    cache_keys,
    cache_values,
    new_keys,
    new_values,
    lengths,
    admitted,
    request_tenant,
    tenant_adapter,
    adapter_slot,
    tenant_tokens,
    out_weight,
    adapter_down_factor,
    adapter_up_factor,
):
    holders = lax.axis_size("batch")
    parts = lax.axis_size("z")
    steps, requests, features = queries.shape
    context, width = cache_keys.shape[1], cache_keys.shape[3]
    heads = features // width
    rows = steps * heads
    total = requests * rows
    pairs = steps * requests
    adapters_held, rank, _ = adapter_down_factor.shape
    every = adapters_held * rank
    threshold = 3 * context
    slots = holders * capacity * steps
    shape = jax.ShapeDtypeStruct

    shared = jnp.concatenate([request_tenant[None], lengths[None], admitted], axis=0)
    shared = jnp.broadcast_to(shared[None], (holders,) + shared.shape)
    shared = lax.all_to_all(shared, "batch", split_axis=0, concat_axis=0, tiled=True)

    old_exp, stats, new_scores, flat, held, back = call(
        functools.partial(score_kernel, steps, requests, heads, adapters_held),
        (
            shape((total, context), f32),
            shape((total, lanes), f32),
            shape((total, pairs), f32),
            shape((requests,), jnp.int32),
            shape((requests,), jnp.int32),
            shape((pairs, slots), bf16),
        ),
        [SMEM, SMEM, SMEM, SMEM, VMEM, VMEM, VMEM],
        (VMEM, VMEM, VMEM, SMEM, SMEM, VMEM),
        2 * total * context * width,
        3 * cache_keys.size,
        [pltpu.SMEM((holders,), jnp.int32)],
    )(
        request_tenant,
        lengths,
        tenant_adapter,
        adapter_slot,
        queries.reshape(pairs, features),
        cache_keys.reshape(requests, context, width),
        new_keys.reshape(pairs, width),
    )
    home, send = call(
        functools.partial(attend_kernel, steps, requests, heads, threshold),
        (shape((pairs, features), bf16), shape((slots, features + lanes), bf16)),
        [SMEM] * 5 + [VMEM] * 6,
        (VMEM, VMEM),
        2 * total * context * width,
        3 * cache_keys.size,
        [pltpu.VMEM((total, width), bf16)],
    )(
        request_tenant,
        tenant_tokens,
        admitted,
        flat,
        held,
        shared,
        old_exp,
        stats,
        new_scores,
        cache_values.reshape(requests, context, width),
        new_values.reshape(pairs, width),
    )
    got = lax.all_to_all(send, "batch", split_axis=0, concat_axis=0, tiled=True)

    def project(flip, dtype):
        return call(
            functools.partial(project_kernel, flip),
            shape((parts, pairs, features), dtype),
            [VMEM, HBM],
            VMEM,
            pairs * out_weight.size,
            out_weight.size,
            [
                pltpu.VMEM((parts, features, features), bf16),
                pltpu.SemaphoreType.DMA((parts,)),
            ],
        )(home, out_weight)

    swap = [(0, 1), (1, 0)]
    theirs = lax.ppermute(project(1, bf16), "core", swap)
    ours = project(0, f32)
    base = (ours + theirs.astype(f32)).astype(bf16)

    rows_got = got[:, 0:features]
    held_got = got[:, features:]
    low = call(
        low_kernel,
        shape((slots // 2, lanes), f32),
        [VMEM] * 3,
        VMEM,
        2 * slots * features * every,
        4 * slots * features,
    )(rows_got, held_got, adapter_down_factor)
    low = (low + lax.ppermute(low, "core", swap)).astype(bf16)
    low = jnp.broadcast_to(low[None], (parts,) + low.shape)
    low = lax.all_to_all(low, "z", split_axis=0, concat_axis=0, tiled=True)
    base = lax.all_to_all(base, "z", split_axis=0, concat_axis=0, tiled=True)
    term = call(
        up_kernel,
        shape((slots, features), bf16),
        [VMEM] * 3,
        VMEM,
        2 * slots * features * every,
        4 * slots * features,
    )(low, held_got, adapter_up_factor)
    term = lax.all_to_all(term, "batch", split_axis=0, concat_axis=0, tiled=True)
    out = call(
        finish_kernel,
        shape((pairs, features), bf16),
        [VMEM] * 3,
        VMEM,
        2 * pairs * slots * features,
        4 * base.size,
    )(base, back, term)
    return out.reshape(steps, requests, features)


def solution(mesh):
    batch, tensor = mesh.shape["batch"], mesh.shape["tensor"]
    split = Mesh(mesh.devices.reshape(batch, tensor // 2, 2), ("batch", "z", "core"))
    tensor_axes = ("z", "core")
    placed = (
        P(None, "batch", tensor_axes),
        P("batch", None, tensor_axes, None),
        P("batch", None, tensor_axes, None),
        P(None, "batch", tensor_axes, None),
        P(None, "batch", tensor_axes, None),
        P("batch"),
        P(None, "batch"),
        P("batch"),
        P(),
        P(),
        P(),
        P(tensor_axes, None),
        P("batch", None, tensor_axes),
        P("batch", None, tensor_axes),
    )
    return jax.shard_map(
        per_device,
        mesh=split,
        in_specs=placed,
        out_specs=P(None, "batch", tensor_axes),
        check_vma=False,
    )
```

time: 274 us -> 88.9 us (0.32)
  blocking collectives: 107 us -> 17.6 us
  waiting for transfers between devices: 68 us -> 18.2 us
  matrix products: 36.8 us -> 0 us
  between operations: 13.5 us -> 0.12 us
  Pallas kernels: 0 us -> 12.5 us
  other arithmetic: 10.9 us -> 0.88 us
  starting transfers between devices: 19.8 us -> 28.1 us
  local copies, waits for them, and re-layouts: 17.1 us -> 10.7 us
    psum x4 -> x0, blocking collectives: 107 us -> none  [the longest x3 58.1 us: per_device(): counters = counters + lax.psum(local_table, 'batch')]
    reduce_scatter x4 -> x0, waiting for transfers between devices: 60.1 us -> none  [per_device(): lax.psum_scatter(lax.dot_general(out_weight, attended_output, (((0,), (1,...]
    dot_general x28 -> x0, matrix products: 36.8 us -> none  [the longest x4 21.7 us: per_device(): lax.dot_general(out_weight, attended_output, (((0,), (1,)), ((), ())), pr...]
    all_to_all x0 -> x1, blocking collectives: none -> 17.6 us  [per_device(): base = lax.all_to_all(base, 'z', split_axis=0, concat_axis=0, tiled=True)]
    gather x10 -> x0, local copies, waits for them, and re-layouts: 14.8 us -> none  [the longest x2 4.82 us: pick_rows(): return jnp.take(merged, flat_index, axis=0)]
    pallas_call x0 -> x7, Pallas kernels: none -> 12.5 us  [the longest x2 5.63 us: project(): call(functools.partial(project_kernel, flip), shape((parts, pairs, featur...]
    unnamed x18 -> x28, local copies, waits for them, and re-layouts: 0.04 us -> 9.38 us
    all_to_all x3 -> x4, waiting for transfers between devices: 7.89 us -> 17 us  [the longest x1 6.61 us: per_device(): low = lax.all_to_all(low, 'z', split_axis=0, concat_axis=0, tiled=True)]
  transfers between devices with their start and end apart: 7 -> 6, of which waited for: 3 -> 4; matrix products, arithmetic and copies ran while one was open for 21% -> 1% of each run, Pallas kernels for 0% -> 10%
where the time goes in v1:
time: 88.9 us; the launch traced here: 88.1 us
  starting transfers between devices  28.1 us (32%)
  waiting for transfers between devices  18.2 us (20%)
  blocking collectives  17.6 us (20%)
  Pallas kernels  12.5 us (14%)
  local copies, waits for them, and re-layouts  10.7 us (12%)
    all_to_all x1, blocking collectives, per_device(): base = lax.all_to_all(base, 'z', split_axis=0, concat_axis=0, tiled=True)  17.6 us
    unnamed x28, local copies, waits for them, and re-layouts  9.38 us
    all_to_all x1, starting transfers between devices, per_device(): low = lax.all_to_all(low, 'z', split_axis=0, concat_axis=0, tiled=True)  8.46 us
    all_to_all x1, starting transfers between devices, per_device(): lax.all_to_all(shared, 'batch', split_axis=0, concat_axis=0, tiled=True)  7.48 us
    all_to_all x1, starting transfers between devices, per_device(): got = lax.all_to_all(send, 'batch', split_axis=0, concat_axis=0, tiled=True)  7.23 us
    all_to_all x1, waiting for transfers between devices, per_device(): low = lax.all_to_all(low, 'z', split_axis=0, concat_axis=0, tiled=True)  6.61 us
    all_to_all x1, waiting for transfers between devices, per_device(): lax.all_to_all(term, 'batch', split_axis=0, concat_axis=0, tiled=True)  6.54 us
    pallas_call x2, Pallas kernels, project(): call(functools.partial(project_kernel, flip), shape((parts, pairs, featur...  5.63 us
  transfers between devices with their start and end apart: 6, of which 4 were waited for; matrix products, arithmetic and copies ran while one was open for 1% of the time, Pallas kernels for 10%

profile of v1, /device:TPU:2, one launch (start us, length us, event | category | flops | bytes accessed | tf_op | source)
XLA Modules:
  0.0 88.1 jit_solution(10242615243480781049)
XLA Ops:
  0.0 0.7 pad_add_fusion
  0.7 0.6 broadcast_in_dim.20
  1.3 7.5 %all-to-all-start = ((s32[16,6,16]{2,1,0:T(8,128)}), s32[16,6,16]{2,1,0:T(8,128)S(1)}, u32[]{:S(2)}, u32[]{:S(2)}) async-start(s32[16,6,16]{2,1,0:T(8,128)} %broadcast_in_dim.20), calls=%async_computation | async-start | bytes 131072 | tf_op jit(solution)/shard_map/all_to_all | solution.py:280
  8.8 0.0 copy-start
  8.8 1.2 %copy-done = bf16[16,256,1,128]{3,1,2,0:T(8,128)(2,1)S(1)} copy-done((bf16[16,256,1,128]{3,1,2,0:T(8,128)(2,1)S(1)}, bf16[16,256,1,128]{3,1,2,0:T(8,128)(2,1)}, u32[]{:S(2)}) %copy-start) | copy-done | bytes 1048600
  10.0 0.0 copy-start.4
  10.1 0.8 copy-done.4
  10.9 0.0 copy-start.5
  10.9 0.7 copy-done.5
  11.6 0.0 copy-start.8
  11.6 0.7 copy-done.8
  12.3 0.0 copy-start.10
  12.3 0.7 copy-done.10
  12.9 0.0 copy-start.12
  12.9 0.7 copy-done.12
  13.6 0.0 copy-start.13
  13.6 0.7 copy-done.13
  14.3 0.0 copy-start.2
  14.3 1.5 %shard_map.136 = (f32[256,256]{1,0:T(8,128)S(1)}, f32[256,128]{1,0:T(8,128)S(1)}, f32[256,64]{1,0:T(8,128)S(1)}, s32[16]{0:T(128)S(1)}, s32[16]{0:T(128)S(1)}, /*index=5*/bf16[64,128]{1,0:T(8,128)(2,1)S(1)}) custom-call(s32[16]{0:T(128)S(1)} %copy-done.8, s32[16]{0:T(128)S(1)} %copy-done.12, s32[512]{0:T(512)S(1)} %copy-done.10, s32[128]{0:T(128)S(1)} %copy-done.13, ...), custom_call_target="tpu_custom_call" | custom-call | flops 16777216 | bytes 1572864 | tf_op jit(solution)/shard_map/pallas_call | solution.py:282
  15.8 0.0 all-to-all-done.shared_ref
  15.8 0.0 copy-start.1
  15.8 1.2 %copy-done.1 = bf16[16,256,1,128]{3,1,2,0:T(8,128)(2,1)S(1)} copy-done((bf16[16,256,1,128]{3,1,2,0:T(8,128)(2,1)S(1)}, bf16[16,256,1,128]{3,1,2,0:T(8,128)(2,1)}, u32[]{:S(2)}) %copy-start.1) | copy-done | bytes 1048600
  17.0 0.0 copy-start.6
  17.0 0.7 copy-done.6
  17.7 0.0 copy-start.7
  17.7 0.7 copy-done.7
  18.4 0.0 copy-start.9
  18.4 0.7 copy-done.9
  19.1 0.0 copy-start.11
  19.1 0.7 copy-done.11
  19.7 3.3 %shard_map.137 = (bf16[64,512]{1,0:T(8,128)(2,1)S(1)}, bf16[128,640]{1,0:T(8,128)(2,1)}) custom-call(s32[16]{0:T(128)S(1)} %copy-done.9, s32[512]{0:T(512)S(1)} %copy-done.11, s32[4,16]{1,0:T(4,128)S(1)} %copy-done.7, s32[16]{0:T(128)S(1)} %get-tuple-element.13.flat_ref, s32[16]{0:T(128)S(1)} %get-tuple-element.14.held_ref, ...), custom_call_target="tpu_custom_call" | custom-call | flops 16777216 | bytes 1572864 | tf_op jit(solution)/shard_map/pallas_call | solution.py:306
  23.0 7.2 %all-to-all-start.2 = ((bf16[16,8,640]{2,1,0:T(8,128)(2,1)}), bf16[16,8,640]{2,1,0:T(8,128)(2,1)S(1)}, u32[]{:S(2)}, u32[]{:S(2)}) async-start(bf16[16,8,640]{2,1,0:T(8,128)(2,1)} %bitcast.7), calls=%async_computation.2 | async-start | bytes 327680 | tf_op jit(solution)/shard_map/all_to_all | solution.py:327
  30.3 0.0 copy-start.3
  30.3 2.9 %shard_map.139 = bf16[8,64,512]{2,1,0:T(8,128)(2,1)S(1)} custom-call(bf16[64,512]{1,0:T(8,128)(2,1)S(1)} %get-tuple-element.18.rows_ref, bf16[512,8192]{1,0:T(8,128)(2,1)} %weight_ref.3), custom_call_target="tpu_custom_call" | custom-call | flops 268435456 | bytes 4194304 | tf_op jit(solution)/shard_map/pallas_call | solution.py:330
  33.1 0.1 collective-permute-start
  33.2 3.8 %all-to-all-done.2 = bf16[16,8,640]{2,1,0:T(8,128)(2,1)S(1)} async-done(((bf16[16,8,640]{2,1,0:T(8,128)(2,1)}), bf16[16,8,640]{2,1,0:T(8,128)(2,1)S(1)}, u32[]{:S(2)}, u32[]{:S(2)}) %all-to-all-start.2) | async-done | bytes 163872 | tf_op jit(solution)/shard_map/all_to_all | solution.py:327
  37.1 0.0 copy-done.2
  37.1 0.4 shard_map.140
  37.5 0.1 collective-permute-start.1
  37.6 1.2 %collective-permute-done.1 = f32[64,128]{1,0:T(8,128)S(1)} collective-permute-done((f32[64,128]{1,0:T(8,128)S(1)}, f32[64,128]{1,0:T(8,128)S(1)}, u32[]{:S(2)}, u32[]{:S(2)}) %collective-permute-start.1) | collective-permute-done | bytes 32800 | tf_op jit(solution)/shard_map/ppermute | solution.py:358
  38.8 0.7 broadcast_in_dim.21
  39.5 8.5 %all-to-all-start.3 = ((bf16[8,64,128]{2,1,0:T(8,128)(2,1)}), bf16[8,64,128]{2,1,0:T(8,128)(2,1)S(1)}, u32[]{:S(2)}, u32[]{:S(2)}) async-start(bf16[8,64,128]{2,1,0:T(8,128)(2,1)} %broadcast_in_dim.21), calls=%async_computation.3 | async-start | bytes 262144 | tf_op jit(solution)/shard_map/all_to_all | solution.py:360
  47.9 2.8 %shard_map.138 = f32[8,64,512]{2,1,0:T(8,128)S(1)} custom-call(bf16[64,512]{1,0:T(8,128)(2,1)S(1)} %get-tuple-element.18.rows_ref, bf16[512,8192]{1,0:T(8,128)(2,1)} %weight_ref.3), custom_call_target="tpu_custom_call" | custom-call | flops 268435456 | bytes 4194304 | tf_op jit(solution)/shard_map/pallas_call | solution.py:330
  50.7 6.6 %all-to-all-done.3.parts_ref = bf16[8,64,128]{2,1,0:T(8,128)(2,1)S(1)} async-done(((bf16[8,64,128]{2,1,0:T(8,128)(2,1)}), bf16[8,64,128]{2,1,0:T(8,128)(2,1)S(1)}, u32[]{:S(2)}, u32[]{:S(2)}) %all-to-all-start.3) | async-done | bytes 131104 | tf_op jit(solution)/shard_map/all_to_all | solution.py:360
  57.3 0.0 copy-done.3
  57.3 0.9 %shard_map.141 = bf16[128,512]{1,0:T(8,128)(2,1)} custom-call(bf16[8,64,128]{2,1,0:T(8,128)(2,1)S(1)} %all-to-all-done.3.parts_ref, bf16[128,128]{1,0:T(8,128)(2,1)S(1)} %slice.9.held_ref, bf16[8,64,512]{2,1,0:T(8,128)(2,1)S(1)} %copy-done.3), custom_call_target="tpu_custom_call" | custom-call | flops 67108864 | bytes 262144 | tf_op jit(solution)/shard_map/pallas_call | solution.py:362
  58.2 4.8 %all-to-all-start.4 = ((bf16[16,8,512]{2,1,0:T(8,128)(2,1)}), bf16[16,8,512]{2,1,0:T(8,128)(2,1)S(1)}, u32[]{:S(2)}, u32[]{:S(2)}) async-start(bf16[16,8,512]{2,1,0:T(8,128)(2,1)} %bitcast.9), calls=%async_computation.4 | async-start | bytes 262144 | tf_op jit(solution)/shard_map/all_to_all | solution.py:370
  63.0 0.0 collective-permute-done
  63.0 0.2 add_convert_fusion
  63.2 6.5 %all-to-all-done.4 = bf16[16,8,512]{2,1,0:T(8,128)(2,1)S(1)} async-done(((bf16[16,8,512]{2,1,0:T(8,128)(2,1)}), bf16[16,8,512]{2,1,0:T(8,128)(2,1)S(1)}, u32[]{:S(2)}, u32[]{:S(2)}) %all-to-all-start.4) | async-done | bytes 131104 | tf_op jit(solution)/shard_map/all_to_all | solution.py:370
  69.7 17.6 %all_to_all.38.base_ref = bf16[8,64,512]{2,1,0:T(8,128)(2,1)S(1)} all-to-all(bf16[8,64,512]{2,1,0:T(8,128)(2,1)S(1)} %add_convert_fusion), channel_id=1, replica_groups=mesh['batch'=16,'z'=8,'core'=2] {'z'}, dimensions={0} | all-to-all | bytes 1048576 | tf_op jit(solution)/shard_map/all_to_all | solution.py:361
  87.3 0.8 shard_map.142
  (3 shorter events, 0.0 us)
Async XLA Ops:
  1.3 14.4 %all-to-all-start = ((s32[16,6,16]{2,1,0:T(8,128)}), s32[16,6,16]{2,1,0:T(8,128)S(1)}, u32[]{:S(2)}, u32[]{:S(2)}) async-start(s32[16,6,16]{2,1,0:T(8,128)} %broadcast_in_dim.20), calls=%async_computation | async-start | bytes 131072 | tf_op jit(solution)/shard_map/all_to_all | solution.py:280
  8.8 1.2 %copy-start = (bf16[16,256,1,128]{3,1,2,0:T(8,128)(2,1)S(1)}, bf16[16,256,1,128]{3,1,2,0:T(8,128)(2,1)}, u32[]{:S(2)}) copy-start(bf16[16,256,1,128]{3,1,2,0:T(8,128)(2,1)} %param.15) | copy-start | bytes 3145732
  10.0 0.8 copy-start.4
  10.9 0.7 copy-start.5
  11.6 0.7 copy-start.8
  12.3 0.7 copy-start.10
  12.9 0.7 copy-start.12
  13.6 0.7 copy-start.13
  14.3 22.8 %copy-start.2 = (bf16[8,64,512]{2,1,0:T(8,128)(2,1)S(1)}, bf16[8,64,512]{2,1,0:T(8,128)(2,1)}, u32[]{:S(2)}) copy-start(bf16[8,64,512]{2,1,0:T(8,128)(2,1)} %down_ref.1) | copy-start | bytes 1572868
  15.8 1.2 %copy-start.1 = (bf16[16,256,1,128]{3,1,2,0:T(8,128)(2,1)S(1)}, bf16[16,256,1,128]{3,1,2,0:T(8,128)(2,1)}, u32[]{:S(2)}) copy-start(bf16[16,256,1,128]{3,1,2,0:T(8,128)(2,1)} %param.16) | copy-start | bytes 3145732
  17.0 0.7 copy-start.6
  17.7 0.7 copy-start.7
  18.4 0.7 copy-start.9
  19.1 0.7 copy-start.11
  23.0 14.0 %all-to-all-start.2 = ((bf16[16,8,640]{2,1,0:T(8,128)(2,1)}), bf16[16,8,640]{2,1,0:T(8,128)(2,1)S(1)}, u32[]{:S(2)}, u32[]{:S(2)}) async-start(bf16[16,8,640]{2,1,0:T(8,128)(2,1)} %bitcast.7), calls=%async_computation.2 | async-start | bytes 327680 | tf_op jit(solution)/shard_map/all_to_all | solution.py:327
  30.3 27.0 %copy-start.3 = (bf16[8,64,512]{2,1,0:T(8,128)(2,1)S(1)}, bf16[8,64,512]{2,1,0:T(8,128)(2,1)}, u32[]{:S(2)}) copy-start(bf16[8,64,512]{2,1,0:T(8,128)(2,1)} %up_ref.1) | copy-start | bytes 1572868
  33.1 29.9 %collective-permute-start = (bf16[8,64,512]{2,1,0:T(8,128)(2,1)S(1)}, bf16[8,64,512]{2,1,0:T(8,128)(2,1)S(1)}, u32[]{:S(2)}, u32[]{:S(2)}) collective-permute-start(bf16[8,64,512]{2,1,0:T(8,128)(2,1)S(1)} %shard_map.139), channel_id=1, source_target_pairs={{0,1},{1,0},{2,3},{3,2},{4,5},{5,4},{6,7},{7,6},{8,9},{9,8},{10,11... | collective-permute-start | bytes 1572872 | tf_op jit(solution)/shard_map/ppermute | solution.py:344
  37.5 1.3 %collective-permute-start.1 = (f32[64,128]{1,0:T(8,128)S(1)}, f32[64,128]{1,0:T(8,128)S(1)}, u32[]{:S(2)}, u32[]{:S(2)}) collective-permute-start(f32[64,128]{1,0:T(8,128)S(1)} %shard_map.140), channel_id=1, source_target_pairs={{0,1},{1,0},{2,3},{3,2},{4,5},{5,4},{6,7},{7,6},{8,9},{9,8},{10,11... | collective-permute-start | bytes 98312 | tf_op jit(solution)/shard_map/ppermute | solution.py:358
  39.5 17.9 %all-to-all-start.3 = ((bf16[8,64,128]{2,1,0:T(8,128)(2,1)}), bf16[8,64,128]{2,1,0:T(8,128)(2,1)S(1)}, u32[]{:S(2)}, u32[]{:S(2)}) async-start(bf16[8,64,128]{2,1,0:T(8,128)(2,1)} %broadcast_in_dim.21), calls=%async_computation.3 | async-start | bytes 262144 | tf_op jit(solution)/shard_map/all_to_all | solution.py:360
  58.2 11.5 %all-to-all-start.4 = ((bf16[16,8,512]{2,1,0:T(8,128)(2,1)}), bf16[16,8,512]{2,1,0:T(8,128)(2,1)S(1)}, u32[]{:S(2)}, u32[]{:S(2)}) async-start(bf16[16,8,512]{2,1,0:T(8,128)(2,1)} %bitcast.9), calls=%async_computation.4 | async-start | bytes 262144 | tf_op jit(solution)/shard_map/all_to_all | solution.py:370

commit v2 on v0

v2 whole, which is shorter than its diff:
```python
import functools

import jax
import jax.numpy as jnp
from jax import lax
from jax.experimental import pallas as pl
from jax.experimental.pallas import tpu as pltpu
from jax.sharding import Mesh
from jax.sharding import PartitionSpec as P

adapter_scale = 2.0
capacity = 2
lanes = 128
f32 = jnp.float32
bf16 = jnp.bfloat16
VMEM = pl.BlockSpec(memory_space=pltpu.VMEM)
SMEM = pl.BlockSpec(memory_space=pltpu.SMEM)
HBM = pl.BlockSpec(memory_space=pltpu.HBM)


def in_hbm(array):
    return pltpu.with_memory_space_constraint(array, pltpu.HBM)


def in_vmem(array):
    return pltpu.with_memory_space_constraint(array, pltpu.VMEM)


def iota(shape, axis):
    return lax.broadcasted_iota(jnp.int32, shape, axis)


def dot(a, b):
    return jnp.dot(a, b, preferred_element_type=f32)


def dot_t(a, b):
    return lax.dot_general(a, b, (((1,), (1,)), ((), ())), preferred_element_type=f32)


def call(kernel, out_shape, in_specs, out_specs, flops, moved, scratch=(), limit=16 << 20):
    return pl.pallas_call(
        kernel,
        out_shape=out_shape,
        in_specs=in_specs,
        out_specs=out_specs,
        scratch_shapes=list(scratch),
        cost_estimate=pl.CostEstimate(flops=flops, bytes_accessed=moved, transcendentals=0),
        compiler_params=pltpu.CompilerParams(vmem_limit_bytes=limit),
    )


def fetch_all(pairs, sems):
    copies = []
    for index, (source, target) in enumerate(pairs):
        copy = pltpu.make_async_copy(source, target, sems.at[index])
        copy.start()
        copies.append(copy)
    return copies


def one_hot(wanted, shape):
    return (wanted == iota(shape, 1)).astype(f32).astype(bf16)


def attend_kernel(
    steps,
    requests,
    heads,
    adapters_held,
    tenant_in,
    length_in,
    admitted_in,
    tenant_adapter_in,
    adapter_slot_in,
    token_in,
    query_in,
    key_in,
    value_in,
    new_key_in,
    new_value_in,
    weight_in,
    home_ref,
    send_ref,
    back_ref,
    weight_ref,
    tenant_ref,
    length_ref,
    admitted_ref,
    tenant_adapter_ref,
    adapter_slot_ref,
    token_ref,
    seen,
    query_ref,
    key_ref,
    value_ref,
    new_key_ref,
    new_value_ref,
    attended,
    own_exp,
    masses,
    sems,
):
    rows = steps * heads
    total = requests * rows
    pairs = steps * requests
    width = key_ref.shape[2]
    context = key_ref.shape[1]
    features = heads * width
    scale = width ** (-0.5)
    copies = fetch_all(
        [
            (tenant_in, tenant_ref),
            (length_in, length_ref),
            (admitted_in, admitted_ref),
            (tenant_adapter_in, tenant_adapter_ref),
            (adapter_slot_in, adapter_slot_ref),
            (token_in, token_ref),
            (query_in, query_ref),
            (new_key_in, new_key_ref),
            (new_value_in, new_value_ref),
            (key_in, key_ref),
            (value_in, value_ref),
            (weight_in, weight_ref),
        ],
        sems,
    )
    for index in range(seen.shape[0]):
        seen[index] = 0
    for copy in copies[:9]:
        copy.wait()

    me = lax.axis_index("batch")
    lane = iota((1, lanes), 1)
    place = iota((pairs, 1), 0)
    lane_of_pair = iota((1, pairs), 1)
    shared_row = iota((8, 2 * lanes), 0)
    shared_lane = iota((8, 2 * lanes), 1)
    flat_rows = jnp.zeros((pairs, 1), jnp.int32)
    flat_lanes = jnp.zeros((1, pairs), jnp.int32)
    scalars = jnp.zeros((pairs, lanes), f32)
    shared = jnp.zeros((8, 2 * lanes), f32)
    first_scalar = 3 * heads * (steps - 1)
    for r in range(requests):
        tenant = tenant_ref[r]
        tokens = token_ref[tenant]
        slot = adapter_slot_ref[tenant_adapter_ref[tenant]]
        holder = slot // adapters_held
        position = seen[holder]
        seen[holder] = position + 1
        flat = (holder * capacity + position) * steps
        flat_rows = jnp.where(place // steps == r, flat, flat_rows)
        flat_lanes = jnp.where(lane_of_pair // steps == r, flat, flat_lanes)
        tenant_parts = [tenant // 16, tenant % 16]
        admits = [admitted_ref[s, r] for s in range(steps)]
        own = [slot - holder * adapters_held] + tenant_parts + [tokens // 32, tokens % 32] + admits
        line = jnp.zeros((1, lanes), jnp.int32)
        for index, value in enumerate(own):
            line = jnp.where(lane == first_scalar + index, value, line)
        scalars = jnp.where(place // steps == r, line.astype(f32), scalars)
        column = jnp.zeros((8, 2 * lanes), jnp.int32)
        for index, value in enumerate(tenant_parts + [length_ref[r]] + admits):
            column = jnp.where(shared_row == index, value, column)
        shared = jnp.where(shared_lane == me * requests + r, column.astype(f32), shared)
    flat_rows = flat_rows + place % steps
    flat_lanes = flat_lanes + lane_of_pair % steps
    back_ref[...] = one_hot(flat_rows, back_ref.shape)

    by_head = jnp.concatenate(
        [query_ref[:, h * width : (h + 1) * width] for h in range(heads)], axis=0
    )
    row = iota((total, total), 0)
    wanted = (row % heads) * pairs + ((row // heads) % steps) * requests + row // rows
    by_request = dot(one_hot(wanted, (total, total)), by_head).astype(bf16)
    new_scores = dot_t(by_request, new_key_ref[...]) * scale
    row = iota((total, 1), 0)
    new_column = iota((total, pairs), 1)
    by_step = [
        jnp.sum(
            jnp.where(new_column == j * requests + row // rows, new_scores, 0.0),
            axis=1,
            keepdims=True,
        )
        for j in range(steps)
    ]
    step_of_row = (row // heads) % steps
    own_score = by_step[0]
    for s in range(1, steps):
        own_score = jnp.where(step_of_row == s, by_step[s], own_score)
    own_place = new_column == step_of_row * requests + row // rows
    position = iota((rows, context), 1)
    copies[9].wait()
    copies[10].wait()
    for r in range(requests):
        block = pl.ds(r * rows, rows)
        scores = dot_t(by_request[r * rows : (r + 1) * rows], key_ref[r]) * scale
        scores = jnp.where(position < length_ref[r], scores, -jnp.inf)
        own = own_score[r * rows : (r + 1) * rows]
        top = jnp.maximum(jnp.max(scores, axis=1, keepdims=True), own)
        weight = jnp.exp(scores - top)
        own_weight = jnp.exp(own - top)
        mass = jnp.sum(weight, axis=1, keepdims=True) + own_weight
        inverse = 1.0 / mass
        attended[block, :] = dot((weight * inverse).astype(bf16), value_ref[r])
        own_exp[block, :] = jnp.broadcast_to(own_weight * inverse, (rows, lanes))
        masses[block, :] = jnp.broadcast_to(top + jnp.log(mass), (rows, lanes))
    own_weights = jnp.where(own_place, own_exp[:, 0:pairs], 0.0).astype(bf16)
    result = (attended[...] + dot(own_weights, new_value_ref[...])).astype(bf16)

    row = iota((total, total), 0)
    wanted = (row % pairs) * heads + row // pairs
    by_head = dot(one_hot(wanted, (total, total)), result).astype(bf16)
    for h in range(heads):
        home_ref[:, h * width : (h + 1) * width] = by_head[h * pairs : (h + 1) * pairs]
    place = iota((pairs, 1), 0)
    wanted = (place % steps) * requests + place // steps
    values = dot(one_hot(wanted, (pairs, pairs)), new_value_ref[...])
    home_ref[:, features : features + width] = values.astype(bf16)
    row = iota((total, 1), 0)
    lane = iota((total, lanes), 1)
    log_mass = masses[:, 0:1]
    pieces = jnp.zeros((total, lanes), f32)
    for j in range(steps - 1):
        rest = by_step[j] - log_mass
        for piece in range(3):
            part = rest.astype(bf16).astype(f32)
            rest = rest - part
            target = (piece * (steps - 1) + j) * heads + row % heads
            pieces = jnp.where(lane == target, part, pieces)
    gather = (iota((pairs, total), 1) // heads == iota((pairs, total), 0)).astype(f32).astype(bf16)
    scalars = scalars + dot(gather, pieces.astype(bf16))
    home_ref[:, features + width :] = scalars.astype(bf16)
    slots = send_ref.shape[0]
    pick = (iota((slots, pairs), 0) == flat_lanes).astype(f32).astype(bf16)
    sent = features + width + lanes
    send_ref[:, 0:sent] = dot(pick, home_ref[...]).astype(bf16)
    spread = (iota((slots, 8), 0) % 8 == iota((slots, 8), 1)).astype(f32).astype(bf16)
    send_ref[:, sent:] = dot(spread, shared.astype(bf16)).astype(bf16)
    copies[11].wait()


def combine_kernel(
    steps,
    heads,
    width,
    threshold,
    got_ref,
    home_ref,
    down_ref,
    weight_ref,
    low_ref,
    theirs_ref,
    ours_ref,
    rows_ref,
    final_ref,
):
    slots, pairs = got_ref.shape[0], home_ref.shape[0]
    features = heads * width
    sent = features + width + lanes
    count = slots + pairs
    shared = got_ref[0:8, sent:].astype(f32)
    for start in range(8, slots, 8):
        shared = shared + got_ref[start : start + 8, sent:].astype(f32)
    tenants = shared[0:1] * 16.0 + shared[1:2]
    charge_rows = []
    for s in range(steps - 1):
        charge = shared[2:3] + (s + 1.0)
        upper = jnp.floor(charge * (1.0 / 16.0))
        admitted = shared[3 + s : 4 + s]
        charge_rows += [upper * admitted, (charge - upper * 16.0) * admitted]
    charge_rows += [jnp.zeros_like(tenants)] * (8 - len(charge_rows))
    charges = jnp.concatenate(charge_rows, axis=0).astype(bf16)

    block = features + width
    scalars = jnp.concatenate(
        [got_ref[:, block:sent].astype(f32), home_ref[:, block:sent].astype(f32)], axis=0
    )
    first = 3 * heads * (steps - 1)
    tenant = scalars[:, first + 1 : first + 2] * 16.0 + scalars[:, first + 2 : first + 3]
    tokens = scalars[:, first + 3 : first + 4] * 32.0 + scalars[:, first + 4 : first + 5]
    same = (tenant == tenants).astype(f32).astype(bf16)
    grows = dot_t(same, charges)
    step_of_row = iota((count, 1), 0) % steps
    served_now = jnp.zeros((count, 1), f32)
    served = []
    for s in range(steps):
        open_now = (tokens < threshold).astype(f32)
        flag = open_now * scalars[:, first + 5 + s : first + 6 + s]
        served.append(flag)
        served_now = jnp.where(step_of_row == s, flag, served_now)
        if s + 1 < steps:
            grow = grows[:, 2 * s : 2 * s + 1] * 16.0 + grows[:, 2 * s + 1 : 2 * s + 2]
            tokens = tokens + open_now * grow

    span = heads * (steps - 1)
    logs = scalars[:, 0:span] + scalars[:, span : 2 * span] + scalars[:, 2 * span : 3 * span]
    shown = [(served[j] > 0.5) & (step_of_row > j) for j in range(steps - 1)]
    by_step = [
        jnp.where(shown[j], logs[:, j * heads : (j + 1) * heads], -jnp.inf)
        for j in range(steps - 1)
    ]
    top = jnp.zeros((count, heads), f32)
    for j in range(steps - 1):
        top = jnp.maximum(top, by_step[j])
    old = jnp.exp(-top)
    new = [jnp.exp(by_step[j] - top) for j in range(steps - 1)]
    mass = old
    for j in range(steps - 1):
        mass = mass + new[j]
    inverse = served_now / mass
    old = old * inverse
    new = [weight * inverse for weight in new]
    values = jnp.concatenate(
        [got_ref[:, features:block], home_ref[:, features:block]], axis=0
    )
    row = iota((count, 1), 0)
    new_values = [
        dot(one_hot(row - row % steps + j, (count, count)), values) for j in range(steps - 1)
    ]
    for h in range(heads):
        part = slice(h * width, (h + 1) * width)
        rows = jnp.concatenate([got_ref[:, part], home_ref[:, part]], axis=0).astype(f32)
        rows = rows * old[:, h : h + 1]
        for j in range(steps - 1):
            rows = rows + new_values[j] * new[j][:, h : h + 1]
        rows = rows.astype(bf16)
        rows_ref[:, part] = rows[0:slots]
        final_ref[:, part] = rows[slots:]

    rank = down_ref.shape[1]
    every = down_ref.shape[0] * rank
    product = dot_t(rows_ref[...], down_ref[...].reshape(every, features))
    owner = (iota(product.shape, 1) // rank).astype(f32)
    product = jnp.where(owner == scalars[0:slots, first : first + 1], product, 0.0)
    folded = product[:, 0:lanes]
    for start in range(lanes, every, lanes):
        folded = folded + product[:, start : start + lanes]
    folded = folded + pltpu.roll(folded, rank, 1)
    half = slots // 2
    low_half = iota((half, lanes), 1) < rank
    low_ref[...] = jnp.where(low_half, folded[0:half], folded[half:])
    parts, _, size = ours_ref.shape
    core = lax.axis_index("core")
    here = lax.axis_index("z")
    for out_ref, column in ((theirs_ref, 1 - core), (ours_ref, core)):
        for part in range(parts):
            target = lax.rem(here + part, parts)
            start = pl.multiple_of((2 * target + column) * size, size)
            product = dot(final_ref[...], weight_ref[:, pl.ds(start, size)])
            out_ref[part] = product.astype(out_ref.dtype)


def spread_kernel(low_ref, low_other_ref, base_ref, low_out):
    low = (low_ref[...] + low_other_ref[...]).astype(bf16)
    for part in range(low_out.shape[0]):
        low_out[part] = low


def mix_kernel(ours_ref, theirs_ref, base_out):
    for part in range(base_out.shape[0]):
        base_out[part] = (ours_ref[part] + theirs_ref[part].astype(f32)).astype(bf16)


def hop_kernel(distance, own_ref, first_ref, second_ref, first_out, second_out):
    back = own_ref.shape[0] - distance
    first_out[...] = (first_ref[...].astype(f32) + own_ref[distance].astype(f32)).astype(bf16)
    second_out[...] = (second_ref[...].astype(f32) + own_ref[back].astype(f32)).astype(bf16)


def start_kernel(distance, own_ref, first_ref, first_out, second_out):
    back = own_ref.shape[0] - distance
    first_out[...] = (first_ref[...].astype(f32) + own_ref[distance].astype(f32)).astype(bf16)
    second_out[...] = own_ref[back]


def up_kernel(first_scalar, parts_ref, held_ref, up_ref, out_ref):
    rank = up_ref.shape[1]
    every = up_ref.shape[0] * rank
    low = parts_ref[0].astype(f32)
    for part in range(1, parts_ref.shape[0]):
        low = low + parts_ref[part].astype(f32)
    other = pltpu.roll(low, rank, 1)
    first = iota(low.shape, 1) < rank
    low = jnp.concatenate(
        [jnp.where(first, low, other), jnp.where(first, other, low)], axis=0
    )
    wide = jnp.concatenate([low] * (every // lanes), axis=1)
    owner = (iota(wide.shape, 1) // rank).astype(f32)
    held = held_ref[:, first_scalar : first_scalar + 1].astype(f32)
    wide = jnp.where(owner == held, wide, 0.0).astype(bf16)
    out_ref[...] = dot(wide, up_ref[...].reshape(every, up_ref.shape[2])).astype(bf16)


def finish_kernel(steps, own_ref, first_ref, second_ref, back_ref, term_ref, out_ref):
    pairs = out_ref.shape[0]
    total = own_ref[0].astype(f32) + first_ref[...].astype(f32) + second_ref[...].astype(f32)
    term = dot(back_ref[...], term_ref[...])
    rows = (total + adapter_scale * term).astype(bf16)
    place = iota((pairs, 1), 0)
    requests = pairs // steps
    wanted = (place % requests) * steps + place // requests
    out_ref[...] = dot(one_hot(wanted, (pairs, pairs)), rows).astype(bf16)


def per_device(
    queries,
    cache_keys,
    cache_values,
    new_keys,
    new_values,
    lengths,
    admitted,
    request_tenant,
    tenant_adapter,
    adapter_slot,
    tenant_tokens,
    out_weight,
    adapter_down_factor,
    adapter_up_factor,
):
    holders = lax.axis_size("batch")
    parts = lax.axis_size("z")
    steps, requests, features = queries.shape
    context, width = cache_keys.shape[1], cache_keys.shape[3]
    heads = features // width
    rows = steps * heads
    total = requests * rows
    pairs = steps * requests
    adapters_held, rank, _ = adapter_down_factor.shape
    every = adapters_held * rank
    threshold = float(3 * context)
    slots = holders * capacity * steps
    first_scalar = 3 * heads * (steps - 1)
    sent = features + width + lanes
    shape = jax.ShapeDtypeStruct

    home, send, back, weight = call(
        functools.partial(attend_kernel, steps, requests, heads, adapters_held),
        (
            shape((pairs, sent), bf16),
            shape((slots, sent + 2 * lanes), bf16),
            shape((pairs, slots), bf16),
            pltpu.VMEM(out_weight.shape, bf16),
        ),
        [HBM] * 12,
        (VMEM,) * 4,
        4 * total * context * width,
        4 * cache_keys.size,
        [
            pltpu.SMEM((requests,), jnp.int32),
            pltpu.SMEM((requests,), jnp.int32),
            pltpu.SMEM((steps, requests), jnp.int32),
            pltpu.SMEM(tenant_adapter.shape, jnp.int32),
            pltpu.SMEM(adapter_slot.shape, jnp.int32),
            pltpu.SMEM(tenant_tokens.shape, jnp.int32),
            pltpu.SMEM((holders,), jnp.int32),
            pltpu.VMEM((pairs, features), bf16),
            pltpu.VMEM((requests, context, width), bf16),
            pltpu.VMEM((requests, context, width), bf16),
            pltpu.VMEM((pairs, width), bf16),
            pltpu.VMEM((pairs, width), bf16),
            pltpu.VMEM((total, width), f32),
            pltpu.VMEM((total, lanes), f32),
            pltpu.VMEM((total, lanes), f32),
            pltpu.SemaphoreType.DMA((12,)),
        ],
        40 << 20,
    )(
        *map(
            in_hbm,
            (
                request_tenant,
                lengths,
                admitted,
                tenant_adapter,
                adapter_slot,
                tenant_tokens,
                queries.reshape(pairs, features),
                cache_keys.reshape(requests, context, width),
                cache_values.reshape(requests, context, width),
                new_keys.reshape(pairs, width),
                new_values.reshape(pairs, width),
                out_weight,
            ),
        )
    )
    got = lax.all_to_all(send, "batch", split_axis=0, concat_axis=0, tiled=True)
    low, theirs, ours = call(
        functools.partial(combine_kernel, steps, heads, width, threshold),
        (
            shape((slots // 2, lanes), f32),
            shape((parts, pairs, features), bf16),
            shape((parts, pairs, features), f32),
        ),
        [VMEM] * 4,
        (VMEM,) * 3,
        2 * slots * features * every,
        out_weight.size,
        [pltpu.VMEM((slots, features), bf16), pltpu.VMEM((pairs, features), bf16)],
    )(got, home, adapter_down_factor, in_vmem(weight))
    swap = [(0, 1), (1, 0)]
    low_other = lax.ppermute(low, "core", swap)
    theirs = lax.ppermute(theirs, "core", swap)
    base = call(
        mix_kernel,
        shape((parts, pairs, features), bf16),
        [VMEM] * 2,
        VMEM,
        2 * ours.size,
        8 * ours.size,
    )(ours, theirs)
    low = call(
        spread_kernel,
        shape((parts, slots // 2, lanes), bf16),
        [VMEM, VMEM, HBM],
        VMEM,
        2 * low.size,
        24 * low.size,
    )(low, low_other, base)

    block = shape((pairs, features), bf16)
    ahead = [(i, (i + 1) % parts) for i in range(parts)]
    behind = [(i, (i - 1) % parts) for i in range(parts)]
    half = parts // 2
    forth = lax.ppermute(base[half], "z", ahead)
    low = lax.all_to_all(low, "z", split_axis=0, concat_axis=0, tiled=True)
    travelling = (forth,)
    for distance in range(half - 1, 0, -1):
        kernel = start_kernel if len(travelling) == 1 else hop_kernel
        forth, backward = call(
            functools.partial(kernel, distance),
            (block, block),
            [VMEM] * (1 + len(travelling)),
            (VMEM, VMEM),
            2 * block.size,
            12 * block.size,
        )(base, *travelling)
        travelling = (
            lax.ppermute(forth, "z", ahead),
            lax.ppermute(backward, "z", behind),
        )

    term = call(
        functools.partial(up_kernel, first_scalar),
        shape((slots, features), bf16),
        [VMEM] * 3,
        VMEM,
        2 * slots * features * every,
        4 * slots * features,
    )(low, got[:, features + width : sent], adapter_up_factor)
    term = lax.all_to_all(term, "batch", split_axis=0, concat_axis=0, tiled=True)
    out = call(
        functools.partial(finish_kernel, steps),
        block,
        [VMEM] * 5,
        VMEM,
        2 * pairs * slots * features,
        10 * block.size,
    )(base, *travelling, back, term)
    return out.reshape(steps, requests, features)


def solution(mesh):
    batch, tensor = mesh.shape["batch"], mesh.shape["tensor"]
    split = Mesh(mesh.devices.reshape(batch, tensor // 2, 2), ("batch", "z", "core"))
    tensor_axes = ("z", "core")
    placed = (
        P(None, "batch", tensor_axes),
        P("batch", None, tensor_axes, None),
        P("batch", None, tensor_axes, None),
        P(None, "batch", tensor_axes, None),
        P(None, "batch", tensor_axes, None),
        P("batch"),
        P(None, "batch"),
        P("batch"),
        P(),
        P(),
        P(),
        P(tensor_axes, None),
        P("batch", None, tensor_axes),
        P("batch", None, tensor_axes),
    )
    return jax.shard_map(
        per_device,
        mesh=split,
        in_specs=placed,
        out_specs=P(None, "batch", tensor_axes),
        check_vma=False,
    )
```

time: 274 us -> 66.6 us (0.24)
  blocking collectives: 107 us -> 14.7 us
  waiting for transfers between devices: 68 us -> 12.7 us
  matrix products: 36.8 us -> 0 us
  local copies, waits for them, and re-layouts: 17.1 us -> 0.03 us
  between operations: 13.5 us -> 0.12 us
  Pallas kernels: 0 us -> 12.7 us
  other arithmetic: 10.9 us -> 0 us
  starting transfers between devices: 19.8 us -> 25.9 us
    psum x4 -> x0, blocking collectives: 107 us -> none  [the longest x3 58.1 us: per_device(): counters = counters + lax.psum(local_table, 'batch')]
    reduce_scatter x4 -> x0, waiting for transfers between devices: 60.1 us -> none  [per_device(): lax.psum_scatter(lax.dot_general(out_weight, attended_output, (((0,), (1,...]
    dot_general x28 -> x0, matrix products: 36.8 us -> none  [the longest x4 21.7 us: per_device(): lax.dot_general(out_weight, attended_output, (((0,), (1,)), ((), ())), pr...]
    gather x10 -> x0, local copies, waits for them, and re-layouts: 14.8 us -> none  [the longest x2 4.82 us: pick_rows(): return jnp.take(merged, flat_index, axis=0)]
    all_to_all x0 -> x1, blocking collectives: none -> 14.7 us  [per_device(): got = lax.all_to_all(send, 'batch', split_axis=0, concat_axis=0, tiled=True)]
    ppermute x0 -> x9, starting transfers between devices: none -> 12.7 us  [the longest x3 9.75 us: per_device(): lax.ppermute(backward, 'z', behind)]
    pallas_call x0 -> x9, Pallas kernels: none -> 12.7 us  [the longest x1 6.93 us: per_device(): call(functools.partial(attend_kernel, steps, requests, heads, adapters_he...]
    ppermute x0 -> x9, waiting for transfers between devices: none -> 11.6 us  [the longest x1 5.75 us: per_device(): forth = lax.ppermute(base[half], 'z', ahead)]
  transfers between devices with their start and end apart: 7 -> 11, of which waited for: 3 -> 5; matrix products, arithmetic and copies ran while one was open for 21% -> 0% of each run, Pallas kernels for 0% -> 2%
where the time goes in v2:
time: 66.6 us; the launch traced here: 66.2 us
  starting transfers between devices  25.9 us (39%)
  blocking collectives  14.7 us (22%)
  Pallas kernels  12.7 us (19%)
  waiting for transfers between devices  12.7 us (19%)
    all_to_all x1, blocking collectives, per_device(): got = lax.all_to_all(send, 'batch', split_axis=0, concat_axis=0, tiled=True)  14.7 us
    ppermute x3, starting transfers between devices, per_device(): lax.ppermute(backward, 'z', behind)  9.75 us
    all_to_all x1, starting transfers between devices, per_device(): low = lax.all_to_all(low, 'z', split_axis=0, concat_axis=0, tiled=True)  8.46 us
    pallas_call x1, Pallas kernels, per_device(): call(functools.partial(attend_kernel, steps, requests, heads, adapters_he...  6.93 us
    ppermute x1, waiting for transfers between devices, per_device(): forth = lax.ppermute(base[half], 'z', ahead)  5.75 us
    all_to_all x1, starting transfers between devices, per_device(): lax.all_to_all(term, 'batch', split_axis=0, concat_axis=0, tiled=True)  4.76 us
    ppermute x3, waiting for transfers between devices, per_device(): lax.ppermute(forth, 'z', ahead)  4.48 us
    pallas_call x1, Pallas kernels, per_device(): call(functools.partial(combine_kernel, steps, heads, width, threshold), (...  3.02 us
  transfers between devices with their start and end apart: 11, of which 5 were waited for; matrix products, arithmetic and copies ran while one was open for 0% of the time, Pallas kernels for 2%

profile of v2, /device:TPU:2, one launch (start us, length us, event | category | flops | bytes accessed | tf_op | source)
XLA Modules:
  0.0 66.2 jit_solution(10837806374042728751)
XLA Ops:
  0.0 0.0 copy-start
  0.0 6.9 %shard_map.136 = (bf16[64,768]{1,0:T(8,128)(2,1)S(1)}, bf16[128,1024]{1,0:T(8,128)(2,1)S(1)}, bf16[64,128]{1,0:T(8,128)(2,1)S(1)}, bf16[512,8192]{1,0:T(8,128)(2,1)S(1)}) custom-call(s32[16]{0:T(128)} %tenant_in.1, s32[16]{0:T(128)} %length_in.1, s32[4,16]{1,0:T(4,128)} %admitted_in.1, s32[512]{0:T(512)} %tenant_adapter_in.1, s32[128]{0:T(128)} %adapter_slot_in.1, ...), custom_call_target="tpu_custom_call" | custom-call | flops 33554432 | bytes 2097152 | tf_op jit(solution)/shard_map/pallas_call | solution.py:437
  6.9 0.0 copy-start.1
  7.0 14.7 %all_to_all.27 = bf16[16,8,1024]{2,1,0:T(8,128)(2,1)S(1)} all-to-all(bf16[16,8,1024]{2,1,0:T(8,128)(2,1)S(1)} %bitcast.15), channel_id=1, replica_groups=mesh['batch'=16,'z'=8,'core'=2] {'batch'}, dimensions={0} | all-to-all | bytes 524288 | tf_op jit(solution)/shard_map/all_to_all | solution.py:487
  21.7 0.0 copy-done
  21.7 3.0 %shard_map.137 = (f32[64,128]{1,0:T(8,128)S(1)}, bf16[8,64,512]{2,1,0:T(8,128)(2,1)S(1)}, f32[8,64,512]{2,1,0:T(8,128)S(1)}) custom-call(bf16[128,1024]{1,0:T(8,128)(2,1)S(1)} %bitcast.12, bf16[64,768]{1,0:T(8,128)(2,1)S(1)} %get-tuple-element.19.home_ref, bf16[8,64,512]{2,1,0:T(8,128)(2,1)S(1)} %copy-done, bf16[512,8192]{1,0:T(8,128)(2,1)S(1)} %get-tuple-element.20.weight_ref), custom_call_target="tpu_custom_call" | custom-call | flops 67108864 | bytes 4194304 | tf_op jit(solution)/shard_map/pallas_call | solution.py:488
  24.7 0.1 collective-permute-start
  24.8 0.5 collective-permute-start.8
  25.3 1.4 %collective-permute-done.theirs_ref = bf16[8,64,512]{2,1,0:T(8,128)(2,1)S(1)} collective-permute-done((bf16[8,64,512]{2,1,0:T(8,128)(2,1)S(1)}, bf16[8,64,512]{2,1,0:T(8,128)(2,1)S(1)}, u32[]{:S(2)}, u32[]{:S(2)}) %collective-permute-start) | collective-permute-done | bytes 524320 | tf_op jit(solution)/shard_map/ppermute | solution.py:503
  26.7 0.1 shard_map.138.own_ref.base_ref
  26.8 0.0 collective-permute-done.8.low_other_ref
  26.8 0.7 %shard_map.142 = bf16[8,64,128]{2,1,0:T(8,128)(2,1)} custom-call(f32[64,128]{1,0:T(8,128)S(1)} %get-tuple-element.30.low_ref, f32[64,128]{1,0:T(8,128)S(1)} %collective-permute-done.8.low_other_ref, bf16[8,64,512]{2,1,0:T(8,128)(2,1)S(1)} %shard_map.138.own_ref.base_ref), custom_call_target="tpu_custom_call" | custom-call | flops 16384 | bytes 196608 | tf_op jit(solution)/shard_map/pallas_call | solution.py:512
  27.5 8.5 %all-to-all-start.1 = ((bf16[8,64,128]{2,1,0:T(8,128)(2,1)}), bf16[8,64,128]{2,1,0:T(8,128)(2,1)S(1)}, u32[]{:S(2)}, u32[]{:S(2)}) async-start(bf16[8,64,128]{2,1,0:T(8,128)(2,1)} %shard_map.142), calls=%async_computation.1 | async-start | bytes 262144 | tf_op jit(solution)/shard_map/all_to_all | solution.py:526
  36.0 2.1 %collective-permute-start.1 = (bf16[64,512]{1,0:T(8,128)(2,1)S(1)}, bf16[64,512]{1,0:T(8,128)(2,1)S(1)}, u32[]{:S(2)}, u32[]{:S(2)}) collective-permute-start(bf16[64,512]{1,0:T(8,128)(2,1)S(1)} %slice_bitcast_fusion), channel_id=1, source_target_pairs={{0,2},{2,4},{4,6},{6,8},{8,10},{10,12},{12,14},{14,0},{1,3},{3,5},... | collective-permute-start | bytes 196616 | tf_op jit(solution)/shard_map/ppermute | solution.py:525
  38.1 5.8 %collective-permute-done.1.first_ref = bf16[64,512]{1,0:T(8,128)(2,1)S(1)} collective-permute-done((bf16[64,512]{1,0:T(8,128)(2,1)S(1)}, bf16[64,512]{1,0:T(8,128)(2,1)S(1)}, u32[]{:S(2)}, u32[]{:S(2)}) %collective-permute-start.1) | collective-permute-done | bytes 65568 | tf_op jit(solution)/shard_map/ppermute | solution.py:525
  43.8 0.1 collective-permute-start.2
  43.9 3.2 %collective-permute-start.3 = (bf16[64,512]{1,0:T(8,128)(2,1)S(1)}, bf16[64,512]{1,0:T(8,128)(2,1)S(1)}, u32[]{:S(2)}, u32[]{:S(2)}) collective-permute-start(bf16[64,512]{1,0:T(8,128)(2,1)S(1)} %get-tuple-element.24), channel_id=1, source_target_pairs={{0,14},{2,0},{4,2},{6,4},{8,6},{10,8},{12,10},{14,12},{1,15},{3,1}... | collective-permute-start | bytes 196616 | tf_op jit(solution)/shard_map/ppermute | solution.py:540
  47.1 2.2 %collective-permute-done.2.first_ref = bf16[64,512]{1,0:T(8,128)(2,1)S(1)} collective-permute-done((bf16[64,512]{1,0:T(8,128)(2,1)S(1)}, bf16[64,512]{1,0:T(8,128)(2,1)S(1)}, u32[]{:S(2)}, u32[]{:S(2)}) %collective-permute-start.2) | collective-permute-done | bytes 65568 | tf_op jit(solution)/shard_map/ppermute | solution.py:539
  49.4 0.0 collective-permute-done.3.second_ref
  49.4 0.1 collective-permute-start.4
  49.5 3.3 %collective-permute-start.5 = (bf16[64,512]{1,0:T(8,128)(2,1)S(1)}, bf16[64,512]{1,0:T(8,128)(2,1)S(1)}, u32[]{:S(2)}, u32[]{:S(2)}) collective-permute-start(bf16[64,512]{1,0:T(8,128)(2,1)S(1)} %get-tuple-element.26), channel_id=1, source_target_pairs={{0,14},{2,0},{4,2},{6,4},{8,6},{10,8},{12,10},{14,12},{1,15},{3,1}... | collective-permute-start | bytes 196616 | tf_op jit(solution)/shard_map/ppermute | solution.py:540
  52.8 0.0 all-to-all-done.1.parts_ref
  52.9 0.0 copy-done.1
  52.9 0.9 %shard_map.143 = bf16[128,512]{1,0:T(8,128)(2,1)} custom-call(bf16[8,64,128]{2,1,0:T(8,128)(2,1)S(1)} %all-to-all-done.1.parts_ref, bf16[128,128]{1,0:T(8,128)(2,1)S(1)} %slice.9.held_ref, bf16[8,64,512]{2,1,0:T(8,128)(2,1)S(1)} %copy-done.1), custom_call_target="tpu_custom_call" | custom-call | flops 67108864 | bytes 262144 | tf_op jit(solution)/shard_map/pallas_call | solution.py:543
  53.8 4.8 %all-to-all-start.2 = ((bf16[16,8,512]{2,1,0:T(8,128)(2,1)}), bf16[16,8,512]{2,1,0:T(8,128)(2,1)S(1)}, u32[]{:S(2)}, u32[]{:S(2)}) async-start(bf16[16,8,512]{2,1,0:T(8,128)(2,1)} %bitcast.8), calls=%async_computation.2 | async-start | bytes 262144 | tf_op jit(solution)/shard_map/all_to_all | solution.py:551
  58.6 0.0 collective-permute-done.4.first_ref
  58.6 0.0 collective-permute-done.5.second_ref
  58.6 0.1 collective-permute-start.6
  58.7 3.2 %collective-permute-start.7 = (bf16[64,512]{1,0:T(8,128)(2,1)S(1)}, bf16[64,512]{1,0:T(8,128)(2,1)S(1)}, u32[]{:S(2)}, u32[]{:S(2)}) collective-permute-start(bf16[64,512]{1,0:T(8,128)(2,1)S(1)} %get-tuple-element.28), channel_id=1, source_target_pairs={{0,14},{2,0},{4,2},{6,4},{8,6},{10,8},{12,10},{14,12},{1,15},{3,1}... | collective-permute-start | bytes 196616 | tf_op jit(solution)/shard_map/ppermute | solution.py:540
  61.9 2.2 %collective-permute-done.6.first_ref = bf16[64,512]{1,0:T(8,128)(2,1)S(1)} collective-permute-done((bf16[64,512]{1,0:T(8,128)(2,1)S(1)}, bf16[64,512]{1,0:T(8,128)(2,1)S(1)}, u32[]{:S(2)}, u32[]{:S(2)}) %collective-permute-start.6) | collective-permute-done | bytes 65568 | tf_op jit(solution)/shard_map/ppermute | solution.py:539
  64.2 0.0 collective-permute-done.7.second_ref
  64.2 1.1 %all-to-all-done.2 = bf16[16,8,512]{2,1,0:T(8,128)(2,1)S(1)} async-done(((bf16[16,8,512]{2,1,0:T(8,128)(2,1)}), bf16[16,8,512]{2,1,0:T(8,128)(2,1)S(1)}, u32[]{:S(2)}, u32[]{:S(2)}) %all-to-all-start.2) | async-done | bytes 131104 | tf_op jit(solution)/shard_map/all_to_all | solution.py:551
  65.3 0.9 %shard_map.144 = bf16[64,512]{1,0:T(8,128)(2,1)} custom-call(bf16[8,64,512]{2,1,0:T(8,128)(2,1)S(1)} %shard_map.138.own_ref.base_ref, bf16[64,512]{1,0:T(8,128)(2,1)S(1)} %collective-permute-done.6.first_ref, bf16[64,512]{1,0:T(8,128)(2,1)S(1)} %collective-permute-done.7.second_ref, bf16[64,128]{1,0:T(8,128)(2,1)S(1)} %get-tuple-element.29.back_ref, ...), custom_call_target="tpu_custom_call" | custom-call | flops 8388608 | bytes 327680 | tf_op jit(solution)/shard_map/pallas_call | solution.py:552
  (5 shorter events, 0.1 us)
Async XLA Ops:
  0.0 21.7 %copy-start = (bf16[8,64,512]{2,1,0:T(8,128)(2,1)S(1)}, bf16[8,64,512]{2,1,0:T(8,128)(2,1)}, u32[]{:S(2)}) copy-start(bf16[8,64,512]{2,1,0:T(8,128)(2,1)} %down_ref.1) | copy-start | bytes 1572868
  6.9 45.9 %copy-start.1 = (bf16[8,64,512]{2,1,0:T(8,128)(2,1)S(1)}, bf16[8,64,512]{2,1,0:T(8,128)(2,1)}, u32[]{:S(2)}) copy-start(bf16[8,64,512]{2,1,0:T(8,128)(2,1)} %up_ref.1) | copy-start | bytes 1572868
  24.7 2.0 %collective-permute-start = (bf16[8,64,512]{2,1,0:T(8,128)(2,1)S(1)}, bf16[8,64,512]{2,1,0:T(8,128)(2,1)S(1)}, u32[]{:S(2)}, u32[]{:S(2)}) collective-permute-start(bf16[8,64,512]{2,1,0:T(8,128)(2,1)S(1)} %get-tuple-element.22), channel_id=1, source_target_pairs={{0,1},{1,0},{2,3},{3,2},{4,5},{5,4},{6,7},{7,6},{8,9},{9,8},{10,11... | collective-permute-start | bytes 1572872 | tf_op jit(solution)/shard_map/ppermute | solution.py:503
  24.8 2.0 %collective-permute-start.8 = (f32[64,128]{1,0:T(8,128)S(1)}, f32[64,128]{1,0:T(8,128)S(1)}, u32[]{:S(2)}, u32[]{:S(2)}) collective-permute-start(f32[64,128]{1,0:T(8,128)S(1)} %get-tuple-element.30.low_ref), channel_id=1, source_target_pairs={{0,1},{1,0},{2,3},{3,2},{4,5},{5,4},{6,7},{7,6},{8,9},{9,8},{10,11... | collective-permute-start | bytes 98312 | tf_op jit(solution)/shard_map/ppermute | solution.py:502
  27.5 25.4 %all-to-all-start.1 = ((bf16[8,64,128]{2,1,0:T(8,128)(2,1)}), bf16[8,64,128]{2,1,0:T(8,128)(2,1)S(1)}, u32[]{:S(2)}, u32[]{:S(2)}) async-start(bf16[8,64,128]{2,1,0:T(8,128)(2,1)} %shard_map.142), calls=%async_computation.1 | async-start | bytes 262144 | tf_op jit(solution)/shard_map/all_to_all | solution.py:526
  36.0 7.9 %collective-permute-start.1 = (bf16[64,512]{1,0:T(8,128)(2,1)S(1)}, bf16[64,512]{1,0:T(8,128)(2,1)S(1)}, u32[]{:S(2)}, u32[]{:S(2)}) collective-permute-start(bf16[64,512]{1,0:T(8,128)(2,1)S(1)} %slice_bitcast_fusion), channel_id=1, source_target_pairs={{0,2},{2,4},{4,6},{6,8},{8,10},{10,12},{12,14},{14,0},{1,3},{3,5},... | collective-permute-start | bytes 196616 | tf_op jit(solution)/shard_map/ppermute | solution.py:525
  43.8 5.6 %collective-permute-start.2 = (bf16[64,512]{1,0:T(8,128)(2,1)S(1)}, bf16[64,512]{1,0:T(8,128)(2,1)S(1)}, u32[]{:S(2)}, u32[]{:S(2)}) collective-permute-start(bf16[64,512]{1,0:T(8,128)(2,1)S(1)} %get-tuple-element.23), channel_id=1, source_target_pairs={{0,2},{2,4},{4,6},{6,8},{8,10},{10,12},{12,14},{14,0},{1,3},{3,5},... | collective-permute-start | bytes 196616 | tf_op jit(solution)/shard_map/ppermute | solution.py:539
  43.9 5.5 %collective-permute-start.3 = (bf16[64,512]{1,0:T(8,128)(2,1)S(1)}, bf16[64,512]{1,0:T(8,128)(2,1)S(1)}, u32[]{:S(2)}, u32[]{:S(2)}) collective-permute-start(bf16[64,512]{1,0:T(8,128)(2,1)S(1)} %get-tuple-element.24), channel_id=1, source_target_pairs={{0,14},{2,0},{4,2},{6,4},{8,6},{10,8},{12,10},{14,12},{1,15},{3,1}... | collective-permute-start | bytes 196616 | tf_op jit(solution)/shard_map/ppermute | solution.py:540
  49.4 9.1 %collective-permute-start.4 = (bf16[64,512]{1,0:T(8,128)(2,1)S(1)}, bf16[64,512]{1,0:T(8,128)(2,1)S(1)}, u32[]{:S(2)}, u32[]{:S(2)}) collective-permute-start(bf16[64,512]{1,0:T(8,128)(2,1)S(1)} %get-tuple-element.25), channel_id=1, source_target_pairs={{0,2},{2,4},{4,6},{6,8},{8,10},{10,12},{12,14},{14,0},{1,3},{3,5},... | collective-permute-start | bytes 196616 | tf_op jit(solution)/shard_map/ppermute | solution.py:539
  49.5 9.1 %collective-permute-start.5 = (bf16[64,512]{1,0:T(8,128)(2,1)S(1)}, bf16[64,512]{1,0:T(8,128)(2,1)S(1)}, u32[]{:S(2)}, u32[]{:S(2)}) collective-permute-start(bf16[64,512]{1,0:T(8,128)(2,1)S(1)} %get-tuple-element.26), channel_id=1, source_target_pairs={{0,14},{2,0},{4,2},{6,4},{8,6},{10,8},{12,10},{14,12},{1,15},{3,1}... | collective-permute-start | bytes 196616 | tf_op jit(solution)/shard_map/ppermute | solution.py:540
  53.8 11.5 %all-to-all-start.2 = ((bf16[16,8,512]{2,1,0:T(8,128)(2,1)}), bf16[16,8,512]{2,1,0:T(8,128)(2,1)S(1)}, u32[]{:S(2)}, u32[]{:S(2)}) async-start(bf16[16,8,512]{2,1,0:T(8,128)(2,1)} %bitcast.8), calls=%async_computation.2 | async-start | bytes 262144 | tf_op jit(solution)/shard_map/all_to_all | solution.py:551
  58.6 5.6 %collective-permute-start.6 = (bf16[64,512]{1,0:T(8,128)(2,1)S(1)}, bf16[64,512]{1,0:T(8,128)(2,1)S(1)}, u32[]{:S(2)}, u32[]{:S(2)}) collective-permute-start(bf16[64,512]{1,0:T(8,128)(2,1)S(1)} %get-tuple-element.27), channel_id=1, source_target_pairs={{0,2},{2,4},{4,6},{6,8},{8,10},{10,12},{12,14},{14,0},{1,3},{3,5},... | collective-permute-start | bytes 196616 | tf_op jit(solution)/shard_map/ppermute | solution.py:539
  58.7 5.5 %collective-permute-start.7 = (bf16[64,512]{1,0:T(8,128)(2,1)S(1)}, bf16[64,512]{1,0:T(8,128)(2,1)S(1)}, u32[]{:S(2)}, u32[]{:S(2)}) collective-permute-start(bf16[64,512]{1,0:T(8,128)(2,1)S(1)} %get-tuple-element.28), channel_id=1, source_target_pairs={{0,14},{2,0},{4,2},{6,4},{8,6},{10,8},{12,10},{14,12},{1,15},{3,1}... | collective-permute-start | bytes 196616 | tf_op jit(solution)/shard_map/ppermute | solution.py:540

commit v3 on v2

--- a/solution.py
+++ b/solution.py
@@ -250,9 +250,8 @@
     weight_ref,
     low_ref,
     theirs_ref,
-    ours_ref,
+    final_ref,
     rows_ref,
-    final_ref,
 ):
     slots, pairs = got_ref.shape[0], home_ref.shape[0]
     features = heads * width
@@ -339,38 +338,39 @@
     half = slots // 2
     low_half = iota((half, lanes), 1) < rank
     low_ref[...] = jnp.where(low_half, folded[0:half], folded[half:])
-    parts, _, size = ours_ref.shape
+    project(1, final_ref, weight_ref, theirs_ref)
+
+
+def project(flip, rows_ref, weight_ref, out_ref):
+    parts, _, width = out_ref.shape
     core = lax.axis_index("core")
+    mine = core if flip == 0 else 1 - core
     here = lax.axis_index("z")
-    for out_ref, column in ((theirs_ref, 1 - core), (ours_ref, core)):
-        for part in range(parts):
-            target = lax.rem(here + part, parts)
-            start = pl.multiple_of((2 * target + column) * size, size)
-            product = dot(final_ref[...], weight_ref[:, pl.ds(start, size)])
-            out_ref[part] = product.astype(out_ref.dtype)
-
-
-def spread_kernel(low_ref, low_other_ref, base_ref, low_out):
+    way = 1 - 2 * lax.rem(here, 2)
+    for part in range(parts):
+        target = lax.rem(here + way * part + parts, parts)
+        start = pl.multiple_of((2 * target + mine) * width, width)
+        product = dot(rows_ref[...], weight_ref[:, pl.ds(start, width)])
+        out_ref[part] = product.astype(out_ref.dtype)
+
+
+def mix_kernel(ours_ref, theirs_ref, low_ref, low_other_ref, low_out, base_out, first_out):
     low = (low_ref[...] + low_other_ref[...]).astype(bf16)
-    for part in range(low_out.shape[0]):
+    for part in range(base_out.shape[0]):
         low_out[part] = low
-
-
-def mix_kernel(ours_ref, theirs_ref, base_out):
-    for part in range(base_out.shape[0]):
         base_out[part] = (ours_ref[part] + theirs_ref[part].astype(f32)).astype(bf16)
-
-
-def hop_kernel(distance, own_ref, first_ref, second_ref, first_out, second_out):
-    back = own_ref.shape[0] - distance
-    first_out[...] = (first_ref[...].astype(f32) + own_ref[distance].astype(f32)).astype(bf16)
-    second_out[...] = (second_ref[...].astype(f32) + own_ref[back].astype(f32)).astype(bf16)
-
-
-def start_kernel(distance, own_ref, first_ref, first_out, second_out):
-    back = own_ref.shape[0] - distance
-    first_out[...] = (first_ref[...].astype(f32) + own_ref[distance].astype(f32)).astype(bf16)
-    second_out[...] = own_ref[back]
+    for index, part in enumerate((4, 3)):
+        first_out[index] = base_out[part]
+
+
+def hop_kernel(wanted, base_ref, came_ref, out_ref):
+    for index, part in enumerate(wanted):
+        total = came_ref[index].astype(f32) + base_ref[part].astype(f32)
+        out_ref[index] = total.astype(bf16)
+
+
+def late_hop_kernel(wanted, base_ref, came_ref, after_ref, out_ref):
+    hop_kernel(wanted, base_ref, came_ref, out_ref)
 
 
 def up_kernel(first_scalar, parts_ref, held_ref, up_ref, out_ref):
@@ -391,9 +391,9 @@
     out_ref[...] = dot(wide, up_ref[...].reshape(every, up_ref.shape[2])).astype(bf16)
 
 
-def finish_kernel(steps, own_ref, first_ref, second_ref, back_ref, term_ref, out_ref):
+def finish_kernel(steps, base_ref, first_ref, second_ref, back_ref, term_ref, out_ref):
     pairs = out_ref.shape[0]
-    total = own_ref[0].astype(f32) + first_ref[...].astype(f32) + second_ref[...].astype(f32)
+    total = base_ref[0].astype(f32) + first_ref[1].astype(f32) + second_ref[0].astype(f32)
     term = dot(back_ref[...], term_ref[...])
     rows = (total + adapter_scale * term).astype(bf16)
     place = iota((pairs, 1), 0)
@@ -485,61 +485,60 @@
         )
     )
     got = lax.all_to_all(send, "batch", split_axis=0, concat_axis=0, tiled=True)
-    low, theirs, ours = call(
+    low, theirs, final = call(
         functools.partial(combine_kernel, steps, heads, width, threshold),
         (
             shape((slots // 2, lanes), f32),
             shape((parts, pairs, features), bf16),
-            shape((parts, pairs, features), f32),
+            shape((pairs, features), bf16),
         ),
         [VMEM] * 4,
         (VMEM,) * 3,
         2 * slots * features * every,
         out_weight.size,
-        [pltpu.VMEM((slots, features), bf16), pltpu.VMEM((pairs, features), bf16)],
+        [pltpu.VMEM((slots, features), bf16)],
     )(got, home, adapter_down_factor, in_vmem(weight))
     swap = [(0, 1), (1, 0)]
     low_other = lax.ppermute(low, "core", swap)
     theirs = lax.ppermute(theirs, "core", swap)
-    base = call(
-        mix_kernel,
-        shape((parts, pairs, features), bf16),
+    ours = call(
+        functools.partial(project, 0),
+        shape((parts, pairs, features), f32),
         [VMEM] * 2,
         VMEM,
+        pairs * out_weight.size,
+        out_weight.size,
+    )(final, in_vmem(weight))
+    two = shape((2, pairs, features), bf16)
+    one = shape((1, pairs, features), bf16)
+    low, base, sums = call(
+        mix_kernel,
+        (
+            shape((parts, slots // 2, lanes), bf16),
+            shape((parts, pairs, features), bf16),
+            two,
+        ),
+        [VMEM] * 4,
+        (VMEM,) * 3,
         2 * ours.size,
         8 * ours.size,
-    )(ours, theirs)
-    low = call(
-        spread_kernel,
-        shape((parts, slots // 2, lanes), bf16),
-        [VMEM, VMEM, HBM],
-        VMEM,
-        2 * low.size,
-        24 * low.size,
-    )(low, low_other, base)
-
-    block = shape((pairs, features), bf16)
-    ahead = [(i, (i + 1) % parts) for i in range(parts)]
-    behind = [(i, (i - 1) % parts) for i in range(parts)]
-    half = parts // 2
-    forth = lax.ppermute(base[half], "z", ahead)
+    )(ours, theirs, low, low_other)
     low = lax.all_to_all(low, "z", split_axis=0, concat_axis=0, tiled=True)
-    travelling = (forth,)
-    for distance in range(half - 1, 0, -1):
-        kernel = start_kernel if len(travelling) == 1 else hop_kernel
-        forth, backward = call(
-            functools.partial(kernel, distance),
-            (block, block),
-            [VMEM] * (1 + len(travelling)),
-            (VMEM, VMEM),
-            2 * block.size,
-            12 * block.size,
-        )(base, *travelling)
-        travelling = (
-            lax.ppermute(forth, "z", ahead),
-            lax.ppermute(backward, "z", behind),
-        )
-
+
+    def hop(kernel, wanted, out, *args):
+        return call(
+            functools.partial(kernel, wanted),
+            out,
+            [VMEM, VMEM] + [HBM] * (len(args) - 2),
+            VMEM,
+            out.size,
+            6 * out.size,
+        )(*args)
+
+    odd = [(i, i + 1 - 2 * (i % 2)) for i in range(parts)]
+    even = [(i, (i - 1 + 2 * (i % 2)) % parts) for i in range(parts)]
+    sums = lax.ppermute(sums, "z", odd)
+    sums = lax.ppermute(hop(hop_kernel, (5, 6), two, base, sums), "z", even)
     term = call(
         functools.partial(up_kernel, first_scalar),
         shape((slots, features), bf16),
@@ -548,15 +547,18 @@
         2 * slots * features * every,
         4 * slots * features,
     )(low, got[:, features + width : sent], adapter_up_factor)
+    sums = hop(late_hop_kernel, (2, 1), two, base, sums, term)
+    sums = lax.ppermute(sums, "z", odd)
+    last = lax.ppermute(hop(hop_kernel, (7,), one, base, sums), "z", even)
     term = lax.all_to_all(term, "batch", split_axis=0, concat_axis=0, tiled=True)
     out = call(
         functools.partial(finish_kernel, steps),
-        block,
+        shape((pairs, features), bf16),
         [VMEM] * 5,
         VMEM,
         2 * pairs * slots * features,
-        10 * block.size,
-    )(base, *travelling, back, term)
+        10 * one.size,
+    )(base, sums, last, back, term)
     return out.reshape(steps, requests, features)
 
 

time: 66.6 us -> 60 us (0.901)
  starting transfers between devices: 25.9 us -> 20.4 us
  waiting for transfers between devices: 12.7 us -> 11.9 us
    ppermute x7 -> x4, waiting for transfers between devices: 10.2 us -> 0.01 us  [the longest x2 0.01 us: per_device(): sums = lax.ppermute(sums, 'z', odd)]
    all_to_all x1, waiting for transfers between devices: 0.01 us -> 5.75 us  [per_device(): low = lax.all_to_all(low, 'z', split_axis=0, concat_axis=0, tiled=True)]
    ppermute x7 -> x4, starting transfers between devices: 12.1 us -> 7.46 us  [the longest x1 3.31 us: per_device(): sums = lax.ppermute(hop(hop_kernel, (5, 6), two, base, sums), 'z', even)]
    all_to_all x1, waiting for transfers between devices: 1.1 us -> 5.54 us  [per_device(): lax.all_to_all(term, 'batch', split_axis=0, concat_axis=0, tiled=True)]
    ppermute x1, waiting for transfers between devices: 1.4 us -> 0.01 us  [per_device(): theirs = lax.ppermute(theirs, 'core', swap)]
    all_to_all x1, starting transfers between devices: 8.46 us -> 7.57 us  [per_device(): low = lax.all_to_all(low, 'z', split_axis=0, concat_axis=0, tiled=True)]
    pallas_call x6, Pallas kernels: 1.77 us -> 2.57 us  [the longest x1 0.92 us: per_device(): call(functools.partial(finish_kernel, steps), shape((pairs, features), bf...]
    pallas_call x1, Pallas kernels: 3.02 us -> 2.26 us  [per_device(): call(functools.partial(combine_kernel, steps, heads, width, threshold), (...]
  transfers between devices with their start and end apart: 11 -> 8, of which waited for: 5 -> 3; matrix products, arithmetic and copies ran while one was open for 0% -> 0% of each run, Pallas kernels for 2% -> 3%
where the time goes in v3:
time: 60 us; the launch traced here: 59.7 us
  starting transfers between devices  20.4 us (34%)
  blocking collectives  14.6 us (24%)
  Pallas kernels  12.7 us (21%)
  waiting for transfers between devices  11.9 us (20%)
    all_to_all x1, blocking collectives, per_device(): got = lax.all_to_all(send, 'batch', split_axis=0, concat_axis=0, tiled=True)  14.6 us
    all_to_all x1, starting transfers between devices, per_device(): low = lax.all_to_all(low, 'z', split_axis=0, concat_axis=0, tiled=True)  7.57 us
    pallas_call x1, Pallas kernels, per_device(): call(functools.partial(attend_kernel, steps, requests, heads, adapters_he...  6.93 us
    all_to_all x1, waiting for transfers between devices, per_device(): low = lax.all_to_all(low, 'z', split_axis=0, concat_axis=0, tiled=True)  5.75 us
    all_to_all x1, waiting for transfers between devices, per_device(): lax.all_to_all(term, 'batch', split_axis=0, concat_axis=0, tiled=True)  5.54 us
    all_to_all x1, starting transfers between devices, per_device(): lax.all_to_all(term, 'batch', split_axis=0, concat_axis=0, tiled=True)  4.76 us
    ppermute x1, starting transfers between devices, per_device(): sums = lax.ppermute(hop(hop_kernel, (5, 6), two, base, sums), 'z', even)  3.31 us
    ppermute x2, starting transfers between devices, per_device(): sums = lax.ppermute(sums, 'z', odd)  3 us
  transfers between devices with their start and end apart: 8, of which 3 were waited for; matrix products, arithmetic and copies ran while one was open for 0% of the time, Pallas kernels for 3%

profile of v3, /device:TPU:2, one launch (start us, length us, event | category | flops | bytes accessed | tf_op | source)
XLA Modules:
  0.0 59.7 jit_solution(1252574478585918842)
XLA Ops:
  0.0 0.0 copy-start
  0.0 6.9 %shard_map.136 = (bf16[64,768]{1,0:T(8,128)(2,1)S(1)}, bf16[128,1024]{1,0:T(8,128)(2,1)S(1)}, bf16[64,128]{1,0:T(8,128)(2,1)S(1)}, bf16[512,8192]{1,0:T(8,128)(2,1)S(1)}) custom-call(s32[16]{0:T(128)} %tenant_in.1, s32[16]{0:T(128)} %length_in.1, s32[4,16]{1,0:T(4,128)} %admitted_in.1, s32[512]{0:T(512)} %tenant_adapter_in.1, s32[128]{0:T(128)} %adapter_slot_in.1, ...), custom_call_target="tpu_custom_call" | custom-call | flops 33554432 | bytes 2097152 | tf_op jit(solution)/shard_map/pallas_call | solution.py:437
  6.9 14.6 %all_to_all.27 = bf16[16,8,1024]{2,1,0:T(8,128)(2,1)S(1)} all-to-all(bf16[16,8,1024]{2,1,0:T(8,128)(2,1)S(1)} %bitcast.13), channel_id=1, replica_groups=mesh['batch'=16,'z'=8,'core'=2] {'batch'}, dimensions={0} | all-to-all | bytes 524288 | tf_op jit(solution)/shard_map/all_to_all | solution.py:487
  21.5 0.0 copy-done
  21.5 2.3 %shard_map.137 = (f32[64,128]{1,0:T(8,128)S(1)}, bf16[8,64,512]{2,1,0:T(8,128)(2,1)S(1)}, bf16[64,512]{1,0:T(8,128)(2,1)S(1)}) custom-call(bf16[128,1024]{1,0:T(8,128)(2,1)S(1)} %bitcast.10, bf16[64,768]{1,0:T(8,128)(2,1)S(1)} %get-tuple-element.16.home_ref, bf16[8,64,512]{2,1,0:T(8,128)(2,1)S(1)} %copy-done, bf16[512,8192]{1,0:T(8,128)(2,1)S(1)} %get-tuple-element.17.weight_ref), custom_call_target="tpu_custom_call" | custom-call | flops 67108864 | bytes 4194304 | tf_op jit(solution)/shard_map/pallas_call | solution.py:488
  23.8 0.0 copy-start.1
  23.8 0.1 collective-permute-start
  23.9 0.5 collective-permute-start.1
  24.4 0.8 %shard_map.138.ours_ref = f32[8,64,512]{2,1,0:T(8,128)S(1)} custom-call(bf16[64,512]{1,0:T(8,128)(2,1)S(1)} %get-tuple-element.18.rows_ref, bf16[512,8192]{1,0:T(8,128)(2,1)S(1)} %get-tuple-element.17.weight_ref), custom_call_target="tpu_custom_call" | custom-call | flops 268435456 | bytes 4194304 | tf_op jit(solution)/shard_map/pallas_call | solution.py:504
  25.3 0.6 %collective-permute-done.1.low_other_ref = f32[64,128]{1,0:T(8,128)S(1)} collective-permute-done((f32[64,128]{1,0:T(8,128)S(1)}, f32[64,128]{1,0:T(8,128)S(1)}, u32[]{:S(2)}, u32[]{:S(2)}) %collective-permute-start.1) | collective-permute-done | bytes 32800 | tf_op jit(solution)/shard_map/ppermute | solution.py:502
  25.9 0.0 collective-permute-done.theirs_ref
  25.9 0.7 %shard_map.139 = (bf16[8,64,128]{2,1,0:T(8,128)(2,1)}, bf16[8,64,512]{2,1,0:T(8,128)(2,1)S(1)}, bf16[2,64,512]{2,1,0:T(8,128)(2,1)S(1)}) custom-call(f32[8,64,512]{2,1,0:T(8,128)S(1)} %shard_map.138.ours_ref, bf16[8,64,512]{2,1,0:T(8,128)(2,1)S(1)} %collective-permute-done.theirs_ref, f32[64,128]{1,0:T(8,128)S(1)} %get-tuple-element.20.low_ref, ...), custom_call_target="tpu_custom_call" | custom-call | flops 524288 | bytes 2097152 | tf_op jit(solution)/shard_map/pallas_call | solution.py:514
  26.6 1.9 %collective-permute-start.2 = (bf16[2,64,512]{2,1,0:T(8,128)(2,1)S(1)}, bf16[2,64,512]{2,1,0:T(8,128)(2,1)S(1)}, u32[]{:S(2)}, u32[]{:S(2)}) collective-permute-start(bf16[2,64,512]{2,1,0:T(8,128)(2,1)S(1)} %get-tuple-element.22), channel_id=1, source_target_pairs={{0,2},{2,0},{4,6},{6,4},{8,10},{10,8},{12,14},{14,12},{1,3},{3,1},... | collective-permute-start | bytes 393224 | tf_op jit(solution)/shard_map/ppermute | solution.py:540
  28.5 7.6 %all-to-all-start.1 = ((bf16[8,64,128]{2,1,0:T(8,128)(2,1)}), bf16[8,64,128]{2,1,0:T(8,128)(2,1)S(1)}, u32[]{:S(2)}, u32[]{:S(2)}) async-start(bf16[8,64,128]{2,1,0:T(8,128)(2,1)} %get-tuple-element.23), calls=%async_computation.1 | async-start | bytes 262144 | tf_op jit(solution)/shard_map/all_to_all | solution.py:526
  36.1 0.0 collective-permute-done.2.came_ref
  36.1 3.3 %collective-permute-start.3 = (bf16[2,64,512]{2,1,0:T(8,128)(2,1)S(1)}, bf16[2,64,512]{2,1,0:T(8,128)(2,1)S(1)}, u32[]{:S(2)}, u32[]{:S(2)}) collective-permute-start(bf16[2,64,512]{2,1,0:T(8,128)(2,1)S(1)} %shard_map.140), channel_id=1, source_target_pairs={{0,14},{2,4},{4,2},{6,8},{8,6},{10,12},{12,10},{14,0},{1,15},{3,5}... | collective-permute-start | bytes 393224 | tf_op jit(solution)/shard_map/ppermute | solution.py:541
  39.5 5.8 %all-to-all-done.1.parts_ref = bf16[8,64,128]{2,1,0:T(8,128)(2,1)S(1)} async-done(((bf16[8,64,128]{2,1,0:T(8,128)(2,1)}), bf16[8,64,128]{2,1,0:T(8,128)(2,1)S(1)}, u32[]{:S(2)}, u32[]{:S(2)}) %all-to-all-start.1) | async-done | bytes 131104 | tf_op jit(solution)/shard_map/all_to_all | solution.py:526
  45.2 0.0 copy-done.1
  45.2 0.9 %shard_map.141.after_ref = bf16[128,512]{1,0:T(8,128)(2,1)} custom-call(bf16[8,64,128]{2,1,0:T(8,128)(2,1)S(1)} %all-to-all-done.1.parts_ref, bf16[128,128]{1,0:T(8,128)(2,1)S(1)} %slice.4.held_ref, bf16[8,64,512]{2,1,0:T(8,128)(2,1)S(1)} %copy-done.1), custom_call_target="tpu_custom_call" | custom-call | flops 67108864 | bytes 262144 | tf_op jit(solution)/shard_map/pallas_call | solution.py:542
  46.2 0.0 collective-permute-done.3.came_ref
  46.2 1.1 %collective-permute-start.4 = (bf16[2,64,512]{2,1,0:T(8,128)(2,1)S(1)}, bf16[2,64,512]{2,1,0:T(8,128)(2,1)S(1)}, u32[]{:S(2)}, u32[]{:S(2)}) collective-permute-start(bf16[2,64,512]{2,1,0:T(8,128)(2,1)S(1)} %shard_map.142), channel_id=1, source_target_pairs={{0,2},{2,0},{4,6},{6,4},{8,10},{10,8},{12,14},{14,12},{1,3},{3,1},... | collective-permute-start | bytes 393224 | tf_op jit(solution)/shard_map/ppermute | solution.py:551
  47.3 4.8 %all-to-all-start.2 = ((bf16[16,8,512]{2,1,0:T(8,128)(2,1)}), bf16[16,8,512]{2,1,0:T(8,128)(2,1)S(1)}, u32[]{:S(2)}, u32[]{:S(2)}) async-start(bf16[16,8,512]{2,1,0:T(8,128)(2,1)} %bitcast.7), calls=%async_computation.2 | async-start | bytes 262144 | tf_op jit(solution)/shard_map/all_to_all | solution.py:553
  52.0 0.0 collective-permute-done.4.came_ref.first_ref
  52.1 1.1 %collective-permute-start.5 = (bf16[1,64,512]{2,1,0:T(8,128)(2,1)S(1)}, bf16[1,64,512]{2,1,0:T(8,128)(2,1)S(1)}, u32[]{:S(2)}, u32[]{:S(2)}) collective-permute-start(bf16[1,64,512]{2,1,0:T(8,128)(2,1)S(1)} %shard_map.143), channel_id=1, source_target_pairs={{0,14},{2,4},{4,2},{6,8},{8,6},{10,12},{12,10},{14,0},{1,15},{3,5}... | collective-permute-start | bytes 196616 | tf_op jit(solution)/shard_map/ppermute | solution.py:552
  53.2 5.5 %all-to-all-done.2 = bf16[16,8,512]{2,1,0:T(8,128)(2,1)S(1)} async-done(((bf16[16,8,512]{2,1,0:T(8,128)(2,1)}), bf16[16,8,512]{2,1,0:T(8,128)(2,1)S(1)}, u32[]{:S(2)}, u32[]{:S(2)}) %all-to-all-start.2) | async-done | bytes 131104 | tf_op jit(solution)/shard_map/all_to_all | solution.py:553
  58.8 0.0 collective-permute-done.5.second_ref
  58.8 0.9 %shard_map.144 = bf16[64,512]{1,0:T(8,128)(2,1)} custom-call(bf16[8,64,512]{2,1,0:T(8,128)(2,1)S(1)} %get-tuple-element.21.base_ref, bf16[2,64,512]{2,1,0:T(8,128)(2,1)S(1)} %collective-permute-done.4.came_ref.first_ref, bf16[1,64,512]{2,1,0:T(8,128)(2,1)S(1)} %collective-permute-done.5.second_ref, bf16[64,128]{1,0:T(8,128)(2,1)S(1)} %get-tuple-element.24.back_ref, ...), custom_call_target="tpu_custom_call" | custom-call | flops 8388608 | bytes 327680 | tf_op jit(solution)/shard_map/pallas_call | solution.py:554
  (4 shorter events, 0.1 us)
Async XLA Ops:
  0.0 21.5 %copy-start = (bf16[8,64,512]{2,1,0:T(8,128)(2,1)S(1)}, bf16[8,64,512]{2,1,0:T(8,128)(2,1)}, u32[]{:S(2)}) copy-start(bf16[8,64,512]{2,1,0:T(8,128)(2,1)} %down_ref.1) | copy-start | bytes 1572868
  23.8 21.4 %copy-start.1 = (bf16[8,64,512]{2,1,0:T(8,128)(2,1)S(1)}, bf16[8,64,512]{2,1,0:T(8,128)(2,1)}, u32[]{:S(2)}) copy-start(bf16[8,64,512]{2,1,0:T(8,128)(2,1)} %up_ref.1) | copy-start | bytes 1572868
  23.8 2.0 %collective-permute-start = (bf16[8,64,512]{2,1,0:T(8,128)(2,1)S(1)}, bf16[8,64,512]{2,1,0:T(8,128)(2,1)S(1)}, u32[]{:S(2)}, u32[]{:S(2)}) collective-permute-start(bf16[8,64,512]{2,1,0:T(8,128)(2,1)S(1)} %get-tuple-element.19), channel_id=1, source_target_pairs={{0,1},{1,0},{2,3},{3,2},{4,5},{5,4},{6,7},{7,6},{8,9},{9,8},{10,11... | collective-permute-start | bytes 1572872 | tf_op jit(solution)/shard_map/ppermute | solution.py:503
  23.9 1.9 %collective-permute-start.1 = (f32[64,128]{1,0:T(8,128)S(1)}, f32[64,128]{1,0:T(8,128)S(1)}, u32[]{:S(2)}, u32[]{:S(2)}) collective-permute-start(f32[64,128]{1,0:T(8,128)S(1)} %get-tuple-element.20.low_ref), channel_id=1, source_target_pairs={{0,1},{1,0},{2,3},{3,2},{4,5},{5,4},{6,7},{7,6},{8,9},{9,8},{10,11... | collective-permute-start | bytes 98312 | tf_op jit(solution)/shard_map/ppermute | solution.py:502
  26.6 9.5 %collective-permute-start.2 = (bf16[2,64,512]{2,1,0:T(8,128)(2,1)S(1)}, bf16[2,64,512]{2,1,0:T(8,128)(2,1)S(1)}, u32[]{:S(2)}, u32[]{:S(2)}) collective-permute-start(bf16[2,64,512]{2,1,0:T(8,128)(2,1)S(1)} %get-tuple-element.22), channel_id=1, source_target_pairs={{0,2},{2,0},{4,6},{6,4},{8,10},{10,8},{12,14},{14,12},{1,3},{3,1},... | collective-permute-start | bytes 393224 | tf_op jit(solution)/shard_map/ppermute | solution.py:540
  28.5 16.7 %all-to-all-start.1 = ((bf16[8,64,128]{2,1,0:T(8,128)(2,1)}), bf16[8,64,128]{2,1,0:T(8,128)(2,1)S(1)}, u32[]{:S(2)}, u32[]{:S(2)}) async-start(bf16[8,64,128]{2,1,0:T(8,128)(2,1)} %get-tuple-element.23), calls=%async_computation.1 | async-start | bytes 262144 | tf_op jit(solution)/shard_map/all_to_all | solution.py:526
  36.1 10.0 %collective-permute-start.3 = (bf16[2,64,512]{2,1,0:T(8,128)(2,1)S(1)}, bf16[2,64,512]{2,1,0:T(8,128)(2,1)S(1)}, u32[]{:S(2)}, u32[]{:S(2)}) collective-permute-start(bf16[2,64,512]{2,1,0:T(8,128)(2,1)S(1)} %shard_map.140), channel_id=1, source_target_pairs={{0,14},{2,4},{4,2},{6,8},{8,6},{10,12},{12,10},{14,0},{1,15},{3,5}... | collective-permute-start | bytes 393224 | tf_op jit(solution)/shard_map/ppermute | solution.py:541
  46.2 5.8 %collective-permute-start.4 = (bf16[2,64,512]{2,1,0:T(8,128)(2,1)S(1)}, bf16[2,64,512]{2,1,0:T(8,128)(2,1)S(1)}, u32[]{:S(2)}, u32[]{:S(2)}) collective-permute-start(bf16[2,64,512]{2,1,0:T(8,128)(2,1)S(1)} %shard_map.142), channel_id=1, source_target_pairs={{0,2},{2,0},{4,6},{6,4},{8,10},{10,8},{12,14},{14,12},{1,3},{3,1},... | collective-permute-start | bytes 393224 | tf_op jit(solution)/shard_map/ppermute | solution.py:551
  47.3 11.5 %all-to-all-start.2 = ((bf16[16,8,512]{2,1,0:T(8,128)(2,1)}), bf16[16,8,512]{2,1,0:T(8,128)(2,1)S(1)}, u32[]{:S(2)}, u32[]{:S(2)}) async-start(bf16[16,8,512]{2,1,0:T(8,128)(2,1)} %bitcast.7), calls=%async_computation.2 | async-start | bytes 262144 | tf_op jit(solution)/shard_map/all_to_all | solution.py:553
  52.1 6.7 %collective-permute-start.5 = (bf16[1,64,512]{2,1,0:T(8,128)(2,1)S(1)}, bf16[1,64,512]{2,1,0:T(8,128)(2,1)S(1)}, u32[]{:S(2)}, u32[]{:S(2)}) collective-permute-start(bf16[1,64,512]{2,1,0:T(8,128)(2,1)S(1)} %shard_map.143), channel_id=1, source_target_pairs={{0,14},{2,4},{4,2},{6,8},{8,6},{10,12},{12,10},{14,0},{1,15},{3,5}... | collective-permute-start | bytes 196616 | tf_op jit(solution)/shard_map/ppermute | solution.py:552

commit v4 on v3

--- a/solution.py
+++ b/solution.py
@@ -11,6 +11,8 @@
 adapter_scale = 2.0
 capacity = 2
 lanes = 128
+first_blocks = (4, 3)
+other_blocks = (5, 6, 2, 1, 7, 0)
 f32 = jnp.float32
 bf16 = jnp.bfloat16
 VMEM = pl.BlockSpec(memory_space=pltpu.VMEM)
@@ -79,11 +81,11 @@
     value_in,
     new_key_in,
     new_value_in,
-    weight_in,
+    projection_in,
     home_ref,
     send_ref,
     back_ref,
-    weight_ref,
+    projection_ref,
     tenant_ref,
     length_ref,
     admitted_ref,
@@ -97,8 +99,8 @@
     new_key_ref,
     new_value_ref,
     attended,
-    own_exp,
-    masses,
+    score_ref,
+    weight_ref,
     sems,
 ):
     rows = steps * heads
@@ -121,7 +123,7 @@
             (new_value_in, new_value_ref),
             (key_in, key_ref),
             (value_in, value_ref),
-            (weight_in, weight_ref),
+            (projection_in, projection_ref),
         ],
         sems,
     )
@@ -130,16 +132,15 @@
     for copy in copies[:9]:
         copy.wait()
 
-    me = lax.axis_index("batch")
     lane = iota((1, lanes), 1)
     place = iota((pairs, 1), 0)
     lane_of_pair = iota((1, pairs), 1)
-    shared_row = iota((8, 2 * lanes), 0)
-    shared_lane = iota((8, 2 * lanes), 1)
+    shared_row = iota((8, lanes), 0)
+    shared_lane = iota((8, lanes), 1)
     flat_rows = jnp.zeros((pairs, 1), jnp.int32)
     flat_lanes = jnp.zeros((1, pairs), jnp.int32)
     scalars = jnp.zeros((pairs, lanes), f32)
-    shared = jnp.zeros((8, 2 * lanes), f32)
+    shared = jnp.zeros((8, lanes), f32)
     first_scalar = 3 * heads * (steps - 1)
     for r in range(requests):
         tenant = tenant_ref[r]
@@ -149,21 +150,21 @@
         position = seen[holder]
         seen[holder] = position + 1
         flat = (holder * capacity + position) * steps
-        flat_rows = jnp.where(place // steps == r, flat, flat_rows)
-        flat_lanes = jnp.where(lane_of_pair // steps == r, flat, flat_lanes)
+        flat_rows = jnp.where(place % requests == r, flat, flat_rows)
+        flat_lanes = jnp.where(lane_of_pair % requests == r, flat, flat_lanes)
         tenant_parts = [tenant // 16, tenant % 16]
         admits = [admitted_ref[s, r] for s in range(steps)]
         own = [slot - holder * adapters_held] + tenant_parts + [tokens // 32, tokens % 32] + admits
         line = jnp.zeros((1, lanes), jnp.int32)
         for index, value in enumerate(own):
             line = jnp.where(lane == first_scalar + index, value, line)
-        scalars = jnp.where(place // steps == r, line.astype(f32), scalars)
-        column = jnp.zeros((8, 2 * lanes), jnp.int32)
+        scalars = jnp.where(place % requests == r, line.astype(f32), scalars)
+        column = jnp.zeros((8, lanes), jnp.int32)
         for index, value in enumerate(tenant_parts + [length_ref[r]] + admits):
             column = jnp.where(shared_row == index, value, column)
-        shared = jnp.where(shared_lane == me * requests + r, column.astype(f32), shared)
-    flat_rows = flat_rows + place % steps
-    flat_lanes = flat_lanes + lane_of_pair % steps
+        shared = jnp.where(shared_lane == lanes // 2 + r, column.astype(f32), shared)
+    flat_rows = flat_rows + place // requests
+    flat_lanes = flat_lanes + lane_of_pair // requests
     back_ref[...] = one_hot(flat_rows, back_ref.shape)
 
     by_head = jnp.concatenate(
@@ -190,35 +191,33 @@
     own_place = new_column == step_of_row * requests + row // rows
     position = iota((rows, context), 1)
     copies[9].wait()
+    for r in range(requests):
+        block = slice(r * rows, (r + 1) * rows)
+        scores = dot_t(by_request[block], key_ref[r]) * scale
+        score_ref[block, :] = jnp.where(position < length_ref[r], scores, -jnp.inf)
+    scores = score_ref[...]
+    top = jnp.maximum(jnp.max(scores, axis=1, keepdims=True), own_score)
+    weight = jnp.exp(scores - top)
+    own_weight = jnp.exp(own_score - top)
+    mass = jnp.sum(weight, axis=1, keepdims=True) + own_weight
+    inverse = 1.0 / mass
+    log_mass = top + jnp.log(mass)
+    weight_ref[...] = (weight * inverse).astype(bf16)
     copies[10].wait()
     for r in range(requests):
-        block = pl.ds(r * rows, rows)
-        scores = dot_t(by_request[r * rows : (r + 1) * rows], key_ref[r]) * scale
-        scores = jnp.where(position < length_ref[r], scores, -jnp.inf)
-        own = own_score[r * rows : (r + 1) * rows]
-        top = jnp.maximum(jnp.max(scores, axis=1, keepdims=True), own)
-        weight = jnp.exp(scores - top)
-        own_weight = jnp.exp(own - top)
-        mass = jnp.sum(weight, axis=1, keepdims=True) + own_weight
-        inverse = 1.0 / mass
-        attended[block, :] = dot((weight * inverse).astype(bf16), value_ref[r])
-        own_exp[block, :] = jnp.broadcast_to(own_weight * inverse, (rows, lanes))
-        masses[block, :] = jnp.broadcast_to(top + jnp.log(mass), (rows, lanes))
-    own_weights = jnp.where(own_place, own_exp[:, 0:pairs], 0.0).astype(bf16)
+        block = slice(r * rows, (r + 1) * rows)
+        attended[block, :] = dot(weight_ref[block, :], value_ref[r])
+    own_weights = jnp.where(own_place, own_weight * inverse, 0.0).astype(bf16)
     result = (attended[...] + dot(own_weights, new_value_ref[...])).astype(bf16)
 
     row = iota((total, total), 0)
-    wanted = (row % pairs) * heads + row // pairs
+    wanted = (row % requests) * rows + ((row // requests) % steps) * heads + row // pairs
     by_head = dot(one_hot(wanted, (total, total)), result).astype(bf16)
     for h in range(heads):
         home_ref[:, h * width : (h + 1) * width] = by_head[h * pairs : (h + 1) * pairs]
-    place = iota((pairs, 1), 0)
-    wanted = (place % steps) * requests + place // steps
-    values = dot(one_hot(wanted, (pairs, pairs)), new_value_ref[...])
-    home_ref[:, features : features + width] = values.astype(bf16)
+    home_ref[:, features : features + width] = new_value_ref[...]
     row = iota((total, 1), 0)
     lane = iota((total, lanes), 1)
-    log_mass = masses[:, 0:1]
     pieces = jnp.zeros((total, lanes), f32)
     for j in range(steps - 1):
         rest = by_step[j] - log_mass
@@ -227,15 +226,19 @@
             rest = rest - part
             target = (piece * (steps - 1) + j) * heads + row % heads
             pieces = jnp.where(lane == target, part, pieces)
-    gather = (iota((pairs, total), 1) // heads == iota((pairs, total), 0)).astype(f32).astype(bf16)
+    column = iota((pairs, total), 1)
+    wanted = ((column // heads) % steps) * requests + column // rows
+    gather = (wanted == iota((pairs, total), 0)).astype(f32).astype(bf16)
     scalars = scalars + dot(gather, pieces.astype(bf16))
     home_ref[:, features + width :] = scalars.astype(bf16)
     slots = send_ref.shape[0]
     pick = (iota((slots, pairs), 0) == flat_lanes).astype(f32).astype(bf16)
-    sent = features + width + lanes
-    send_ref[:, 0:sent] = dot(pick, home_ref[...]).astype(bf16)
+    block = features + width
+    picked = dot(pick, home_ref[...])
     spread = (iota((slots, 8), 0) % 8 == iota((slots, 8), 1)).astype(f32).astype(bf16)
-    send_ref[:, sent:] = dot(spread, shared.astype(bf16)).astype(bf16)
+    send_ref[:, 0:block] = picked[:, 0:block].astype(bf16)
+    integers = dot(spread, shared.astype(bf16))
+    send_ref[:, block:] = (picked[:, block:] + integers).astype(bf16)
     copies[11].wait()
 
 
@@ -250,6 +253,7 @@
     weight_ref,
     low_ref,
     theirs_ref,
+    others_ref,
     final_ref,
     rows_ref,
 ):
@@ -257,9 +261,16 @@
     features = heads * width
     sent = features + width + lanes
     count = slots + pairs
-    shared = got_ref[0:8, sent:].astype(f32)
-    for start in range(8, slots, 8):
-        shared = shared + got_ref[start : start + 8, sent:].astype(f32)
+    block = features + width
+    requests = pairs // steps
+    everyone = requests * (slots // 8)
+    column = iota((lanes, everyone), 1)
+    tile = (iota((lanes, everyone), 0) == lanes // 2 + column % requests).astype(f32).astype(bf16)
+    column = iota((slots, everyone), 1)
+    from_row = column // requests == iota((slots, everyone), 0) // 8
+    tiled = jnp.where(from_row, dot(got_ref[:, block:], tile), 0.0).astype(bf16)
+    kind = (iota((8, slots), 1) % 8 == iota((8, slots), 0)).astype(f32).astype(bf16)
+    shared = dot(kind, tiled)
     tenants = shared[0:1] * 16.0 + shared[1:2]
     charge_rows = []
     for s in range(steps - 1):
@@ -270,7 +281,6 @@
     charge_rows += [jnp.zeros_like(tenants)] * (8 - len(charge_rows))
     charges = jnp.concatenate(charge_rows, axis=0).astype(bf16)
 
-    block = features + width
     scalars = jnp.concatenate(
         [got_ref[:, block:sent].astype(f32), home_ref[:, block:sent].astype(f32)], axis=0
     )
@@ -279,7 +289,8 @@
     tokens = scalars[:, first + 3 : first + 4] * 32.0 + scalars[:, first + 4 : first + 5]
     same = (tenant == tenants).astype(f32).astype(bf16)
     grows = dot_t(same, charges)
-    step_of_row = iota((count, 1), 0) % steps
+    row = iota((count, 1), 0)
+    step_of_row = jnp.where(row < slots, row % steps, (row - slots) // requests)
     served_now = jnp.zeros((count, 1), f32)
     served = []
     for s in range(steps):
@@ -312,9 +323,10 @@
     values = jnp.concatenate(
         [got_ref[:, features:block], home_ref[:, features:block]], axis=0
     )
-    row = iota((count, 1), 0)
+    first_row = jnp.where(row < slots, row - row % steps, slots + (row - slots) % requests)
+    stride = jnp.where(row < slots, 1, requests)
     new_values = [
-        dot(one_hot(row - row % steps + j, (count, count)), values) for j in range(steps - 1)
+        dot(one_hot(first_row + stride * j, (count, count)), values) for j in range(steps - 1)
     ]
     for h in range(heads):
         part = slice(h * width, (h + 1) * width)
@@ -337,40 +349,61 @@
     folded = folded + pltpu.roll(folded, rank, 1)
     half = slots // 2
     low_half = iota((half, lanes), 1) < rank
-    low_ref[...] = jnp.where(low_half, folded[0:half], folded[half:])
-    project(1, final_ref, weight_ref, theirs_ref)
-
-
-def project(flip, rows_ref, weight_ref, out_ref):
-    parts, _, width = out_ref.shape
+    low = jnp.where(low_half, folded[0:half], folded[half:])
+    low_ref[...] = low
+    for index, product in enumerate(project(1, first_blocks, final_ref, weight_ref)):
+        theirs_ref[:, index * features : (index + 1) * features] = product.astype(bf16)
+    start = len(first_blocks) * features
+    upper = low.astype(bf16)
+    theirs_ref[:, start : start + lanes] = upper
+    theirs_ref[:, start + lanes :] = (low - upper.astype(f32)).astype(bf16)
+    for index, product in enumerate(project(1, other_blocks, final_ref, weight_ref)):
+        others_ref[index] = product.astype(bf16)
+
+
+def project(flip, wanted, rows_ref, weight_ref):
+    parts = lax.axis_size("z")
+    width = weight_ref.shape[1] // (2 * parts)
     core = lax.axis_index("core")
     mine = core if flip == 0 else 1 - core
     here = lax.axis_index("z")
     way = 1 - 2 * lax.rem(here, 2)
-    for part in range(parts):
+    products = []
+    for part in wanted:
         target = lax.rem(here + way * part + parts, parts)
         start = pl.multiple_of((2 * target + mine) * width, width)
-        product = dot(rows_ref[...], weight_ref[:, pl.ds(start, width)])
-        out_ref[part] = product.astype(out_ref.dtype)
-
-
-def mix_kernel(ours_ref, theirs_ref, low_ref, low_other_ref, low_out, base_out, first_out):
-    low = (low_ref[...] + low_other_ref[...]).astype(bf16)
-    for part in range(base_out.shape[0]):
+        products.append(dot(rows_ref[...], weight_ref[:, pl.ds(start, width)]))
+    return products
+
+
+def ours_kernel(rows_ref, weight_ref, out_ref):
+    blocks = first_blocks + other_blocks
+    for index, product in enumerate(project(0, blocks, rows_ref, weight_ref)):
+        out_ref[index] = product
+
+
+def mix_kernel(low_ref, ours_ref, came_ref, low_out, first_out):
+    count, _, width = first_out.shape
+    start = count * width
+    other = came_ref[:, start : start + lanes].astype(f32)
+    other = other + came_ref[:, start + lanes :].astype(f32)
+    low = (low_ref[...] + other).astype(bf16)
+    for part in range(low_out.shape[0]):
         low_out[part] = low
-        base_out[part] = (ours_ref[part] + theirs_ref[part].astype(f32)).astype(bf16)
-    for index, part in enumerate((4, 3)):
-        first_out[index] = base_out[part]
-
-
-def hop_kernel(wanted, base_ref, came_ref, out_ref):
-    for index, part in enumerate(wanted):
-        total = came_ref[index].astype(f32) + base_ref[part].astype(f32)
-        out_ref[index] = total.astype(bf16)
-
-
-def late_hop_kernel(wanted, base_ref, came_ref, after_ref, out_ref):
-    hop_kernel(wanted, base_ref, came_ref, out_ref)
+    for index in range(count):
+        came = came_ref[:, index * width : (index + 1) * width].astype(f32)
+        first_out[index] = (ours_ref[index] + came).astype(bf16)
+
+
+def hop_kernel(first, ours_ref, others_ref, came_ref, out_ref):
+    skip = len(first_blocks) + first
+    for index in range(out_ref.shape[0]):
+        here = ours_ref[skip + index] + others_ref[first + index].astype(f32)
+        out_ref[index] = (came_ref[index].astype(f32) + here).astype(bf16)
+
+
+def late_hop_kernel(first, ours_ref, others_ref, came_ref, after_ref, out_ref):
+    hop_kernel(first, ours_ref, others_ref, came_ref, out_ref)
 
 
 def up_kernel(first_scalar, parts_ref, held_ref, up_ref, out_ref):
@@ -391,15 +424,11 @@
     out_ref[...] = dot(wide, up_ref[...].reshape(every, up_ref.shape[2])).astype(bf16)
 
 
-def finish_kernel(steps, base_ref, first_ref, second_ref, back_ref, term_ref, out_ref):
-    pairs = out_ref.shape[0]
-    total = base_ref[0].astype(f32) + first_ref[1].astype(f32) + second_ref[0].astype(f32)
+def finish_kernel(ours_ref, others_ref, first_ref, second_ref, back_ref, term_ref, out_ref):
+    total = ours_ref[0] + others_ref[0].astype(f32)
+    total = total + first_ref[0].astype(f32) + second_ref[0].astype(f32)
     term = dot(back_ref[...], term_ref[...])
-    rows = (total + adapter_scale * term).astype(bf16)
-    place = iota((pairs, 1), 0)
-    requests = pairs // steps
-    wanted = (place % requests) * steps + place // requests
-    out_ref[...] = dot(one_hot(wanted, (pairs, pairs)), rows).astype(bf16)
+    out_ref[...] = (total + adapter_scale * term).astype(bf16)
 
 
 def per_device(
@@ -438,7 +467,7 @@
         functools.partial(attend_kernel, steps, requests, heads, adapters_held),
         (
             shape((pairs, sent), bf16),
-            shape((slots, sent + 2 * lanes), bf16),
+            shape((slots, sent), bf16),
             shape((pairs, slots), bf16),
             pltpu.VMEM(out_weight.shape, bf16),
         ),
@@ -460,8 +489,8 @@
             pltpu.VMEM((pairs, width), bf16),
             pltpu.VMEM((pairs, width), bf16),
             pltpu.VMEM((total, width), f32),
-            pltpu.VMEM((total, lanes), f32),
-            pltpu.VMEM((total, lanes), f32),
+            pltpu.VMEM((total, context), f32),
+            pltpu.VMEM((total, context), bf16),
             pltpu.SemaphoreType.DMA((12,)),
         ],
         40 << 20,
@@ -485,51 +514,51 @@
         )
     )
     got = lax.all_to_all(send, "batch", split_axis=0, concat_axis=0, tiled=True)
-    low, theirs, final = call(
+    weight = in_vmem(weight)
+    two = shape((2, pairs, features), bf16)
+    one = shape((1, pairs, features), bf16)
+    six = shape((len(other_blocks), pairs, features), bf16)
+    blocks = shape((parts, pairs, features), f32)
+    low, theirs, others, final = call(
         functools.partial(combine_kernel, steps, heads, width, threshold),
         (
             shape((slots // 2, lanes), f32),
-            shape((parts, pairs, features), bf16),
+            shape((pairs, 2 * features + 2 * lanes), bf16),
+            six,
             shape((pairs, features), bf16),
         ),
         [VMEM] * 4,
-        (VMEM,) * 3,
+        (VMEM,) * 4,
         2 * slots * features * every,
         out_weight.size,
         [pltpu.VMEM((slots, features), bf16)],
-    )(got, home, adapter_down_factor, in_vmem(weight))
+    )(got, home, adapter_down_factor, weight)
     swap = [(0, 1), (1, 0)]
-    low_other = lax.ppermute(low, "core", swap)
     theirs = lax.ppermute(theirs, "core", swap)
+    others = lax.ppermute(others, "core", swap)
     ours = call(
-        functools.partial(project, 0),
-        shape((parts, pairs, features), f32),
+        ours_kernel,
+        blocks,
         [VMEM] * 2,
         VMEM,
         pairs * out_weight.size,
         out_weight.size,
-    )(final, in_vmem(weight))
-    two = shape((2, pairs, features), bf16)
-    one = shape((1, pairs, features), bf16)
-    low, base, sums = call(
+    )(final, weight)
+    low, sums = call(
         mix_kernel,
-        (
-            shape((parts, slots // 2, lanes), bf16),
-            shape((parts, pairs, features), bf16),
-            two,
-        ),
-        [VMEM] * 4,
-        (VMEM,) * 3,
-        2 * ours.size,
-        8 * ours.size,
-    )(ours, theirs, low, low_other)
+        (shape((parts, slots // 2, lanes), bf16), two),
+        [VMEM] * 3,
+        (VMEM,) * 2,
+        2 * two.size,
+        8 * two.size,
+    )(low, ours, theirs)
     low = lax.all_to_all(low, "z", split_axis=0, concat_axis=0, tiled=True)
 
-    def hop(kernel, wanted, out, *args):
+    def hop(kernel, first, out, *args):
         return call(
-            functools.partial(kernel, wanted),
+            functools.partial(kernel, first),
             out,
-            [VMEM, VMEM] + [HBM] * (len(args) - 2),
+            [VMEM] * 3 + [HBM] * (len(args) - 3),
             VMEM,
             out.size,
             6 * out.size,
@@ -538,7 +567,7 @@
     odd = [(i, i + 1 - 2 * (i % 2)) for i in range(parts)]
     even = [(i, (i - 1 + 2 * (i % 2)) % parts) for i in range(parts)]
     sums = lax.ppermute(sums, "z", odd)
-    sums = lax.ppermute(hop(hop_kernel, (5, 6), two, base, sums), "z", even)
+    sums = lax.ppermute(hop(hop_kernel, 0, two, ours, others, sums), "z", even)
     term = call(
         functools.partial(up_kernel, first_scalar),
         shape((slots, features), bf16),
@@ -547,18 +576,18 @@
         2 * slots * features * every,
         4 * slots * features,
     )(low, got[:, features + width : sent], adapter_up_factor)
-    sums = hop(late_hop_kernel, (2, 1), two, base, sums, term)
+    sums = hop(late_hop_kernel, 2, two, ours, others, sums, term)
     sums = lax.ppermute(sums, "z", odd)
-    last = lax.ppermute(hop(hop_kernel, (7,), one, base, sums), "z", even)
+    last = lax.ppermute(hop(hop_kernel, 4, one, ours, others, sums), "z", even)
     term = lax.all_to_all(term, "batch", split_axis=0, concat_axis=0, tiled=True)
     out = call(
-        functools.partial(finish_kernel, steps),
+        finish_kernel,
         shape((pairs, features), bf16),
-        [VMEM] * 5,
+        [VMEM] * 6,
         VMEM,
         2 * pairs * slots * features,
         10 * one.size,
-    )(base, sums, last, back, term)
+    )(ours[-1:], others[-1:], sums[1:], last, back, term)
     return out.reshape(steps, requests, features)
 
 

time: 60 us -> 57.1 us (0.952)
  Pallas kernels: 12.7 us -> 10.1 us
    pallas_call x1, Pallas kernels: 6.93 us -> 4.25 us  [per_device(): call(functools.partial(attend_kernel, steps, requests, heads, adapters_he...]
    ppermute x3, waiting for transfers between devices: 0.61 us -> 0.01 us  [the longest x1 0.01 us: per_device(): others = lax.ppermute(others, 'core', swap)]
    ppermute x1, waiting for transfers between devices: 0.01 us -> 0.61 us  [per_device(): theirs = lax.ppermute(theirs, 'core', swap)]
  transfers between devices with their start and end apart: 8 -> 8, of which waited for: 3 -> 3; matrix products, arithmetic and copies ran while one was open for 0% -> 0% of each run, Pallas kernels for 3% -> 4%
where the time goes in v4:
time: 57.1 us; the launch traced here: 56.8 us
  starting transfers between devices  20.4 us (36%)
  blocking collectives  14.2 us (25%)
  waiting for transfers between devices  11.9 us (21%)
  Pallas kernels  10.1 us (18%)
    all_to_all x1, blocking collectives, per_device(): got = lax.all_to_all(send, 'batch', split_axis=0, concat_axis=0, tiled=True)  14.2 us
    all_to_all x1, starting transfers between devices, per_device(): low = lax.all_to_all(low, 'z', split_axis=0, concat_axis=0, tiled=True)  7.56 us
    all_to_all x1, waiting for transfers between devices, per_device(): low = lax.all_to_all(low, 'z', split_axis=0, concat_axis=0, tiled=True)  5.74 us
    all_to_all x1, waiting for transfers between devices, per_device(): lax.all_to_all(term, 'batch', split_axis=0, concat_axis=0, tiled=True)  5.49 us
    all_to_all x1, starting transfers between devices, per_device(): lax.all_to_all(term, 'batch', split_axis=0, concat_axis=0, tiled=True)  4.76 us
    pallas_call x1, Pallas kernels, per_device(): call(functools.partial(attend_kernel, steps, requests, heads, adapters_he...  4.25 us
    ppermute x1, starting transfers between devices, per_device(): sums = lax.ppermute(hop(hop_kernel, 0, two, ours, others, sums), 'z', even)  3.31 us
    ppermute x2, starting transfers between devices, per_device(): sums = lax.ppermute(sums, 'z', odd)  3.01 us
  transfers between devices with their start and end apart: 8, of which 3 were waited for; matrix products, arithmetic and copies ran while one was open for 0% of the time, Pallas kernels for 4%

profile of v4, /device:TPU:2, one launch (start us, length us, event | category | flops | bytes accessed | tf_op | source)
XLA Modules:
  0.0 56.8 jit_solution(3065583008562426815)
XLA Ops:
  0.0 0.0 copy-start
  0.0 4.3 %shard_map.136 = (bf16[64,768]{1,0:T(8,128)(2,1)S(1)}, bf16[128,768]{1,0:T(8,128)(2,1)S(1)}, bf16[64,128]{1,0:T(8,128)(2,1)S(1)}, bf16[512,8192]{1,0:T(8,128)(2,1)S(1)}) custom-call(s32[16]{0:T(128)} %tenant_in.1, s32[16]{0:T(128)} %length_in.1, s32[4,16]{1,0:T(4,128)} %admitted_in.1, s32[512]{0:T(512)} %tenant_adapter_in.1, s32[128]{0:T(128)} %adapter_slot_in.1, ...), custom_call_target="tpu_custom_call" | custom-call | flops 33554432 | bytes 2097152 | tf_op jit(solution)/shard_map/pallas_call | solution.py:466
  4.3 14.2 %all_to_all.27 = bf16[16,8,768]{2,1,0:T(8,128)(2,1)S(1)} all-to-all(bf16[16,8,768]{2,1,0:T(8,128)(2,1)S(1)} %bitcast.13), channel_id=1, replica_groups=mesh['batch'=16,'z'=8,'core'=2] {'batch'}, dimensions={0} | all-to-all | bytes 393216 | tf_op jit(solution)/shard_map/all_to_all | solution.py:516
  18.5 0.0 copy-done
  18.5 2.5 %shard_map.137 = (f32[64,128]{1,0:T(8,128)S(1)}, bf16[64,1280]{1,0:T(8,128)(2,1)S(1)}, bf16[6,64,512]{2,1,0:T(8,128)(2,1)S(1)}, bf16[64,512]{1,0:T(8,128)(2,1)S(1)}) custom-call(bf16[128,768]{1,0:T(8,128)(2,1)S(1)} %bitcast.10, bf16[64,768]{1,0:T(8,128)(2,1)S(1)} %get-tuple-element.16.home_ref, bf16[8,64,512]{2,1,0:T(8,128)(2,1)S(1)} %copy-done, ...), custom_call_target="tpu_custom_call" | custom-call | flops 67108864 | bytes 4194304 | tf_op jit(solution)/shard_map/pallas_call | solution.py:522
  21.1 0.0 copy-start.1
  21.1 0.1 collective-permute-start
  21.2 0.5 collective-permute-start.1
  21.7 0.8 %shard_map.138.ours_ref = f32[8,64,512]{2,1,0:T(8,128)S(1)} custom-call(bf16[64,512]{1,0:T(8,128)(2,1)S(1)} %get-tuple-element.18.rows_ref, bf16[512,8192]{1,0:T(8,128)(2,1)S(1)} %get-tuple-element.17.weight_ref), custom_call_target="tpu_custom_call" | custom-call | flops 268435456 | bytes 4194304 | tf_op jit(solution)/shard_map/pallas_call | solution.py:539
  22.5 0.6 %collective-permute-done.1.came_ref = bf16[64,1280]{1,0:T(8,128)(2,1)S(1)} collective-permute-done((bf16[64,1280]{1,0:T(8,128)(2,1)S(1)}, bf16[64,1280]{1,0:T(8,128)(2,1)S(1)}, u32[]{:S(2)}, u32[]{:S(2)}) %collective-permute-start.1) | collective-permute-done | bytes 163872 | tf_op jit(solution)/shard_map/ppermute | solution.py:537
  23.1 0.7 %shard_map.139 = (bf16[8,64,128]{2,1,0:T(8,128)(2,1)}, bf16[2,64,512]{2,1,0:T(8,128)(2,1)S(1)}) custom-call(f32[64,128]{1,0:T(8,128)S(1)} %get-tuple-element.20.low_ref, f32[8,64,512]{2,1,0:T(8,128)S(1)} %shard_map.138.ours_ref, bf16[64,1280]{1,0:T(8,128)(2,1)S(1)} %collective-permute-done.1.came_ref), custom_call_target="tpu_custom_call" | custom-call | flops 131072 | bytes 524288 | tf_op jit(solution)/shard_map/pallas_call | solution.py:547
  23.8 1.9 %collective-permute-start.2 = (bf16[2,64,512]{2,1,0:T(8,128)(2,1)S(1)}, bf16[2,64,512]{2,1,0:T(8,128)(2,1)S(1)}, u32[]{:S(2)}, u32[]{:S(2)}) collective-permute-start(bf16[2,64,512]{2,1,0:T(8,128)(2,1)S(1)} %get-tuple-element.22), channel_id=1, source_target_pairs={{0,2},{2,0},{4,6},{6,4},{8,10},{10,8},{12,14},{14,12},{1,3},{3,1},... | collective-permute-start | bytes 393224 | tf_op jit(solution)/shard_map/ppermute | solution.py:569
  25.7 7.6 %all-to-all-start.1 = ((bf16[8,64,128]{2,1,0:T(8,128)(2,1)}), bf16[8,64,128]{2,1,0:T(8,128)(2,1)S(1)}, u32[]{:S(2)}, u32[]{:S(2)}) async-start(bf16[8,64,128]{2,1,0:T(8,128)(2,1)} %get-tuple-element.23), calls=%async_computation.1 | async-start | bytes 262144 | tf_op jit(solution)/shard_map/all_to_all | solution.py:555
  33.3 0.0 collective-permute-done.2.came_ref
  33.3 0.0 collective-permute-done.others_ref
  33.4 3.3 %collective-permute-start.3 = (bf16[2,64,512]{2,1,0:T(8,128)(2,1)S(1)}, bf16[2,64,512]{2,1,0:T(8,128)(2,1)S(1)}, u32[]{:S(2)}, u32[]{:S(2)}) collective-permute-start(bf16[2,64,512]{2,1,0:T(8,128)(2,1)S(1)} %shard_map.140), channel_id=1, source_target_pairs={{0,14},{2,4},{4,2},{6,8},{8,6},{10,12},{12,10},{14,0},{1,15},{3,5}... | collective-permute-start | bytes 393224 | tf_op jit(solution)/shard_map/ppermute | solution.py:570
  36.7 5.7 %all-to-all-done.1.parts_ref = bf16[8,64,128]{2,1,0:T(8,128)(2,1)S(1)} async-done(((bf16[8,64,128]{2,1,0:T(8,128)(2,1)}), bf16[8,64,128]{2,1,0:T(8,128)(2,1)S(1)}, u32[]{:S(2)}, u32[]{:S(2)}) %all-to-all-start.1) | async-done | bytes 131104 | tf_op jit(solution)/shard_map/all_to_all | solution.py:555
  42.4 0.0 copy-done.1
  42.4 0.9 %shard_map.141.after_ref = bf16[128,512]{1,0:T(8,128)(2,1)} custom-call(bf16[8,64,128]{2,1,0:T(8,128)(2,1)S(1)} %all-to-all-done.1.parts_ref, bf16[128,128]{1,0:T(8,128)(2,1)S(1)} %slice.18.held_ref, bf16[8,64,512]{2,1,0:T(8,128)(2,1)S(1)} %copy-done.1), custom_call_target="tpu_custom_call" | custom-call | flops 67108864 | bytes 262144 | tf_op jit(solution)/shard_map/pallas_call | solution.py:571
  43.4 0.0 collective-permute-done.3.came_ref
  43.4 1.1 %collective-permute-start.4 = (bf16[2,64,512]{2,1,0:T(8,128)(2,1)S(1)}, bf16[2,64,512]{2,1,0:T(8,128)(2,1)S(1)}, u32[]{:S(2)}, u32[]{:S(2)}) collective-permute-start(bf16[2,64,512]{2,1,0:T(8,128)(2,1)S(1)} %shard_map.142), channel_id=1, source_target_pairs={{0,2},{2,0},{4,6},{6,4},{8,10},{10,8},{12,14},{14,12},{1,3},{3,1},... | collective-permute-start | bytes 393224 | tf_op jit(solution)/shard_map/ppermute | solution.py:580
  44.5 4.8 %all-to-all-start.2 = ((bf16[16,8,512]{2,1,0:T(8,128)(2,1)}), bf16[16,8,512]{2,1,0:T(8,128)(2,1)S(1)}, u32[]{:S(2)}, u32[]{:S(2)}) async-start(bf16[16,8,512]{2,1,0:T(8,128)(2,1)} %bitcast.7), calls=%async_computation.2 | async-start | bytes 262144 | tf_op jit(solution)/shard_map/all_to_all | solution.py:582
  49.2 0.0 collective-permute-done.4.came_ref
  49.3 1.1 %collective-permute-start.5 = (bf16[1,64,512]{2,1,0:T(8,128)(2,1)S(1)}, bf16[1,64,512]{2,1,0:T(8,128)(2,1)S(1)}, u32[]{:S(2)}, u32[]{:S(2)}) collective-permute-start(bf16[1,64,512]{2,1,0:T(8,128)(2,1)S(1)} %shard_map.143), channel_id=1, source_target_pairs={{0,14},{2,4},{4,2},{6,8},{8,6},{10,12},{12,10},{14,0},{1,15},{3,5}... | collective-permute-start | bytes 196616 | tf_op jit(solution)/shard_map/ppermute | solution.py:581
  50.5 5.5 %all-to-all-done.2 = bf16[16,8,512]{2,1,0:T(8,128)(2,1)S(1)} async-done(((bf16[16,8,512]{2,1,0:T(8,128)(2,1)}), bf16[16,8,512]{2,1,0:T(8,128)(2,1)S(1)}, u32[]{:S(2)}, u32[]{:S(2)}) %all-to-all-start.2) | async-done | bytes 131104 | tf_op jit(solution)/shard_map/all_to_all | solution.py:582
  56.0 0.0 collective-permute-done.5.second_ref
  56.0 0.8 %shard_map.144 = bf16[64,512]{1,0:T(8,128)(2,1)} custom-call(f32[1,64,512]{2,1,0:T(8,128)S(1)} %slice.16.ours_ref, bf16[1,64,512]{2,1,0:T(8,128)(2,1)S(1)} %slice.17.others_ref, bf16[1,64,512]{2,1,0:T(8,128)(2,1)S(1)} %slice.19.first_ref, bf16[1,64,512]{2,1,0:T(8,128)(2,1)S(1)} %collective-permute-done.5.second_ref, ...), custom_call_target="tpu_custom_call" | custom-call | flops 8388608 | bytes 327680 | tf_op jit(solution)/shard_map/pallas_call | solution.py:583
  (7 shorter events, 0.1 us)
Async XLA Ops:
  0.0 18.5 %copy-start = (bf16[8,64,512]{2,1,0:T(8,128)(2,1)S(1)}, bf16[8,64,512]{2,1,0:T(8,128)(2,1)}, u32[]{:S(2)}) copy-start(bf16[8,64,512]{2,1,0:T(8,128)(2,1)} %down_ref.1) | copy-start | bytes 1572868
  21.1 21.3 %copy-start.1 = (bf16[8,64,512]{2,1,0:T(8,128)(2,1)S(1)}, bf16[8,64,512]{2,1,0:T(8,128)(2,1)}, u32[]{:S(2)}) copy-start(bf16[8,64,512]{2,1,0:T(8,128)(2,1)} %up_ref.1) | copy-start | bytes 1572868
  21.1 12.2 %collective-permute-start = (bf16[6,64,512]{2,1,0:T(8,128)(2,1)S(1)}, bf16[6,64,512]{2,1,0:T(8,128)(2,1)S(1)}, u32[]{:S(2)}, u32[]{:S(2)}) collective-permute-start(bf16[6,64,512]{2,1,0:T(8,128)(2,1)S(1)} %get-tuple-element.19), channel_id=1, source_target_pairs={{0,1},{1,0},{2,3},{3,2},{4,5},{5,4},{6,7},{7,6},{8,9},{9,8},{10,11... | collective-permute-start | bytes 1179656 | tf_op jit(solution)/shard_map/ppermute | solution.py:538
  21.2 1.9 %collective-permute-start.1 = (bf16[64,1280]{1,0:T(8,128)(2,1)S(1)}, bf16[64,1280]{1,0:T(8,128)(2,1)S(1)}, u32[]{:S(2)}, u32[]{:S(2)}) collective-permute-start(bf16[64,1280]{1,0:T(8,128)(2,1)S(1)} %get-tuple-element.21), channel_id=1, source_target_pairs={{0,1},{1,0},{2,3},{3,2},{4,5},{5,4},{6,7},{7,6},{8,9},{9,8},{10,11... | collective-permute-start | bytes 491528 | tf_op jit(solution)/shard_map/ppermute | solution.py:537
  23.8 9.5 %collective-permute-start.2 = (bf16[2,64,512]{2,1,0:T(8,128)(2,1)S(1)}, bf16[2,64,512]{2,1,0:T(8,128)(2,1)S(1)}, u32[]{:S(2)}, u32[]{:S(2)}) collective-permute-start(bf16[2,64,512]{2,1,0:T(8,128)(2,1)S(1)} %get-tuple-element.22), channel_id=1, source_target_pairs={{0,2},{2,0},{4,6},{6,4},{8,10},{10,8},{12,14},{14,12},{1,3},{3,1},... | collective-permute-start | bytes 393224 | tf_op jit(solution)/shard_map/ppermute | solution.py:569
  25.7 16.7 %all-to-all-start.1 = ((bf16[8,64,128]{2,1,0:T(8,128)(2,1)}), bf16[8,64,128]{2,1,0:T(8,128)(2,1)S(1)}, u32[]{:S(2)}, u32[]{:S(2)}) async-start(bf16[8,64,128]{2,1,0:T(8,128)(2,1)} %get-tuple-element.23), calls=%async_computation.1 | async-start | bytes 262144 | tf_op jit(solution)/shard_map/all_to_all | solution.py:555
  33.4 10.0 %collective-permute-start.3 = (bf16[2,64,512]{2,1,0:T(8,128)(2,1)S(1)}, bf16[2,64,512]{2,1,0:T(8,128)(2,1)S(1)}, u32[]{:S(2)}, u32[]{:S(2)}) collective-permute-start(bf16[2,64,512]{2,1,0:T(8,128)(2,1)S(1)} %shard_map.140), channel_id=1, source_target_pairs={{0,14},{2,4},{4,2},{6,8},{8,6},{10,12},{12,10},{14,0},{1,15},{3,5}... | collective-permute-start | bytes 393224 | tf_op jit(solution)/shard_map/ppermute | solution.py:570
  43.4 5.8 %collective-permute-start.4 = (bf16[2,64,512]{2,1,0:T(8,128)(2,1)S(1)}, bf16[2,64,512]{2,1,0:T(8,128)(2,1)S(1)}, u32[]{:S(2)}, u32[]{:S(2)}) collective-permute-start(bf16[2,64,512]{2,1,0:T(8,128)(2,1)S(1)} %shard_map.142), channel_id=1, source_target_pairs={{0,2},{2,0},{4,6},{6,4},{8,10},{10,8},{12,14},{14,12},{1,3},{3,1},... | collective-permute-start | bytes 393224 | tf_op jit(solution)/shard_map/ppermute | solution.py:580
  44.5 11.5 %all-to-all-start.2 = ((bf16[16,8,512]{2,1,0:T(8,128)(2,1)}), bf16[16,8,512]{2,1,0:T(8,128)(2,1)S(1)}, u32[]{:S(2)}, u32[]{:S(2)}) async-start(bf16[16,8,512]{2,1,0:T(8,128)(2,1)} %bitcast.7), calls=%async_computation.2 | async-start | bytes 262144 | tf_op jit(solution)/shard_map/all_to_all | solution.py:582
  49.3 6.7 %collective-permute-start.5 = (bf16[1,64,512]{2,1,0:T(8,128)(2,1)S(1)}, bf16[1,64,512]{2,1,0:T(8,128)(2,1)S(1)}, u32[]{:S(2)}, u32[]{:S(2)}) collective-permute-start(bf16[1,64,512]{2,1,0:T(8,128)(2,1)S(1)} %shard_map.143), channel_id=1, source_target_pairs={{0,14},{2,4},{4,2},{6,8},{8,6},{10,12},{12,10},{14,0},{1,15},{3,5}... | collective-permute-start | bytes 196616 | tf_op jit(solution)/shard_map/ppermute | solution.py:581

commit v5 on v4

--- a/solution.py
+++ b/solution.py
@@ -123,7 +123,7 @@
             (new_value_in, new_value_ref),
             (key_in, key_ref),
             (value_in, value_ref),
-            (projection_in, projection_ref),
+            (projection_in.at[pl.ds(0, projection_ref.shape[0])], projection_ref),
         ],
         sems,
     )
@@ -251,12 +251,18 @@
     home_ref,
     down_ref,
     weight_ref,
+    weight_in,
     low_ref,
     theirs_ref,
     others_ref,
     final_ref,
+    late_ref,
     rows_ref,
+    sem,
 ):
+    early = weight_ref.shape[0]
+    copy = pltpu.make_async_copy(weight_in.at[pl.ds(early, late_ref.shape[0])], late_ref, sem)
+    copy.start()
     slots, pairs = got_ref.shape[0], home_ref.shape[0]
     features = heads * width
     sent = features + width + lanes
@@ -351,19 +357,21 @@
     low_half = iota((half, lanes), 1) < rank
     low = jnp.where(low_half, folded[0:half], folded[half:])
     low_ref[...] = low
-    for index, product in enumerate(project(1, first_blocks, final_ref, weight_ref)):
+    copy.wait()
+    for index, product in enumerate(project(1, first_blocks, final_ref, weight_ref, late_ref)):
         theirs_ref[:, index * features : (index + 1) * features] = product.astype(bf16)
     start = len(first_blocks) * features
     upper = low.astype(bf16)
     theirs_ref[:, start : start + lanes] = upper
     theirs_ref[:, start + lanes :] = (low - upper.astype(f32)).astype(bf16)
-    for index, product in enumerate(project(1, other_blocks, final_ref, weight_ref)):
+    for index, product in enumerate(project(1, other_blocks, final_ref, weight_ref, late_ref)):
         others_ref[index] = product.astype(bf16)
 
 
-def project(flip, wanted, rows_ref, weight_ref):
+def project(flip, wanted, rows_ref, weight_ref, late_ref):
     parts = lax.axis_size("z")
     width = weight_ref.shape[1] // (2 * parts)
+    early = weight_ref.shape[0]
     core = lax.axis_index("core")
     mine = core if flip == 0 else 1 - core
     here = lax.axis_index("z")
@@ -372,17 +380,19 @@
     for part in wanted:
         target = lax.rem(here + way * part + parts, parts)
         start = pl.multiple_of((2 * target + mine) * width, width)
-        products.append(dot(rows_ref[...], weight_ref[:, pl.ds(start, width)]))
+        block = pl.ds(start, width)
+        product = dot(rows_ref[:, 0:early], weight_ref[:, block])
+        products.append(product + dot(rows_ref[:, early:], late_ref[:, block]))
     return products
 
 
-def ours_kernel(rows_ref, weight_ref, out_ref):
+def ours_kernel(rows_ref, weight_ref, late_ref, out_ref):
     blocks = first_blocks + other_blocks
-    for index, product in enumerate(project(0, blocks, rows_ref, weight_ref)):
+    for index, product in enumerate(project(0, blocks, rows_ref, weight_ref, late_ref)):
         out_ref[index] = product
 
 
-def mix_kernel(low_ref, ours_ref, came_ref, low_out, first_out):
+def mix_kernel(low_ref, ours_ref, came_ref, others_ref, low_out, first_out, others_out):
     count, _, width = first_out.shape
     start = count * width
     other = came_ref[:, start : start + lanes].astype(f32)
@@ -393,6 +403,7 @@
     for index in range(count):
         came = came_ref[:, index * width : (index + 1) * width].astype(f32)
         first_out[index] = (ours_ref[index] + came).astype(bf16)
+    others_out[...] = others_ref[...]
 
 
 def hop_kernel(first, ours_ref, others_ref, came_ref, out_ref):
@@ -458,6 +469,7 @@
     adapters_held, rank, _ = adapter_down_factor.shape
     every = adapters_held * rank
     threshold = float(3 * context)
+    early = features * 4 // 8
     slots = holders * capacity * steps
     first_scalar = 3 * heads * (steps - 1)
     sent = features + width + lanes
@@ -469,7 +481,7 @@
             shape((pairs, sent), bf16),
             shape((slots, sent), bf16),
             shape((pairs, slots), bf16),
-            pltpu.VMEM(out_weight.shape, bf16),
+            pltpu.VMEM((early, out_weight.shape[1]), bf16),
         ),
         [HBM] * 12,
         (VMEM,) * 4,
@@ -519,39 +531,40 @@
     one = shape((1, pairs, features), bf16)
     six = shape((len(other_blocks), pairs, features), bf16)
     blocks = shape((parts, pairs, features), f32)
-    low, theirs, others, final = call(
+    low, theirs, others, final, late = call(
         functools.partial(combine_kernel, steps, heads, width, threshold),
         (
             shape((slots // 2, lanes), f32),
             shape((pairs, 2 * features + 2 * lanes), bf16),
             six,
             shape((pairs, features), bf16),
+            pltpu.VMEM((features - early, out_weight.shape[1]), bf16),
         ),
-        [VMEM] * 4,
-        (VMEM,) * 4,
+        [VMEM] * 4 + [HBM],
+        (VMEM,) * 5,
         2 * slots * features * every,
         out_weight.size,
-        [pltpu.VMEM((slots, features), bf16)],
-    )(got, home, adapter_down_factor, weight)
+        [pltpu.VMEM((slots, features), bf16), pltpu.SemaphoreType.DMA],
+    )(got, home, adapter_down_factor, weight, in_hbm(out_weight))
     swap = [(0, 1), (1, 0)]
     theirs = lax.ppermute(theirs, "core", swap)
-    others = lax.ppermute(others, "core", swap)
     ours = call(
         ours_kernel,
         blocks,
-        [VMEM] * 2,
+        [VMEM] * 3,
         VMEM,
         pairs * out_weight.size,
         out_weight.size,
-    )(final, weight)
-    low, sums = call(
+    )(final, weight, in_vmem(late))
+    low, sums, others = call(
         mix_kernel,
-        (shape((parts, slots // 2, lanes), bf16), two),
-        [VMEM] * 3,
-        (VMEM,) * 2,
+        (shape((parts, slots // 2, lanes), bf16), two, six),
+        [VMEM] * 4,
+        (VMEM,) * 3,
         2 * two.size,
         8 * two.size,
-    )(low, ours, theirs)
+    )(low, ours, theirs, others)
+    others = lax.ppermute(others, "core", swap)
     low = lax.all_to_all(low, "z", split_axis=0, concat_axis=0, tiled=True)
 
     def hop(kernel, first, out, *args):

time: 57.1 us -> 56.3 us (0.986)
  Pallas kernels: 10.1 us -> 9.51 us
    pallas_call x1, Pallas kernels: 4.25 us -> 3.06 us  [per_device(): call(functools.partial(attend_kernel, steps, requests, heads, adapters_he...]
  transfers between devices with their start and end apart: 8 -> 8, of which waited for: 3 -> 3; matrix products, arithmetic and copies ran while one was open for 0% -> 0% of each run, Pallas kernels for 4% -> 3%
where the time goes in v5:
time: 56.3 us; the launch traced here: 56 us
  starting transfers between devices  20.1 us (36%)
  blocking collectives  14.2 us (25%)
  waiting for transfers between devices  12 us (21%)
  Pallas kernels  9.51 us (17%)
    all_to_all x1, blocking collectives, per_device(): got = lax.all_to_all(send, 'batch', split_axis=0, concat_axis=0, tiled=True)  14.2 us
    all_to_all x1, starting transfers between devices, per_device(): low = lax.all_to_all(low, 'z', split_axis=0, concat_axis=0, tiled=True)  7.56 us
    all_to_all x1, waiting for transfers between devices, per_device(): low = lax.all_to_all(low, 'z', split_axis=0, concat_axis=0, tiled=True)  5.93 us
    all_to_all x1, waiting for transfers between devices, per_device(): lax.all_to_all(term, 'batch', split_axis=0, concat_axis=0, tiled=True)  5.58 us
    all_to_all x1, starting transfers between devices, per_device(): lax.all_to_all(term, 'batch', split_axis=0, concat_axis=0, tiled=True)  4.76 us
    ppermute x1, starting transfers between devices, per_device(): sums = lax.ppermute(hop(hop_kernel, 0, two, ours, others, sums), 'z', even)  3.31 us
    ppermute x2, starting transfers between devices, per_device(): sums = lax.ppermute(sums, 'z', odd)  3.14 us
    pallas_call x1, Pallas kernels, per_device(): call(functools.partial(attend_kernel, steps, requests, heads, adapters_he...  3.06 us
  transfers between devices with their start and end apart: 8, of which 3 were waited for; matrix products, arithmetic and copies ran while one was open for 0% of the time, Pallas kernels for 3%

profile of v5, /device:TPU:2, one launch (start us, length us, event | category | flops | bytes accessed | tf_op | source)
XLA Modules:
  0.0 56.0 jit_solution(4283325003610444167)
XLA Ops:
  0.0 0.0 copy-start
  0.0 3.1 %shard_map.136 = (bf16[64,768]{1,0:T(8,128)(2,1)S(1)}, bf16[128,768]{1,0:T(8,128)(2,1)S(1)}, bf16[64,128]{1,0:T(8,128)(2,1)S(1)}, bf16[256,8192]{1,0:T(8,128)(2,1)S(1)}) custom-call(s32[16]{0:T(128)} %tenant_in.1, s32[16]{0:T(128)} %length_in.1, s32[4,16]{1,0:T(4,128)} %admitted_in.1, s32[512]{0:T(512)} %tenant_adapter_in.1, s32[128]{0:T(128)} %adapter_slot_in.1, ...), custom_call_target="tpu_custom_call" | custom-call | flops 33554432 | bytes 2097152 | tf_op jit(solution)/shard_map/pallas_call | solution.py:478
  3.1 14.2 %all_to_all.27 = bf16[16,8,768]{2,1,0:T(8,128)(2,1)S(1)} all-to-all(bf16[16,8,768]{2,1,0:T(8,128)(2,1)S(1)} %bitcast.13), channel_id=1, replica_groups=mesh['batch'=16,'z'=8,'core'=2] {'batch'}, dimensions={0} | all-to-all | bytes 393216 | tf_op jit(solution)/shard_map/all_to_all | solution.py:528
  17.3 0.0 copy-done
  17.3 3.1 %shard_map.137 = (f32[64,128]{1,0:T(8,128)S(1)}, bf16[64,1280]{1,0:T(8,128)(2,1)S(1)}, bf16[6,64,512]{2,1,0:T(8,128)(2,1)S(1)}, bf16[64,512]{1,0:T(8,128)(2,1)S(1)}, bf16[256,8192]{1,0:T(8,128)(2,1)S(1)}) custom-call(bf16[128,768]{1,0:T(8,128)(2,1)S(1)} %bitcast.10, bf16[64,768]{1,0:T(8,128)(2,1)S(1)} %get-tuple-element.18.home_ref, ...), custom_call_target="tpu_custom_call" | custom-call | flops 67108864 | bytes 4194304 | tf_op jit(solution)/shard_map/pallas_call | solution.py:534
  20.4 0.1 collective-permute-start
  20.5 0.0 copy-start.1
  20.5 0.9 %shard_map.138.ours_ref = f32[8,64,512]{2,1,0:T(8,128)S(1)} custom-call(bf16[64,512]{1,0:T(8,128)(2,1)S(1)} %get-tuple-element.20.rows_ref, bf16[256,8192]{1,0:T(8,128)(2,1)S(1)} %get-tuple-element.19.weight_ref, bf16[256,8192]{1,0:T(8,128)(2,1)S(1)} %get-tuple-element.21.late_ref), custom_call_target="tpu_custom_call" | custom-call | flops 268435456 | bytes 4194304 | tf_op jit(solution)/shard_map/pallas_call | solution.py:551
  21.4 0.5 collective-permute-done.came_ref
  21.9 0.7 %shard_map.139 = (bf16[8,64,128]{2,1,0:T(8,128)(2,1)}, bf16[2,64,512]{2,1,0:T(8,128)(2,1)S(1)}, bf16[6,64,512]{2,1,0:T(8,128)(2,1)S(1)}) custom-call(f32[64,128]{1,0:T(8,128)S(1)} %get-tuple-element.22.low_ref, f32[8,64,512]{2,1,0:T(8,128)S(1)} %shard_map.138.ours_ref, bf16[64,1280]{1,0:T(8,128)(2,1)S(1)} %collective-permute-done.came_ref, ...), custom_call_target="tpu_custom_call" | custom-call | flops 131072 | bytes 524288 | tf_op jit(solution)/shard_map/pallas_call | solution.py:559
  22.6 0.1 collective-permute-start.1
  22.7 1.9 %collective-permute-start.2 = (bf16[2,64,512]{2,1,0:T(8,128)(2,1)S(1)}, bf16[2,64,512]{2,1,0:T(8,128)(2,1)S(1)}, u32[]{:S(2)}, u32[]{:S(2)}) collective-permute-start(bf16[2,64,512]{2,1,0:T(8,128)(2,1)S(1)} %get-tuple-element.26), channel_id=1, source_target_pairs={{0,2},{2,0},{4,6},{6,4},{8,10},{10,8},{12,14},{14,12},{1,3},{3,1},... | collective-permute-start | bytes 393224 | tf_op jit(solution)/shard_map/ppermute | solution.py:582
  24.6 7.6 %all-to-all-start.1 = ((bf16[8,64,128]{2,1,0:T(8,128)(2,1)}), bf16[8,64,128]{2,1,0:T(8,128)(2,1)S(1)}, u32[]{:S(2)}, u32[]{:S(2)}) async-start(bf16[8,64,128]{2,1,0:T(8,128)(2,1)} %get-tuple-element.27), calls=%async_computation.1 | async-start | bytes 262144 | tf_op jit(solution)/shard_map/all_to_all | solution.py:568
  32.2 0.0 collective-permute-done.2.came_ref
  32.2 0.0 collective-permute-done.1.others_ref
  32.3 3.3 %collective-permute-start.3 = (bf16[2,64,512]{2,1,0:T(8,128)(2,1)S(1)}, bf16[2,64,512]{2,1,0:T(8,128)(2,1)S(1)}, u32[]{:S(2)}, u32[]{:S(2)}) collective-permute-start(bf16[2,64,512]{2,1,0:T(8,128)(2,1)S(1)} %shard_map.140), channel_id=1, source_target_pairs={{0,14},{2,4},{4,2},{6,8},{8,6},{10,12},{12,10},{14,0},{1,15},{3,5}... | collective-permute-start | bytes 393224 | tf_op jit(solution)/shard_map/ppermute | solution.py:583
  35.6 5.9 %all-to-all-done.1.parts_ref = bf16[8,64,128]{2,1,0:T(8,128)(2,1)S(1)} async-done(((bf16[8,64,128]{2,1,0:T(8,128)(2,1)}), bf16[8,64,128]{2,1,0:T(8,128)(2,1)S(1)}, u32[]{:S(2)}, u32[]{:S(2)}) %all-to-all-start.1) | async-done | bytes 131104 | tf_op jit(solution)/shard_map/all_to_all | solution.py:568
  41.5 0.0 copy-done.1
  41.5 0.9 %shard_map.141.after_ref = bf16[128,512]{1,0:T(8,128)(2,1)} custom-call(bf16[8,64,128]{2,1,0:T(8,128)(2,1)S(1)} %all-to-all-done.1.parts_ref, bf16[128,128]{1,0:T(8,128)(2,1)S(1)} %slice.18.held_ref, bf16[8,64,512]{2,1,0:T(8,128)(2,1)S(1)} %copy-done.1), custom_call_target="tpu_custom_call" | custom-call | flops 67108864 | bytes 262144 | tf_op jit(solution)/shard_map/pallas_call | solution.py:584
  42.5 0.0 collective-permute-done.3.came_ref
  42.5 1.2 %collective-permute-start.4 = (bf16[2,64,512]{2,1,0:T(8,128)(2,1)S(1)}, bf16[2,64,512]{2,1,0:T(8,128)(2,1)S(1)}, u32[]{:S(2)}, u32[]{:S(2)}) collective-permute-start(bf16[2,64,512]{2,1,0:T(8,128)(2,1)S(1)} %shard_map.142), channel_id=1, source_target_pairs={{0,2},{2,0},{4,6},{6,4},{8,10},{10,8},{12,14},{14,12},{1,3},{3,1},... | collective-permute-start | bytes 393224 | tf_op jit(solution)/shard_map/ppermute | solution.py:593
  43.7 4.8 %all-to-all-start.2 = ((bf16[16,8,512]{2,1,0:T(8,128)(2,1)}), bf16[16,8,512]{2,1,0:T(8,128)(2,1)S(1)}, u32[]{:S(2)}, u32[]{:S(2)}) async-start(bf16[16,8,512]{2,1,0:T(8,128)(2,1)} %bitcast.7), calls=%async_computation.2 | async-start | bytes 262144 | tf_op jit(solution)/shard_map/all_to_all | solution.py:595
  48.5 0.0 collective-permute-done.4.came_ref
  48.5 1.1 %collective-permute-start.5 = (bf16[1,64,512]{2,1,0:T(8,128)(2,1)S(1)}, bf16[1,64,512]{2,1,0:T(8,128)(2,1)S(1)}, u32[]{:S(2)}, u32[]{:S(2)}) collective-permute-start(bf16[1,64,512]{2,1,0:T(8,128)(2,1)S(1)} %shard_map.143), channel_id=1, source_target_pairs={{0,14},{2,4},{4,2},{6,8},{8,6},{10,12},{12,10},{14,0},{1,15},{3,5}... | collective-permute-start | bytes 196616 | tf_op jit(solution)/shard_map/ppermute | solution.py:594
  49.6 5.6 %all-to-all-done.2 = bf16[16,8,512]{2,1,0:T(8,128)(2,1)S(1)} async-done(((bf16[16,8,512]{2,1,0:T(8,128)(2,1)}), bf16[16,8,512]{2,1,0:T(8,128)(2,1)S(1)}, u32[]{:S(2)}, u32[]{:S(2)}) %all-to-all-start.2) | async-done | bytes 131104 | tf_op jit(solution)/shard_map/all_to_all | solution.py:595
  55.2 0.0 collective-permute-done.5.second_ref
  55.2 0.8 %shard_map.144 = bf16[64,512]{1,0:T(8,128)(2,1)} custom-call(f32[1,64,512]{2,1,0:T(8,128)S(1)} %slice.16.ours_ref, bf16[1,64,512]{2,1,0:T(8,128)(2,1)S(1)} %slice.17.others_ref, bf16[1,64,512]{2,1,0:T(8,128)(2,1)S(1)} %slice.19.first_ref, bf16[1,64,512]{2,1,0:T(8,128)(2,1)S(1)} %collective-permute-done.5.second_ref, ...), custom_call_target="tpu_custom_call" | custom-call | flops 8388608 | bytes 327680 | tf_op jit(solution)/shard_map/pallas_call | solution.py:596
  (7 shorter events, 0.1 us)
Async XLA Ops:
  0.0 17.3 %copy-start = (bf16[8,64,512]{2,1,0:T(8,128)(2,1)S(1)}, bf16[8,64,512]{2,1,0:T(8,128)(2,1)}, u32[]{:S(2)}) copy-start(bf16[8,64,512]{2,1,0:T(8,128)(2,1)} %down_ref.1) | copy-start | bytes 1572868
  20.4 1.5 %collective-permute-start = (bf16[64,1280]{1,0:T(8,128)(2,1)S(1)}, bf16[64,1280]{1,0:T(8,128)(2,1)S(1)}, u32[]{:S(2)}, u32[]{:S(2)}) collective-permute-start(bf16[64,1280]{1,0:T(8,128)(2,1)S(1)} %get-tuple-element.23), channel_id=1, source_target_pairs={{0,1},{1,0},{2,3},{3,2},{4,5},{5,4},{6,7},{7,6},{8,9},{9,8},{10,11... | collective-permute-start | bytes 491528 | tf_op jit(solution)/shard_map/ppermute | solution.py:550
  20.5 21.0 %copy-start.1 = (bf16[8,64,512]{2,1,0:T(8,128)(2,1)S(1)}, bf16[8,64,512]{2,1,0:T(8,128)(2,1)}, u32[]{:S(2)}) copy-start(bf16[8,64,512]{2,1,0:T(8,128)(2,1)} %up_ref.1) | copy-start | bytes 1572868
  22.6 9.7 %collective-permute-start.1 = (bf16[6,64,512]{2,1,0:T(8,128)(2,1)S(1)}, bf16[6,64,512]{2,1,0:T(8,128)(2,1)S(1)}, u32[]{:S(2)}, u32[]{:S(2)}) collective-permute-start(bf16[6,64,512]{2,1,0:T(8,128)(2,1)S(1)} %get-tuple-element.25), channel_id=1, source_target_pairs={{0,1},{1,0},{2,3},{3,2},{4,5},{5,4},{6,7},{7,6},{8,9},{9,8},{10,11... | collective-permute-start | bytes 1179656 | tf_op jit(solution)/shard_map/ppermute | solution.py:567
  22.7 9.5 %collective-permute-start.2 = (bf16[2,64,512]{2,1,0:T(8,128)(2,1)S(1)}, bf16[2,64,512]{2,1,0:T(8,128)(2,1)S(1)}, u32[]{:S(2)}, u32[]{:S(2)}) collective-permute-start(bf16[2,64,512]{2,1,0:T(8,128)(2,1)S(1)} %get-tuple-element.26), channel_id=1, source_target_pairs={{0,2},{2,0},{4,6},{6,4},{8,10},{10,8},{12,14},{14,12},{1,3},{3,1},... | collective-permute-start | bytes 393224 | tf_op jit(solution)/shard_map/ppermute | solution.py:582
  24.6 16.9 %all-to-all-start.1 = ((bf16[8,64,128]{2,1,0:T(8,128)(2,1)}), bf16[8,64,128]{2,1,0:T(8,128)(2,1)S(1)}, u32[]{:S(2)}, u32[]{:S(2)}) async-start(bf16[8,64,128]{2,1,0:T(8,128)(2,1)} %get-tuple-element.27), calls=%async_computation.1 | async-start | bytes 262144 | tf_op jit(solution)/shard_map/all_to_all | solution.py:568
  32.3 10.2 %collective-permute-start.3 = (bf16[2,64,512]{2,1,0:T(8,128)(2,1)S(1)}, bf16[2,64,512]{2,1,0:T(8,128)(2,1)S(1)}, u32[]{:S(2)}, u32[]{:S(2)}) collective-permute-start(bf16[2,64,512]{2,1,0:T(8,128)(2,1)S(1)} %shard_map.140), channel_id=1, source_target_pairs={{0,14},{2,4},{4,2},{6,8},{8,6},{10,12},{12,10},{14,0},{1,15},{3,5}... | collective-permute-start | bytes 393224 | tf_op jit(solution)/shard_map/ppermute | solution.py:583
  42.5 6.0 %collective-permute-start.4 = (bf16[2,64,512]{2,1,0:T(8,128)(2,1)S(1)}, bf16[2,64,512]{2,1,0:T(8,128)(2,1)S(1)}, u32[]{:S(2)}, u32[]{:S(2)}) collective-permute-start(bf16[2,64,512]{2,1,0:T(8,128)(2,1)S(1)} %shard_map.142), channel_id=1, source_target_pairs={{0,2},{2,0},{4,6},{6,4},{8,10},{10,8},{12,14},{14,12},{1,3},{3,1},... | collective-permute-start | bytes 393224 | tf_op jit(solution)/shard_map/ppermute | solution.py:593
  43.7 11.5 %all-to-all-start.2 = ((bf16[16,8,512]{2,1,0:T(8,128)(2,1)}), bf16[16,8,512]{2,1,0:T(8,128)(2,1)S(1)}, u32[]{:S(2)}, u32[]{:S(2)}) async-start(bf16[16,8,512]{2,1,0:T(8,128)(2,1)} %bitcast.7), calls=%async_computation.2 | async-start | bytes 262144 | tf_op jit(solution)/shard_map/all_to_all | solution.py:595
  48.5 6.7 %collective-permute-start.5 = (bf16[1,64,512]{2,1,0:T(8,128)(2,1)S(1)}, bf16[1,64,512]{2,1,0:T(8,128)(2,1)S(1)}, u32[]{:S(2)}, u32[]{:S(2)}) collective-permute-start(bf16[1,64,512]{2,1,0:T(8,128)(2,1)S(1)} %shard_map.143), channel_id=1, source_target_pairs={{0,14},{2,4},{4,2},{6,8},{8,6},{10,12},{12,10},{14,0},{1,15},{3,5}... | collective-permute-start | bytes 196616 | tf_op jit(solution)/shard_map/ppermute | solution.py:594

commit v6 on v5

--- a/solution.py
+++ b/solution.py
@@ -364,7 +364,7 @@
     upper = low.astype(bf16)
     theirs_ref[:, start : start + lanes] = upper
     theirs_ref[:, start + lanes :] = (low - upper.astype(f32)).astype(bf16)
-    for index, product in enumerate(project(1, other_blocks, final_ref, weight_ref, late_ref)):
+    for index, product in enumerate(project(1, other_blocks[:1], final_ref, weight_ref, late_ref)):
         others_ref[index] = product.astype(bf16)
 
 
@@ -386,13 +386,15 @@
     return products
 
 
-def ours_kernel(rows_ref, weight_ref, late_ref, out_ref):
+def rest_kernel(rows_ref, weight_ref, late_ref, out_ref, others_ref):
     blocks = first_blocks + other_blocks
     for index, product in enumerate(project(0, blocks, rows_ref, weight_ref, late_ref)):
         out_ref[index] = product
-
-
-def mix_kernel(low_ref, ours_ref, came_ref, others_ref, low_out, first_out, others_out):
+    for index, product in enumerate(project(1, other_blocks[1:], rows_ref, weight_ref, late_ref)):
+        others_ref[index] = product.astype(bf16)
+
+
+def mix_kernel(low_ref, ours_ref, came_ref, next_ref, others_ref, low_out, first_out, others_out):
     count, _, width = first_out.shape
     start = count * width
     other = came_ref[:, start : start + lanes].astype(f32)
@@ -403,7 +405,8 @@
     for index in range(count):
         came = came_ref[:, index * width : (index + 1) * width].astype(f32)
         first_out[index] = (ours_ref[index] + came).astype(bf16)
-    others_out[...] = others_ref[...]
+    others_out[0:1] = next_ref[...]
+    others_out[1:] = others_ref[...]
 
 
 def hop_kernel(first, ours_ref, others_ref, came_ref, out_ref):
@@ -531,12 +534,12 @@
     one = shape((1, pairs, features), bf16)
     six = shape((len(other_blocks), pairs, features), bf16)
     blocks = shape((parts, pairs, features), f32)
-    low, theirs, others, final, late = call(
+    low, theirs, following, final, late = call(
         functools.partial(combine_kernel, steps, heads, width, threshold),
         (
             shape((slots // 2, lanes), f32),
             shape((pairs, 2 * features + 2 * lanes), bf16),
-            six,
+            one,
             shape((pairs, features), bf16),
             pltpu.VMEM((features - early, out_weight.shape[1]), bf16),
         ),
@@ -548,22 +551,22 @@
     )(got, home, adapter_down_factor, weight, in_hbm(out_weight))
     swap = [(0, 1), (1, 0)]
     theirs = lax.ppermute(theirs, "core", swap)
-    ours = call(
-        ours_kernel,
-        blocks,
+    ours, others = call(
+        rest_kernel,
+        (blocks, shape((len(other_blocks) - 1, pairs, features), bf16)),
         [VMEM] * 3,
-        VMEM,
+        (VMEM,) * 2,
         pairs * out_weight.size,
         out_weight.size,
     )(final, weight, in_vmem(late))
     low, sums, others = call(
         mix_kernel,
         (shape((parts, slots // 2, lanes), bf16), two, six),
-        [VMEM] * 4,
+        [VMEM] * 5,
         (VMEM,) * 3,
         2 * two.size,
         8 * two.size,
-    )(low, ours, theirs, others)
+    )(low, ours, theirs, following, others)
     others = lax.ppermute(others, "core", swap)
     low = lax.all_to_all(low, "z", split_axis=0, concat_axis=0, tiled=True)
 

time: 56.3 us -> 55.8 us (level)
  waiting for transfers between devices: 12 us -> 11.3 us
  transfers between devices with their start and end apart: 8 -> 8, of which waited for: 3 -> 3; matrix products, arithmetic and copies ran while one was open for 0% -> 0% of each run, Pallas kernels for 3% -> 4%
where the time goes in v6:
time: 55.8 us; the launch traced here: 55.4 us
  starting transfers between devices  20.3 us (36%)
  blocking collectives  14.2 us (25%)
  waiting for transfers between devices  11.3 us (20%)
  Pallas kernels  9.53 us (17%)
    all_to_all x1, blocking collectives, per_device(): got = lax.all_to_all(send, 'batch', split_axis=0, concat_axis=0, tiled=True)  14.2 us
    all_to_all x1, starting transfers between devices, per_device(): low = lax.all_to_all(low, 'z', split_axis=0, concat_axis=0, tiled=True)  7.57 us
    all_to_all x1, waiting for transfers between devices, per_device(): low = lax.all_to_all(low, 'z', split_axis=0, concat_axis=0, tiled=True)  5.71 us
    all_to_all x1, waiting for transfers between devices, per_device(): lax.all_to_all(term, 'batch', split_axis=0, concat_axis=0, tiled=True)  5.48 us
    all_to_all x1, starting transfers between devices, per_device(): lax.all_to_all(term, 'batch', split_axis=0, concat_axis=0, tiled=True)  4.76 us
    ppermute x1, starting transfers between devices, per_device(): sums = lax.ppermute(hop(hop_kernel, 0, two, ours, others, sums), 'z', even)  3.31 us
    pallas_call x1, Pallas kernels, per_device(): call(functools.partial(attend_kernel, steps, requests, heads, adapters_he...  3.06 us
    ppermute x2, starting transfers between devices, per_device(): sums = lax.ppermute(sums, 'z', odd)  2.97 us
  transfers between devices with their start and end apart: 8, of which 3 were waited for; matrix products, arithmetic and copies ran while one was open for 0% of the time, Pallas kernels for 4%

profile of v6, /device:TPU:2, one launch (start us, length us, event | category | flops | bytes accessed | tf_op | source)
XLA Modules:
  0.0 55.4 jit_solution(13789371712352912369)
XLA Ops:
  0.0 0.0 copy-start
  0.0 3.1 %shard_map.136 = (bf16[64,768]{1,0:T(8,128)(2,1)S(1)}, bf16[128,768]{1,0:T(8,128)(2,1)S(1)}, bf16[64,128]{1,0:T(8,128)(2,1)S(1)}, bf16[256,8192]{1,0:T(8,128)(2,1)S(1)}) custom-call(s32[16]{0:T(128)} %tenant_in.1, s32[16]{0:T(128)} %length_in.1, s32[4,16]{1,0:T(4,128)} %admitted_in.1, s32[512]{0:T(512)} %tenant_adapter_in.1, s32[128]{0:T(128)} %adapter_slot_in.1, ...), custom_call_target="tpu_custom_call" | custom-call | flops 33554432 | bytes 2097152 | tf_op jit(solution)/shard_map/pallas_call | solution.py:481
  3.1 14.2 %all_to_all.27 = bf16[16,8,768]{2,1,0:T(8,128)(2,1)S(1)} all-to-all(bf16[16,8,768]{2,1,0:T(8,128)(2,1)S(1)} %bitcast.13), channel_id=1, replica_groups=mesh['batch'=16,'z'=8,'core'=2] {'batch'}, dimensions={0} | all-to-all | bytes 393216 | tf_op jit(solution)/shard_map/all_to_all | solution.py:531
  17.3 0.0 copy-done
  17.3 2.6 %shard_map.137 = (f32[64,128]{1,0:T(8,128)S(1)}, bf16[64,1280]{1,0:T(8,128)(2,1)S(1)}, bf16[1,64,512]{2,1,0:T(8,128)(2,1)S(1)}, bf16[64,512]{1,0:T(8,128)(2,1)S(1)}, bf16[256,8192]{1,0:T(8,128)(2,1)S(1)}) custom-call(bf16[128,768]{1,0:T(8,128)(2,1)S(1)} %bitcast.10, bf16[64,768]{1,0:T(8,128)(2,1)S(1)} %get-tuple-element.20.home_ref, ...), custom_call_target="tpu_custom_call" | custom-call | flops 67108864 | bytes 4194304 | tf_op jit(solution)/shard_map/pallas_call | solution.py:537
  19.9 0.1 collective-permute-start
  20.0 0.0 copy-start.1
  20.0 1.3 %shard_map.138 = (f32[8,64,512]{2,1,0:T(8,128)S(1)}, bf16[5,64,512]{2,1,0:T(8,128)(2,1)S(1)}) custom-call(bf16[64,512]{1,0:T(8,128)(2,1)S(1)} %get-tuple-element.22.rows_ref, bf16[256,8192]{1,0:T(8,128)(2,1)S(1)} %get-tuple-element.21.weight_ref, bf16[256,8192]{1,0:T(8,128)(2,1)S(1)} %get-tuple-element.23.late_ref), custom_call_target="tpu_custom_call" | custom-call | flops 268435456 | bytes 4194304 | tf_op jit(solution)/shard_map/pallas_call | solution.py:554
  21.4 0.1 collective-permute-done.came_ref
  21.4 0.7 %shard_map.139 = (bf16[8,64,128]{2,1,0:T(8,128)(2,1)}, bf16[2,64,512]{2,1,0:T(8,128)(2,1)S(1)}, bf16[6,64,512]{2,1,0:T(8,128)(2,1)S(1)}) custom-call(f32[64,128]{1,0:T(8,128)S(1)} %get-tuple-element.25.low_ref, f32[8,64,512]{2,1,0:T(8,128)S(1)} %get-tuple-element.24.ours_ref, bf16[64,1280]{1,0:T(8,128)(2,1)S(1)} %collective-permute-done.came_ref, ...), custom_call_target="tpu_custom_call" | custom-call | flops 131072 | bytes 524288 | tf_op jit(solution)/shard_map/pallas_call | solution.py:562
  22.1 0.4 collective-permute-start.1
  22.6 1.9 %collective-permute-start.2 = (bf16[2,64,512]{2,1,0:T(8,128)(2,1)S(1)}, bf16[2,64,512]{2,1,0:T(8,128)(2,1)S(1)}, u32[]{:S(2)}, u32[]{:S(2)}) collective-permute-start(bf16[2,64,512]{2,1,0:T(8,128)(2,1)S(1)} %get-tuple-element.30), channel_id=1, source_target_pairs={{0,2},{2,0},{4,6},{6,4},{8,10},{10,8},{12,14},{14,12},{1,3},{3,1},... | collective-permute-start | bytes 393224 | tf_op jit(solution)/shard_map/ppermute | solution.py:585
  24.5 7.6 %all-to-all-start.1 = ((bf16[8,64,128]{2,1,0:T(8,128)(2,1)}), bf16[8,64,128]{2,1,0:T(8,128)(2,1)S(1)}, u32[]{:S(2)}, u32[]{:S(2)}) async-start(bf16[8,64,128]{2,1,0:T(8,128)(2,1)} %get-tuple-element.31), calls=%async_computation.1 | async-start | bytes 262144 | tf_op jit(solution)/shard_map/all_to_all | solution.py:571
  32.0 0.0 collective-permute-done.2.came_ref
  32.0 0.0 collective-permute-done.1.others_ref
  32.1 3.3 %collective-permute-start.3 = (bf16[2,64,512]{2,1,0:T(8,128)(2,1)S(1)}, bf16[2,64,512]{2,1,0:T(8,128)(2,1)S(1)}, u32[]{:S(2)}, u32[]{:S(2)}) collective-permute-start(bf16[2,64,512]{2,1,0:T(8,128)(2,1)S(1)} %shard_map.140), channel_id=1, source_target_pairs={{0,14},{2,4},{4,2},{6,8},{8,6},{10,12},{12,10},{14,0},{1,15},{3,5}... | collective-permute-start | bytes 393224 | tf_op jit(solution)/shard_map/ppermute | solution.py:586
  35.4 5.7 %all-to-all-done.1.parts_ref = bf16[8,64,128]{2,1,0:T(8,128)(2,1)S(1)} async-done(((bf16[8,64,128]{2,1,0:T(8,128)(2,1)}), bf16[8,64,128]{2,1,0:T(8,128)(2,1)S(1)}, u32[]{:S(2)}, u32[]{:S(2)}) %all-to-all-start.1) | async-done | bytes 131104 | tf_op jit(solution)/shard_map/all_to_all | solution.py:571
  41.1 0.0 copy-done.1
  41.1 0.9 %shard_map.141.after_ref = bf16[128,512]{1,0:T(8,128)(2,1)} custom-call(bf16[8,64,128]{2,1,0:T(8,128)(2,1)S(1)} %all-to-all-done.1.parts_ref, bf16[128,128]{1,0:T(8,128)(2,1)S(1)} %slice.17.held_ref, bf16[8,64,512]{2,1,0:T(8,128)(2,1)S(1)} %copy-done.1), custom_call_target="tpu_custom_call" | custom-call | flops 67108864 | bytes 262144 | tf_op jit(solution)/shard_map/pallas_call | solution.py:587
  42.1 0.0 collective-permute-done.3.came_ref
  42.1 1.0 %collective-permute-start.4 = (bf16[2,64,512]{2,1,0:T(8,128)(2,1)S(1)}, bf16[2,64,512]{2,1,0:T(8,128)(2,1)S(1)}, u32[]{:S(2)}, u32[]{:S(2)}) collective-permute-start(bf16[2,64,512]{2,1,0:T(8,128)(2,1)S(1)} %shard_map.142), channel_id=1, source_target_pairs={{0,2},{2,0},{4,6},{6,4},{8,10},{10,8},{12,14},{14,12},{1,3},{3,1},... | collective-permute-start | bytes 393224 | tf_op jit(solution)/shard_map/ppermute | solution.py:596
  43.2 4.8 %all-to-all-start.2 = ((bf16[16,8,512]{2,1,0:T(8,128)(2,1)}), bf16[16,8,512]{2,1,0:T(8,128)(2,1)S(1)}, u32[]{:S(2)}, u32[]{:S(2)}) async-start(bf16[16,8,512]{2,1,0:T(8,128)(2,1)} %bitcast.7), calls=%async_computation.2 | async-start | bytes 262144 | tf_op jit(solution)/shard_map/all_to_all | solution.py:598
  47.9 0.0 collective-permute-done.4.came_ref
  48.0 1.2 %collective-permute-start.5 = (bf16[1,64,512]{2,1,0:T(8,128)(2,1)S(1)}, bf16[1,64,512]{2,1,0:T(8,128)(2,1)S(1)}, u32[]{:S(2)}, u32[]{:S(2)}) collective-permute-start(bf16[1,64,512]{2,1,0:T(8,128)(2,1)S(1)} %shard_map.143), channel_id=1, source_target_pairs={{0,14},{2,4},{4,2},{6,8},{8,6},{10,12},{12,10},{14,0},{1,15},{3,5}... | collective-permute-start | bytes 196616 | tf_op jit(solution)/shard_map/ppermute | solution.py:597
  49.2 5.5 %all-to-all-done.2 = bf16[16,8,512]{2,1,0:T(8,128)(2,1)S(1)} async-done(((bf16[16,8,512]{2,1,0:T(8,128)(2,1)}), bf16[16,8,512]{2,1,0:T(8,128)(2,1)S(1)}, u32[]{:S(2)}, u32[]{:S(2)}) %all-to-all-start.2) | async-done | bytes 131104 | tf_op jit(solution)/shard_map/all_to_all | solution.py:598
  54.6 0.0 collective-permute-done.5.second_ref
  54.7 0.8 %shard_map.144 = bf16[64,512]{1,0:T(8,128)(2,1)} custom-call(f32[1,64,512]{2,1,0:T(8,128)S(1)} %slice.12.ours_ref, bf16[1,64,512]{2,1,0:T(8,128)(2,1)S(1)} %slice.16.others_ref, bf16[1,64,512]{2,1,0:T(8,128)(2,1)S(1)} %slice.18.first_ref, bf16[1,64,512]{2,1,0:T(8,128)(2,1)S(1)} %collective-permute-done.5.second_ref, ...), custom_call_target="tpu_custom_call" | custom-call | flops 8388608 | bytes 327680 | tf_op jit(solution)/shard_map/pallas_call | solution.py:599
  (7 shorter events, 0.1 us)
Async XLA Ops:
  0.0 17.3 %copy-start = (bf16[8,64,512]{2,1,0:T(8,128)(2,1)S(1)}, bf16[8,64,512]{2,1,0:T(8,128)(2,1)}, u32[]{:S(2)}) copy-start(bf16[8,64,512]{2,1,0:T(8,128)(2,1)} %down_ref.1) | copy-start | bytes 1572868
  19.9 1.5 %collective-permute-start = (bf16[64,1280]{1,0:T(8,128)(2,1)S(1)}, bf16[64,1280]{1,0:T(8,128)(2,1)S(1)}, u32[]{:S(2)}, u32[]{:S(2)}) collective-permute-start(bf16[64,1280]{1,0:T(8,128)(2,1)S(1)} %get-tuple-element.26), channel_id=1, source_target_pairs={{0,1},{1,0},{2,3},{3,2},{4,5},{5,4},{6,7},{7,6},{8,9},{9,8},{10,11... | collective-permute-start | bytes 491528 | tf_op jit(solution)/shard_map/ppermute | solution.py:553
  20.0 21.1 %copy-start.1 = (bf16[8,64,512]{2,1,0:T(8,128)(2,1)S(1)}, bf16[8,64,512]{2,1,0:T(8,128)(2,1)}, u32[]{:S(2)}) copy-start(bf16[8,64,512]{2,1,0:T(8,128)(2,1)} %up_ref.1) | copy-start | bytes 1572868
  22.1 9.9 %collective-permute-start.1 = (bf16[6,64,512]{2,1,0:T(8,128)(2,1)S(1)}, bf16[6,64,512]{2,1,0:T(8,128)(2,1)S(1)}, u32[]{:S(2)}, u32[]{:S(2)}) collective-permute-start(bf16[6,64,512]{2,1,0:T(8,128)(2,1)S(1)} %get-tuple-element.29), channel_id=1, source_target_pairs={{0,1},{1,0},{2,3},{3,2},{4,5},{5,4},{6,7},{7,6},{8,9},{9,8},{10,11... | collective-permute-start | bytes 1179656 | tf_op jit(solution)/shard_map/ppermute | solution.py:570
  22.6 9.5 %collective-permute-start.2 = (bf16[2,64,512]{2,1,0:T(8,128)(2,1)S(1)}, bf16[2,64,512]{2,1,0:T(8,128)(2,1)S(1)}, u32[]{:S(2)}, u32[]{:S(2)}) collective-permute-start(bf16[2,64,512]{2,1,0:T(8,128)(2,1)S(1)} %get-tuple-element.30), channel_id=1, source_target_pairs={{0,2},{2,0},{4,6},{6,4},{8,10},{10,8},{12,14},{14,12},{1,3},{3,1},... | collective-permute-start | bytes 393224 | tf_op jit(solution)/shard_map/ppermute | solution.py:585
  24.5 16.7 %all-to-all-start.1 = ((bf16[8,64,128]{2,1,0:T(8,128)(2,1)}), bf16[8,64,128]{2,1,0:T(8,128)(2,1)S(1)}, u32[]{:S(2)}, u32[]{:S(2)}) async-start(bf16[8,64,128]{2,1,0:T(8,128)(2,1)} %get-tuple-element.31), calls=%async_computation.1 | async-start | bytes 262144 | tf_op jit(solution)/shard_map/all_to_all | solution.py:571
  32.1 10.0 %collective-permute-start.3 = (bf16[2,64,512]{2,1,0:T(8,128)(2,1)S(1)}, bf16[2,64,512]{2,1,0:T(8,128)(2,1)S(1)}, u32[]{:S(2)}, u32[]{:S(2)}) collective-permute-start(bf16[2,64,512]{2,1,0:T(8,128)(2,1)S(1)} %shard_map.140), channel_id=1, source_target_pairs={{0,14},{2,4},{4,2},{6,8},{8,6},{10,12},{12,10},{14,0},{1,15},{3,5}... | collective-permute-start | bytes 393224 | tf_op jit(solution)/shard_map/ppermute | solution.py:586
  42.1 5.8 %collective-permute-start.4 = (bf16[2,64,512]{2,1,0:T(8,128)(2,1)S(1)}, bf16[2,64,512]{2,1,0:T(8,128)(2,1)S(1)}, u32[]{:S(2)}, u32[]{:S(2)}) collective-permute-start(bf16[2,64,512]{2,1,0:T(8,128)(2,1)S(1)} %shard_map.142), channel_id=1, source_target_pairs={{0,2},{2,0},{4,6},{6,4},{8,10},{10,8},{12,14},{14,12},{1,3},{3,1},... | collective-permute-start | bytes 393224 | tf_op jit(solution)/shard_map/ppermute | solution.py:596
  43.2 11.5 %all-to-all-start.2 = ((bf16[16,8,512]{2,1,0:T(8,128)(2,1)}), bf16[16,8,512]{2,1,0:T(8,128)(2,1)S(1)}, u32[]{:S(2)}, u32[]{:S(2)}) async-start(bf16[16,8,512]{2,1,0:T(8,128)(2,1)} %bitcast.7), calls=%async_computation.2 | async-start | bytes 262144 | tf_op jit(solution)/shard_map/all_to_all | solution.py:598
  48.0 6.7 %collective-permute-start.5 = (bf16[1,64,512]{2,1,0:T(8,128)(2,1)S(1)}, bf16[1,64,512]{2,1,0:T(8,128)(2,1)S(1)}, u32[]{:S(2)}, u32[]{:S(2)}) collective-permute-start(bf16[1,64,512]{2,1,0:T(8,128)(2,1)S(1)} %shard_map.143), channel_id=1, source_target_pairs={{0,14},{2,4},{4,2},{6,8},{8,6},{10,12},{12,10},{14,0},{1,15},{3,5}... | collective-permute-start | bytes 196616 | tf_op jit(solution)/shard_map/ppermute | solution.py:597

commit v7 on v6

--- a/solution.py
+++ b/solution.py
@@ -375,7 +375,7 @@
     core = lax.axis_index("core")
     mine = core if flip == 0 else 1 - core
     here = lax.axis_index("z")
-    way = 1 - 2 * lax.rem(here, 2)
+    way = 2 * lax.rem(here, 2) - 1
     products = []
     for part in wanted:
         target = lax.rem(here + way * part + parts, parts)
@@ -438,11 +438,14 @@
     out_ref[...] = dot(wide, up_ref[...].reshape(every, up_ref.shape[2])).astype(bf16)
 
 
-def finish_kernel(ours_ref, others_ref, first_ref, second_ref, back_ref, term_ref, out_ref):
+def sum_kernel(ours_ref, others_ref, first_ref, second_ref, out_ref):
     total = ours_ref[0] + others_ref[0].astype(f32)
-    total = total + first_ref[0].astype(f32) + second_ref[0].astype(f32)
+    out_ref[...] = total + first_ref[0].astype(f32) + second_ref[0].astype(f32)
+
+
+def finish_kernel(base_ref, back_ref, term_ref, out_ref):
     term = dot(back_ref[...], term_ref[...])
-    out_ref[...] = (total + adapter_scale * term).astype(bf16)
+    out_ref[...] = (base_ref[...] + adapter_scale * term).astype(bf16)
 
 
 def per_device(
@@ -580,8 +583,8 @@
             6 * out.size,
         )(*args)
 
-    odd = [(i, i + 1 - 2 * (i % 2)) for i in range(parts)]
-    even = [(i, (i - 1 + 2 * (i % 2)) % parts) for i in range(parts)]
+    even = [(i, i + 1 - 2 * (i % 2)) for i in range(parts)]
+    odd = [(i, (i - 1 + 2 * (i % 2)) % parts) for i in range(parts)]
     sums = lax.ppermute(sums, "z", odd)
     sums = lax.ppermute(hop(hop_kernel, 0, two, ours, others, sums), "z", even)
     term = call(
@@ -596,14 +599,22 @@
     sums = lax.ppermute(sums, "z", odd)
     last = lax.ppermute(hop(hop_kernel, 4, one, ours, others, sums), "z", even)
     term = lax.all_to_all(term, "batch", split_axis=0, concat_axis=0, tiled=True)
+    base = call(
+        sum_kernel,
+        shape((pairs, features), f32),
+        [VMEM] * 4,
+        VMEM,
+        4 * one.size,
+        12 * one.size,
+    )(ours[-1:], others[-1:], sums[1:], last)
     out = call(
         finish_kernel,
         shape((pairs, features), bf16),
-        [VMEM] * 6,
+        [VMEM] * 3,
         VMEM,
         2 * pairs * slots * features,
         10 * one.size,
-    )(ours[-1:], others[-1:], sums[1:], last, back, term)
+    )(base, back, term)
     return out.reshape(steps, requests, features)
 
 

time: 55.8 us -> 55.7 us (level)
  starting transfers between devices: 20.3 us -> 16.6 us
  waiting for transfers between devices: 11.3 us -> 14.8 us
    all_to_all x1, waiting for transfers between devices: 5.48 us -> 1.1 us  [per_device(): lax.all_to_all(term, 'batch', split_axis=0, concat_axis=0, tiled=True)]
    ppermute x1, waiting for transfers between devices: 0.01 us -> 4.21 us  [per_device(): last = lax.ppermute(hop(hop_kernel, 4, one, ours, others, sums), 'z', even)]
    all_to_all x1, starting transfers between devices: 7.57 us -> 3.37 us  [per_device(): low = lax.all_to_all(low, 'z', split_axis=0, concat_axis=0, tiled=True)]
    ppermute x2, starting transfers between devices: 2.97 us -> 6.16 us  [per_device(): sums = lax.ppermute(sums, 'z', odd)]
    all_to_all x1, waiting for transfers between devices: 5.71 us -> 7.82 us  [per_device(): low = lax.all_to_all(low, 'z', split_axis=0, concat_axis=0, tiled=True)]
    ppermute x1, starting transfers between devices: 3.31 us -> 1.65 us  [per_device(): sums = lax.ppermute(hop(hop_kernel, 0, two, ours, others, sums), 'z', even)]
    ppermute x2, waiting for transfers between devices: 0.01 us -> 1.56 us  [per_device(): sums = lax.ppermute(sums, 'z', odd)]
    ppermute x1, starting transfers between devices: 1.16 us -> 0.09 us  [per_device(): last = lax.ppermute(hop(hop_kernel, 4, one, ours, others, sums), 'z', even)]
  transfers between devices with their start and end apart: 8 -> 8, of which waited for: 3 -> 6; matrix products, arithmetic and copies ran while one was open for 0% -> 0% of each run, Pallas kernels for 4% -> 4%
where the time goes in v7:
time: 55.7 us; the launch traced here: 55.2 us
  starting transfers between devices  16.6 us (30%)
  waiting for transfers between devices  14.8 us (27%)
  blocking collectives  14.2 us (25%)
  Pallas kernels  9.55 us (17%)
    all_to_all x1, blocking collectives, per_device(): got = lax.all_to_all(send, 'batch', split_axis=0, concat_axis=0, tiled=True)  14.2 us
    all_to_all x1, waiting for transfers between devices, per_device(): low = lax.all_to_all(low, 'z', split_axis=0, concat_axis=0, tiled=True)  7.82 us
    ppermute x2, starting transfers between devices, per_device(): sums = lax.ppermute(sums, 'z', odd)  6.16 us
    all_to_all x1, starting transfers between devices, per_device(): lax.all_to_all(term, 'batch', split_axis=0, concat_axis=0, tiled=True)  4.76 us
    ppermute x1, waiting for transfers between devices, per_device(): last = lax.ppermute(hop(hop_kernel, 4, one, ours, others, sums), 'z', even)  4.21 us
    all_to_all x1, starting transfers between devices, per_device(): low = lax.all_to_all(low, 'z', split_axis=0, concat_axis=0, tiled=True)  3.37 us
    pallas_call x1, Pallas kernels, per_device(): call(functools.partial(attend_kernel, steps, requests, heads, adapters_he...  3.06 us
    pallas_call x1, Pallas kernels, per_device(): call(functools.partial(combine_kernel, steps, heads, width, threshold), (...  2.6 us
  transfers between devices with their start and end apart: 8, of which 6 were waited for; matrix products, arithmetic and copies ran while one was open for 0% of the time, Pallas kernels for 4%

profile of v7, /device:TPU:2, one launch (start us, length us, event | category | flops | bytes accessed | tf_op | source)
XLA Modules:
  0.0 55.2 jit_solution(15548455456314534132)
XLA Ops:
  0.0 0.0 copy-start
  0.0 3.1 %shard_map.136 = (bf16[64,768]{1,0:T(8,128)(2,1)S(1)}, bf16[128,768]{1,0:T(8,128)(2,1)S(1)}, bf16[64,128]{1,0:T(8,128)(2,1)S(1)}, bf16[256,8192]{1,0:T(8,128)(2,1)S(1)}) custom-call(s32[16]{0:T(128)} %tenant_in.1, s32[16]{0:T(128)} %length_in.1, s32[4,16]{1,0:T(4,128)} %admitted_in.1, s32[512]{0:T(512)} %tenant_adapter_in.1, s32[128]{0:T(128)} %adapter_slot_in.1, ...), custom_call_target="tpu_custom_call" | custom-call | flops 33554432 | bytes 2097152 | tf_op jit(solution)/shard_map/pallas_call | solution.py:484
  3.1 14.2 %all_to_all.27 = bf16[16,8,768]{2,1,0:T(8,128)(2,1)S(1)} all-to-all(bf16[16,8,768]{2,1,0:T(8,128)(2,1)S(1)} %bitcast.13), channel_id=1, replica_groups=mesh['batch'=16,'z'=8,'core'=2] {'batch'}, dimensions={0} | all-to-all | bytes 393216 | tf_op jit(solution)/shard_map/all_to_all | solution.py:534
  17.3 0.0 copy-done
  17.3 2.6 %shard_map.137 = (f32[64,128]{1,0:T(8,128)S(1)}, bf16[64,1280]{1,0:T(8,128)(2,1)S(1)}, bf16[1,64,512]{2,1,0:T(8,128)(2,1)S(1)}, bf16[64,512]{1,0:T(8,128)(2,1)S(1)}, bf16[256,8192]{1,0:T(8,128)(2,1)S(1)}) custom-call(bf16[128,768]{1,0:T(8,128)(2,1)S(1)} %bitcast.10, bf16[64,768]{1,0:T(8,128)(2,1)S(1)} %get-tuple-element.20.home_ref, ...), custom_call_target="tpu_custom_call" | custom-call | flops 67108864 | bytes 4194304 | tf_op jit(solution)/shard_map/pallas_call | solution.py:540
  19.9 0.1 collective-permute-start
  20.0 0.0 copy-start.1
  20.0 1.3 %shard_map.138 = (f32[8,64,512]{2,1,0:T(8,128)S(1)}, bf16[5,64,512]{2,1,0:T(8,128)(2,1)S(1)}) custom-call(bf16[64,512]{1,0:T(8,128)(2,1)S(1)} %get-tuple-element.22.rows_ref, bf16[256,8192]{1,0:T(8,128)(2,1)S(1)} %get-tuple-element.21.weight_ref, bf16[256,8192]{1,0:T(8,128)(2,1)S(1)} %get-tuple-element.23.late_ref), custom_call_target="tpu_custom_call" | custom-call | flops 268435456 | bytes 4194304 | tf_op jit(solution)/shard_map/pallas_call | solution.py:557
  21.4 0.1 collective-permute-done.came_ref
  21.4 0.7 %shard_map.139 = (bf16[8,64,128]{2,1,0:T(8,128)(2,1)}, bf16[2,64,512]{2,1,0:T(8,128)(2,1)S(1)}, bf16[6,64,512]{2,1,0:T(8,128)(2,1)S(1)}) custom-call(f32[64,128]{1,0:T(8,128)S(1)} %get-tuple-element.25.low_ref, f32[8,64,512]{2,1,0:T(8,128)S(1)} %get-tuple-element.24.ours_ref, bf16[64,1280]{1,0:T(8,128)(2,1)S(1)} %collective-permute-done.came_ref, ...), custom_call_target="tpu_custom_call" | custom-call | flops 131072 | bytes 524288 | tf_op jit(solution)/shard_map/pallas_call | solution.py:565
  22.1 0.4 collective-permute-start.1
  22.6 5.9 %collective-permute-start.2 = (bf16[2,64,512]{2,1,0:T(8,128)(2,1)S(1)}, bf16[2,64,512]{2,1,0:T(8,128)(2,1)S(1)}, u32[]{:S(2)}, u32[]{:S(2)}) collective-permute-start(bf16[2,64,512]{2,1,0:T(8,128)(2,1)S(1)} %get-tuple-element.30), channel_id=1, source_target_pairs={{0,14},{2,4},{4,2},{6,8},{8,6},{10,12},{12,10},{14,0},{1,15},{3,5}... | collective-permute-start | bytes 393224 | tf_op jit(solution)/shard_map/ppermute | solution.py:588
  28.4 3.4 %all-to-all-start.1 = ((bf16[8,64,128]{2,1,0:T(8,128)(2,1)}), bf16[8,64,128]{2,1,0:T(8,128)(2,1)S(1)}, u32[]{:S(2)}, u32[]{:S(2)}) async-start(bf16[8,64,128]{2,1,0:T(8,128)(2,1)} %get-tuple-element.31), calls=%async_computation.1 | async-start | bytes 262144 | tf_op jit(solution)/shard_map/all_to_all | solution.py:574
  31.8 0.4 collective-permute-done.2.came_ref
  32.2 0.0 collective-permute-done.1.others_ref
  32.2 1.7 %collective-permute-start.3 = (bf16[2,64,512]{2,1,0:T(8,128)(2,1)S(1)}, bf16[2,64,512]{2,1,0:T(8,128)(2,1)S(1)}, u32[]{:S(2)}, u32[]{:S(2)}) collective-permute-start(bf16[2,64,512]{2,1,0:T(8,128)(2,1)S(1)} %shard_map.140), channel_id=1, source_target_pairs={{0,2},{2,0},{4,6},{6,4},{8,10},{10,8},{12,14},{14,12},{1,3},{3,1},... | collective-permute-start | bytes 393224 | tf_op jit(solution)/shard_map/ppermute | solution.py:589
  33.9 7.8 %all-to-all-done.1.parts_ref = bf16[8,64,128]{2,1,0:T(8,128)(2,1)S(1)} async-done(((bf16[8,64,128]{2,1,0:T(8,128)(2,1)}), bf16[8,64,128]{2,1,0:T(8,128)(2,1)S(1)}, u32[]{:S(2)}, u32[]{:S(2)}) %all-to-all-start.1) | async-done | bytes 131104 | tf_op jit(solution)/shard_map/all_to_all | solution.py:574
  41.7 0.0 copy-done.1
  41.7 0.9 %shard_map.141.after_ref = bf16[128,512]{1,0:T(8,128)(2,1)} custom-call(bf16[8,64,128]{2,1,0:T(8,128)(2,1)S(1)} %all-to-all-done.1.parts_ref, bf16[128,128]{1,0:T(8,128)(2,1)S(1)} %slice.17.held_ref, bf16[8,64,512]{2,1,0:T(8,128)(2,1)S(1)} %copy-done.1), custom_call_target="tpu_custom_call" | custom-call | flops 67108864 | bytes 262144 | tf_op jit(solution)/shard_map/pallas_call | solution.py:590
  42.6 0.0 collective-permute-done.3.came_ref
  42.7 0.3 collective-permute-start.4
  43.0 4.8 %all-to-all-start.2 = ((bf16[16,8,512]{2,1,0:T(8,128)(2,1)}), bf16[16,8,512]{2,1,0:T(8,128)(2,1)S(1)}, u32[]{:S(2)}, u32[]{:S(2)}) async-start(bf16[16,8,512]{2,1,0:T(8,128)(2,1)} %bitcast.7), calls=%async_computation.2 | async-start | bytes 262144 | tf_op jit(solution)/shard_map/all_to_all | solution.py:601
  47.7 1.2 %collective-permute-done.4.came_ref = bf16[2,64,512]{2,1,0:T(8,128)(2,1)S(1)} collective-permute-done((bf16[2,64,512]{2,1,0:T(8,128)(2,1)S(1)}, bf16[2,64,512]{2,1,0:T(8,128)(2,1)S(1)}, u32[]{:S(2)}, u32[]{:S(2)}) %collective-permute-start.4) | collective-permute-done | bytes 131104 | tf_op jit(solution)/shard_map/ppermute | solution.py:599
  49.0 0.1 collective-permute-start.5
  49.1 4.2 %collective-permute-done.5.second_ref = bf16[1,64,512]{2,1,0:T(8,128)(2,1)S(1)} collective-permute-done((bf16[1,64,512]{2,1,0:T(8,128)(2,1)S(1)}, bf16[1,64,512]{2,1,0:T(8,128)(2,1)S(1)}, u32[]{:S(2)}, u32[]{:S(2)}) %collective-permute-start.5) | collective-permute-done | bytes 65568 | tf_op jit(solution)/shard_map/ppermute | solution.py:600
  53.4 1.1 %all-to-all-done.2 = bf16[16,8,512]{2,1,0:T(8,128)(2,1)S(1)} async-done(((bf16[16,8,512]{2,1,0:T(8,128)(2,1)}), bf16[16,8,512]{2,1,0:T(8,128)(2,1)S(1)}, u32[]{:S(2)}, u32[]{:S(2)}) %all-to-all-start.2) | async-done | bytes 131104 | tf_op jit(solution)/shard_map/all_to_all | solution.py:601
  54.5 0.8 %shard_map.145 = bf16[64,512]{1,0:T(8,128)(2,1)} custom-call(f32[64,512]{1,0:T(8,128)S(1)} %shard_map.144.base_ref, bf16[64,128]{1,0:T(8,128)(2,1)S(1)} %get-tuple-element.32.back_ref, bf16[128,512]{1,0:T(8,128)(2,1)S(1)} %bitcast.12), custom_call_target="tpu_custom_call" | custom-call | flops 8388608 | bytes 327680 | tf_op jit(solution)/shard_map/pallas_call | solution.py:610
  (8 shorter events, 0.2 us)
Async XLA Ops:
  0.0 17.3 %copy-start = (bf16[8,64,512]{2,1,0:T(8,128)(2,1)S(1)}, bf16[8,64,512]{2,1,0:T(8,128)(2,1)}, u32[]{:S(2)}) copy-start(bf16[8,64,512]{2,1,0:T(8,128)(2,1)} %down_ref.1) | copy-start | bytes 1572868
  19.9 1.5 %collective-permute-start = (bf16[64,1280]{1,0:T(8,128)(2,1)S(1)}, bf16[64,1280]{1,0:T(8,128)(2,1)S(1)}, u32[]{:S(2)}, u32[]{:S(2)}) collective-permute-start(bf16[64,1280]{1,0:T(8,128)(2,1)S(1)} %get-tuple-element.26), channel_id=1, source_target_pairs={{0,1},{1,0},{2,3},{3,2},{4,5},{5,4},{6,7},{7,6},{8,9},{9,8},{10,11... | collective-permute-start | bytes 491528 | tf_op jit(solution)/shard_map/ppermute | solution.py:556
  20.0 21.6 %copy-start.1 = (bf16[8,64,512]{2,1,0:T(8,128)(2,1)S(1)}, bf16[8,64,512]{2,1,0:T(8,128)(2,1)}, u32[]{:S(2)}) copy-start(bf16[8,64,512]{2,1,0:T(8,128)(2,1)} %up_ref.1) | copy-start | bytes 1572868
  22.1 10.0 %collective-permute-start.1 = (bf16[6,64,512]{2,1,0:T(8,128)(2,1)S(1)}, bf16[6,64,512]{2,1,0:T(8,128)(2,1)S(1)}, u32[]{:S(2)}, u32[]{:S(2)}) collective-permute-start(bf16[6,64,512]{2,1,0:T(8,128)(2,1)S(1)} %get-tuple-element.29), channel_id=1, source_target_pairs={{0,1},{1,0},{2,3},{3,2},{4,5},{5,4},{6,7},{7,6},{8,9},{9,8},{10,11... | collective-permute-start | bytes 1179656 | tf_op jit(solution)/shard_map/ppermute | solution.py:573
  22.6 9.6 %collective-permute-start.2 = (bf16[2,64,512]{2,1,0:T(8,128)(2,1)S(1)}, bf16[2,64,512]{2,1,0:T(8,128)(2,1)S(1)}, u32[]{:S(2)}, u32[]{:S(2)}) collective-permute-start(bf16[2,64,512]{2,1,0:T(8,128)(2,1)S(1)} %get-tuple-element.30), channel_id=1, source_target_pairs={{0,14},{2,4},{4,2},{6,8},{8,6},{10,12},{12,10},{14,0},{1,15},{3,5}... | collective-permute-start | bytes 393224 | tf_op jit(solution)/shard_map/ppermute | solution.py:588
  28.4 13.3 %all-to-all-start.1 = ((bf16[8,64,128]{2,1,0:T(8,128)(2,1)}), bf16[8,64,128]{2,1,0:T(8,128)(2,1)S(1)}, u32[]{:S(2)}, u32[]{:S(2)}) async-start(bf16[8,64,128]{2,1,0:T(8,128)(2,1)} %get-tuple-element.31), calls=%async_computation.1 | async-start | bytes 262144 | tf_op jit(solution)/shard_map/all_to_all | solution.py:574
  32.2 10.4 %collective-permute-start.3 = (bf16[2,64,512]{2,1,0:T(8,128)(2,1)S(1)}, bf16[2,64,512]{2,1,0:T(8,128)(2,1)S(1)}, u32[]{:S(2)}, u32[]{:S(2)}) collective-permute-start(bf16[2,64,512]{2,1,0:T(8,128)(2,1)S(1)} %shard_map.140), channel_id=1, source_target_pairs={{0,2},{2,0},{4,6},{6,4},{8,10},{10,8},{12,14},{14,12},{1,3},{3,1},... | collective-permute-start | bytes 393224 | tf_op jit(solution)/shard_map/ppermute | solution.py:589
  42.7 6.3 %collective-permute-start.4 = (bf16[2,64,512]{2,1,0:T(8,128)(2,1)S(1)}, bf16[2,64,512]{2,1,0:T(8,128)(2,1)S(1)}, u32[]{:S(2)}, u32[]{:S(2)}) collective-permute-start(bf16[2,64,512]{2,1,0:T(8,128)(2,1)S(1)} %shard_map.142), channel_id=1, source_target_pairs={{0,14},{2,4},{4,2},{6,8},{8,6},{10,12},{12,10},{14,0},{1,15},{3,5}... | collective-permute-start | bytes 393224 | tf_op jit(solution)/shard_map/ppermute | solution.py:599
  43.0 11.5 %all-to-all-start.2 = ((bf16[16,8,512]{2,1,0:T(8,128)(2,1)}), bf16[16,8,512]{2,1,0:T(8,128)(2,1)S(1)}, u32[]{:S(2)}, u32[]{:S(2)}) async-start(bf16[16,8,512]{2,1,0:T(8,128)(2,1)} %bitcast.7), calls=%async_computation.2 | async-start | bytes 262144 | tf_op jit(solution)/shard_map/all_to_all | solution.py:601
  49.0 4.4 %collective-permute-start.5 = (bf16[1,64,512]{2,1,0:T(8,128)(2,1)S(1)}, bf16[1,64,512]{2,1,0:T(8,128)(2,1)S(1)}, u32[]{:S(2)}, u32[]{:S(2)}) collective-permute-start(bf16[1,64,512]{2,1,0:T(8,128)(2,1)S(1)} %shard_map.143), channel_id=1, source_target_pairs={{0,2},{2,0},{4,6},{6,4},{8,10},{10,8},{12,14},{14,12},{1,3},{3,1},... | collective-permute-start | bytes 196616 | tf_op jit(solution)/shard_map/ppermute | solution.py:600
